TPU v7x, 32 devices: a whole 2x2x4 slice. The times are simulated.
32 devices in a mesh: dp: 16 (over z, y, core), mem: 2 (over x).
Axes of the slice: x: 2, y: 2, z: 4, core: 2. Of those that a mesh axis runs over, the one named last changes fastest.
Arguments:
- decoder_in: bfloat16 [16, 1024, 768], P('dp', 'mem'), may hold values from -6 to 6
- encoder_out: bfloat16 [16, 1024, 768], P('dp', 'mem'), may hold values from -6 to 6
- dec_segments: int32 [16, 1024], P('dp', 'mem'), may hold values from 0 to 2, as said below
- dec_mask: int32 [16, 1024], P('dp', 'mem'), may hold values from 0 to 1, as said below
- enc_segments: int32 [16, 1024], P('dp', 'mem'), may hold values from 0 to 2, as said below
- enc_mask: int32 [16, 1024], P('dp', 'mem'), may hold values from 0 to 1, as said below
- self_gain: float32 [768], replicated, may hold values from 0.25 to 1.75
- cross_gain: float32 [768], replicated, may hold values from 0.25 to 1.75
- ffn_gain: float32 [768], replicated, may hold values from 0.25 to 1.75
- rel_bias: float32 [32, 12], replicated, may hold values from -4 to 4
- self_query: bfloat16 [768, 768], replicated, may hold values from -0.109375 to 0.109375
- self_key: bfloat16 [768, 768], replicated, may hold values from -0.109375 to 0.109375
- self_value: bfloat16 [768, 768], replicated, may hold values from -0.21875 to 0.21875
- self_out: bfloat16 [768, 768], replicated, may hold values from -1.25 to 1.25
- cross_query: bfloat16 [768, 768], replicated, may hold values from -0.109375 to 0.109375
- cross_key: bfloat16 [768, 768], replicated, may hold values from -0.109375 to 0.109375
- cross_value: bfloat16 [768, 768], replicated, may hold values from -0.21875 to 0.21875
- cross_out: bfloat16 [768, 768], replicated, may hold values from -1.25 to 1.25
- ffn_in: bfloat16 [768, 3072], replicated, may hold values from -0.21875 to 0.21875
- ffn_out: bfloat16 [3072, 768], replicated, may hold values from -0.109375 to 0.109375
- out_grad: bfloat16 [16, 1024, 768], P('dp', 'mem'), may hold values from -6 to 6
Outputs:
- layer_out: bfloat16 [16, 1024, 768], P('dp', 'mem')
- decoder_in_grad: bfloat16 [16, 1024, 768], P('dp', 'mem')
- encoder_out_grad: bfloat16 [16, 1024, 768], P('dp', 'mem')
- self_gain_grad: float32 [768], replicated
- cross_gain_grad: float32 [768], replicated
- ffn_gain_grad: float32 [768], replicated
- rel_bias_grad: float32 [32, 12], replicated
- self_query_grad: float32 [768, 768], P('dp', 'mem')
- self_key_grad: float32 [768, 768], P('dp', 'mem')
- self_value_grad: float32 [768, 768], P('dp', 'mem')
- self_out_grad: float32 [768, 768], P('dp', 'mem')
- cross_query_grad: float32 [768, 768], P('dp', 'mem')
- cross_key_grad: float32 [768, 768], P('dp', 'mem')
- cross_value_grad: float32 [768, 768], P('dp', 'mem')
- cross_out_grad: float32 [768, 768], P('dp', 'mem')
- ffn_in_grad: float32 [768, 3072], P('dp', 'mem')
- ffn_out_grad: float32 [3072, 768], P('dp', 'mem')
Inputs may be any that keep to these rules, and one draw needn't show every extreme that they name: `dec_segments`: every row holds three decoder documents 0, 1, 2 in order, never falling; document 0 ends within the first 128 positions and document 2 takes at least the last 64 positions, so document 1 starts in the first eighth and ends in the last eighth of the row. `dec_mask`: the zeros of a row are its last positions, fewer than 32 of them. `enc_segments`: every row holds three encoder documents 0, 1, 2 in order, never falling; document 0 ends within the first 128 positions and document 2 takes at least the last 64 positions. `enc_mask`: the zeros of a row are its last positions, fewer than 32 of them.
All inputs are finite; a program needn't handle non-finite values.
Results may differ from a plain program's by a relative error of at most 0.029.
The roundings to bfloat16 on the way count: a program that leaves them out, or rounds other values in their place, can miss the bound.
Values may be sent and summed in bfloat16 or wider, within the bound.
No kernel may reach another device: no remote copies, remote signals or barrier semaphores. Data moves between devices by JAX's collectives and lax.ppermute only.
A program may use at most 320 MiB of HBM per device.

v0:
```python
import math

import jax
import jax.numpy as jnp
from jax import lax
from jax.sharding import PartitionSpec as P

HEADS = 12
HEAD_DIM = 64
BUCKETS = 32
MAX_DIST = 128


EPSILON = 1e-06
NEGATIVE = -1000000000.0


def rel_bucket(distance):
    exact_max = BUCKETS // 2
    bucket_edges = [
        math.ceil(exact_max * (MAX_DIST / exact_max) ** (degree / exact_max))
        for degree in range(1, exact_max)
    ]
    log_bucket = exact_max + sum(
        ((distance >= edge_value).astype(jnp.int32) for edge_value in bucket_edges)
    )
    return jnp.where(distance < exact_max, distance, log_bucket)


def bias_table(query_pos, key_pos, rel_bias):
    distance = jnp.maximum(query_pos[:, None] - key_pos[None, :], 0)
    hot = (rel_bucket(distance)[:, :, None] == jnp.arange(BUCKETS, dtype=jnp.int32)).astype(
        jnp.float32
    )
    return (jnp.einsum("qkb,bh->hqk", hot, rel_bias, precision=lax.Precision.HIGHEST), hot)


def rms_scale(hidden, gain):
    return hidden * lax.rsqrt(jnp.mean(hidden * hidden, axis=-1, keepdims=True) + EPSILON) * gain


def smooth_gate(values):
    return jax.nn.gelu(values, approximate=True)


def project(values, weight):
    return jnp.einsum("rsd,de->rse", values, weight, preferred_element_type=jnp.float32)


def project_back(values, weight):
    return jnp.einsum("rse,de->rsd", values, weight, preferred_element_type=jnp.float32)


def weight_grad(inputs, grads):
    return jnp.einsum("rsd,rse->de", inputs, grads, preferred_element_type=jnp.float32)


def split_heads(values):
    return values.reshape(values.shape[0], values.shape[1], HEADS, HEAD_DIM)


def masked_scores(query_rows, key_all, allowed, bias):
    scores = jnp.einsum(
        "rqhd,rkhd->rhqk",
        split_heads(query_rows),
        split_heads(key_all),
        preferred_element_type=jnp.float32,
    )
    if bias is not None:
        scores = scores + bias[None]
    return jnp.where(allowed[:, None], scores, NEGATIVE)


def attend(query_rows, key_all, value_all, allowed, bias):
    scores = masked_scores(query_rows, key_all, allowed, bias)
    top_score = jnp.max(scores, axis=-1, keepdims=True)
    weights = jnp.exp(scores - top_score)
    total = jnp.sum(weights, axis=-1, keepdims=True)
    probs = (weights / total).astype(jnp.bfloat16)
    mixed = jnp.einsum(
        "rhqk,rkhd->rqhd", probs, split_heads(value_all), preferred_element_type=jnp.float32
    )
    return (mixed.reshape(query_rows.shape).astype(jnp.bfloat16), top_score + jnp.log(total))


def attend_back(query_rows, key_all, value_all, allowed, bias, log_total, mixed_grad):
    scores = masked_scores(query_rows, key_all, allowed, bias)
    probs = jnp.exp(scores - log_total)
    prob_grad = jnp.einsum(
        "rqhd,rkhd->rhqk",
        split_heads(mixed_grad),
        split_heads(value_all),
        preferred_element_type=jnp.float32,
    )
    inner = jnp.sum(probs * prob_grad, axis=-1, keepdims=True)
    score_grad = (probs * (prob_grad - inner)).astype(jnp.bfloat16)
    query_grad = jnp.einsum(
        "rhqk,rkhd->rqhd", score_grad, split_heads(key_all), preferred_element_type=jnp.float32
    )
    return (query_grad.reshape(query_rows.shape).astype(jnp.bfloat16), inner, score_grad, probs)


def key_parts(score_grad, probs, query_rows, mixed_grad, key_shape):
    key_grad = jnp.einsum(
        "rhqk,rqhd->rkhd", score_grad, split_heads(query_rows), preferred_element_type=jnp.float32
    )
    value_grad = jnp.einsum(
        "rhqk,rqhd->rkhd",
        probs.astype(jnp.bfloat16),
        split_heads(mixed_grad),
        preferred_element_type=jnp.float32,
    )
    return (key_grad.reshape(key_shape), value_grad.reshape(key_shape))


def on_device(
    decoder_in,
    encoder_out,
    dec_segments,
    dec_mask,
    enc_segments,
    enc_mask,
    self_gain,
    cross_gain,
    ffn_gain,
    rel_bias,
    self_query,
    self_key,
    self_value,
    self_out,
    cross_query,
    cross_key,
    cross_value,
    cross_out,
    ffn_in,
    ffn_out,
    out_grad,
):
    local_len = decoder_in.shape[1]
    query_pos = lax.axis_index("mem") * local_len + jnp.arange(local_len, dtype=jnp.int32)
    key_pos = jnp.arange(local_len * lax.axis_size("mem"), dtype=jnp.int32)
    self_bias, bucket_hot = bias_table(query_pos, key_pos, rel_bias)
    causal = query_pos[:, None] >= key_pos[None, :]
    query_tag = (dec_segments + 1).astype(jnp.float32)
    dec_tag = ((dec_segments + 1) * dec_mask).astype(jnp.bfloat16)
    enc_tag = ((enc_segments + 1) * enc_mask).astype(jnp.bfloat16)
    hidden_zero = decoder_in.astype(jnp.float32)
    self_norm, self_pull = jax.vjp(rms_scale, hidden_zero, self_gain)
    self_in = self_norm.astype(jnp.bfloat16)
    query_rows = project(self_in, self_query).astype(jnp.bfloat16)
    key_rows = project(self_in, self_key).astype(jnp.bfloat16)
    value_rows = project(self_in, self_value).astype(jnp.bfloat16)
    key_all, value_all, tag_all = (
        lax.all_gather(key_rows, "mem", axis=1, tiled=True),
        lax.all_gather(value_rows, "mem", axis=1, tiled=True),
        lax.all_gather(dec_tag, "mem", axis=1, tiled=True),
    )
    self_allowed = causal[None] & (tag_all.astype(jnp.float32)[:, None, :] == query_tag[:, :, None])
    self_mixed, self_lse = attend(query_rows, key_all, value_all, self_allowed, self_bias)
    hidden_one = hidden_zero + project(self_mixed, self_out)
    cross_norm, cross_pull = jax.vjp(rms_scale, hidden_one, cross_gain)
    cross_in = cross_norm.astype(jnp.bfloat16)
    cross_rows = project(cross_in, cross_query).astype(jnp.bfloat16)
    cross_key_own = project(encoder_out, cross_key).astype(jnp.bfloat16)
    cross_value_own = project(encoder_out, cross_value).astype(jnp.bfloat16)
    cross_key_all, cross_value_all, cross_tag_all = (
        lax.all_gather(cross_key_own, "mem", axis=1, tiled=True),
        lax.all_gather(cross_value_own, "mem", axis=1, tiled=True),
        lax.all_gather(enc_tag, "mem", axis=1, tiled=True),
    )
    cross_allowed = cross_tag_all.astype(jnp.float32)[:, None, :] == query_tag[:, :, None]
    cross_mixed, cross_lse = attend(cross_rows, cross_key_all, cross_value_all, cross_allowed, None)
    hidden_two = hidden_one + project(cross_mixed, cross_out)
    ffn_norm, ffn_pull = jax.vjp(rms_scale, hidden_two, ffn_gain)
    ffn_input = ffn_norm.astype(jnp.bfloat16)
    ffn_pre = project(ffn_input, ffn_in)
    ffn_wide, gate_pull = jax.vjp(smooth_gate, ffn_pre)
    ffn_act = ffn_wide.astype(jnp.bfloat16)
    layer_out = (hidden_two + project(ffn_act, ffn_out)).astype(jnp.bfloat16)
    out_wide = out_grad.astype(jnp.float32)
    ffn_out_grad = weight_grad(ffn_act, out_grad)
    (pre_grad_wide,) = gate_pull(project_back(out_grad, ffn_out))
    pre_grad = pre_grad_wide.astype(jnp.bfloat16)
    ffn_in_grad = weight_grad(ffn_input, pre_grad)
    norm_grad_three, ffn_gain_grad = ffn_pull(project_back(pre_grad, ffn_in))
    hidden_two_grad = out_wide + norm_grad_three
    cross_branch_grad = hidden_two_grad.astype(jnp.bfloat16)
    cross_out_grad = weight_grad(cross_mixed, cross_branch_grad)
    cross_mixed_grad = project_back(cross_branch_grad, cross_out).astype(jnp.bfloat16)
    cross_key_all, cross_value_all = (
        lax.all_gather(cross_key_own, "mem", axis=1, tiled=True),
        lax.all_gather(cross_value_own, "mem", axis=1, tiled=True),
    )
    cross_q_grad, cross_inner, cross_score_grad, cross_probs = attend_back(
        cross_rows, cross_key_all, cross_value_all, cross_allowed, None, cross_lse, cross_mixed_grad
    )
    cross_k_part, cross_v_part = key_parts(
        cross_score_grad, cross_probs, cross_rows, cross_mixed_grad, cross_key_all.shape
    )
    cross_k_sum, cross_v_sum = (
        lax.psum_scatter(
            cross_k_part.astype(jnp.bfloat16), "mem", scatter_dimension=1, tiled=True
        ).astype(jnp.float32),
        lax.psum_scatter(
            cross_v_part.astype(jnp.bfloat16), "mem", scatter_dimension=1, tiled=True
        ).astype(jnp.float32),
    )
    cross_k_grad = cross_k_sum.astype(jnp.bfloat16)
    cross_v_grad = cross_v_sum.astype(jnp.bfloat16)
    cross_query_grad = weight_grad(cross_in, cross_q_grad)
    cross_key_grad = weight_grad(encoder_out, cross_k_grad)
    cross_value_grad = weight_grad(encoder_out, cross_v_grad)
    encoder_out_grad = (
        project_back(cross_k_grad, cross_key) + project_back(cross_v_grad, cross_value)
    ).astype(jnp.bfloat16)
    norm_grad_two, cross_gain_grad = cross_pull(project_back(cross_q_grad, cross_query))
    hidden_one_grad = hidden_two_grad + norm_grad_two
    self_branch_grad = hidden_one_grad.astype(jnp.bfloat16)
    self_out_grad = weight_grad(self_mixed, self_branch_grad)
    self_mixed_grad = project_back(self_branch_grad, self_out).astype(jnp.bfloat16)
    self_q_grad, self_inner, self_score_grad, self_probs = attend_back(
        query_rows, key_all, value_all, self_allowed, self_bias, self_lse, self_mixed_grad
    )
    table_grad = jnp.einsum(
        "rhqk,qkb->bh",
        self_score_grad.astype(jnp.float32),
        bucket_hot,
        precision=lax.Precision.HIGHEST,
    )
    self_k_part, self_v_part = key_parts(
        self_score_grad, self_probs, query_rows, self_mixed_grad, key_all.shape
    )
    self_k_sum, self_v_sum = (
        lax.psum_scatter(
            self_k_part.astype(jnp.bfloat16), "mem", scatter_dimension=1, tiled=True
        ).astype(jnp.float32),
        lax.psum_scatter(
            self_v_part.astype(jnp.bfloat16), "mem", scatter_dimension=1, tiled=True
        ).astype(jnp.float32),
    )
    self_k_grad = self_k_sum.astype(jnp.bfloat16)
    self_v_grad = self_v_sum.astype(jnp.bfloat16)
    self_query_grad = weight_grad(self_in, self_q_grad)
    self_key_grad = weight_grad(self_in, self_k_grad)
    self_value_grad = weight_grad(self_in, self_v_grad)
    norm_input_grad = (
        project_back(self_q_grad, self_query)
        + project_back(self_k_grad, self_key)
        + project_back(self_v_grad, self_value)
    )
    norm_grad_one, self_gain_grad = self_pull(norm_input_grad)
    decoder_in_grad = (hidden_one_grad + norm_grad_one).astype(jnp.bfloat16)
    self_gain_sum, cross_gain_sum, ffn_gain_sum, table_sum = lax.psum(
        (self_gain_grad, cross_gain_grad, ffn_gain_grad, table_grad), ("dp", "mem")
    )
    grad_sq, grad_sk, grad_sv, grad_so, grad_cq, grad_ck, grad_cv, grad_co, grad_fi, grad_fo = (
        lax.psum_scatter(
            self_query_grad.astype(jnp.bfloat16), "dp", scatter_dimension=0, tiled=True
        ).astype(jnp.float32),
        lax.psum_scatter(
            self_key_grad.astype(jnp.bfloat16), "dp", scatter_dimension=0, tiled=True
        ).astype(jnp.float32),
        lax.psum_scatter(
            self_value_grad.astype(jnp.bfloat16), "dp", scatter_dimension=0, tiled=True
        ).astype(jnp.float32),
        lax.psum_scatter(
            self_out_grad.astype(jnp.bfloat16), "dp", scatter_dimension=0, tiled=True
        ).astype(jnp.float32),
        lax.psum_scatter(
            cross_query_grad.astype(jnp.bfloat16), "dp", scatter_dimension=0, tiled=True
        ).astype(jnp.float32),
        lax.psum_scatter(
            cross_key_grad.astype(jnp.bfloat16), "dp", scatter_dimension=0, tiled=True
        ).astype(jnp.float32),
        lax.psum_scatter(
            cross_value_grad.astype(jnp.bfloat16), "dp", scatter_dimension=0, tiled=True
        ).astype(jnp.float32),
        lax.psum_scatter(
            cross_out_grad.astype(jnp.bfloat16), "dp", scatter_dimension=0, tiled=True
        ).astype(jnp.float32),
        lax.psum_scatter(
            ffn_in_grad.astype(jnp.bfloat16), "dp", scatter_dimension=0, tiled=True
        ).astype(jnp.float32),
        lax.psum_scatter(
            ffn_out_grad.astype(jnp.bfloat16), "dp", scatter_dimension=0, tiled=True
        ).astype(jnp.float32),
    )
    grad_sq, grad_sk, grad_sv, grad_so, grad_cq, grad_ck, grad_cv, grad_co, grad_fi, grad_fo = (
        lax.psum_scatter(
            grad_sq.astype(jnp.bfloat16), "mem", scatter_dimension=1, tiled=True
        ).astype(jnp.float32),
        lax.psum_scatter(
            grad_sk.astype(jnp.bfloat16), "mem", scatter_dimension=1, tiled=True
        ).astype(jnp.float32),
        lax.psum_scatter(
            grad_sv.astype(jnp.bfloat16), "mem", scatter_dimension=1, tiled=True
        ).astype(jnp.float32),
        lax.psum_scatter(
            grad_so.astype(jnp.bfloat16), "mem", scatter_dimension=1, tiled=True
        ).astype(jnp.float32),
        lax.psum_scatter(
            grad_cq.astype(jnp.bfloat16), "mem", scatter_dimension=1, tiled=True
        ).astype(jnp.float32),
        lax.psum_scatter(
            grad_ck.astype(jnp.bfloat16), "mem", scatter_dimension=1, tiled=True
        ).astype(jnp.float32),
        lax.psum_scatter(
            grad_cv.astype(jnp.bfloat16), "mem", scatter_dimension=1, tiled=True
        ).astype(jnp.float32),
        lax.psum_scatter(
            grad_co.astype(jnp.bfloat16), "mem", scatter_dimension=1, tiled=True
        ).astype(jnp.float32),
        lax.psum_scatter(
            grad_fi.astype(jnp.bfloat16), "mem", scatter_dimension=1, tiled=True
        ).astype(jnp.float32),
        lax.psum_scatter(
            grad_fo.astype(jnp.bfloat16), "mem", scatter_dimension=1, tiled=True
        ).astype(jnp.float32),
    )
    return (
        layer_out,
        decoder_in_grad,
        encoder_out_grad,
        self_gain_sum,
        cross_gain_sum,
        ffn_gain_sum,
        table_sum,
        grad_sq,
        grad_sk,
        grad_sv,
        grad_so,
        grad_cq,
        grad_ck,
        grad_cv,
        grad_co,
        grad_fi,
        grad_fo,
    )


def solution(mesh):
    in_specs = (
        P("dp", "mem", None),
        P("dp", "mem", None),
        P("dp", "mem"),
        P("dp", "mem"),
        P("dp", "mem"),
        P("dp", "mem"),
        P(),
        P(),
        P(),
        P(),
        P(),
        P(),
        P(),
        P(),
        P(),
        P(),
        P(),
        P(),
        P(),
        P(),
        P("dp", "mem", None),
    )
    out_specs = (
        P("dp", "mem", None),
        P("dp", "mem", None),
        P("dp", "mem", None),
        P(),
        P(),
        P(),
        P(),
        P("dp", "mem"),
        P("dp", "mem"),
        P("dp", "mem"),
        P("dp", "mem"),
        P("dp", "mem"),
        P("dp", "mem"),
        P("dp", "mem"),
        P("dp", "mem"),
        P("dp", "mem"),
        P("dp", "mem"),
    )
    return jax.shard_map(
        on_device, mesh=mesh, in_specs=in_specs, out_specs=out_specs, check_vma=False
    )
```

profile of v0, /device:TPU:0, one launch (start us, length us, event | category | flops | bytes accessed | tf_op | source)
XLA Modules:
  0.0 1191.8 jit_solution(4485790504601915162)
XLA Ops:
  9.3 3.4 convolution_convert_fusion.17
  14.6 3.3 convolution_convert_fusion.14
  18.0 2.8 convolution_convert_fusion.16
  21.0 5.2 all_gather.24
  26.3 4.4 all_gather.21
  33.9 5.0 compare_select_fusion
  40.9 23.8 %fusion.1 = f32[512,1024,12]{0,2,1:T(8,128)} fusion(s32[512,1024]{0,1:T(8,128)S(1)} %copy.77, f32[32,12]{0,1:T(8,128)S(1)} %copy-done.41), kind=kOutput, calls=%fused_computation.2 | convolution fusion | flops 2432696320 | bytes 27264512 | tf_op jit(solution)/shard_map/qkb,bh->hqk/dot_general | solution.py:35
  64.6 30.5 %copy.78 = f32[512,1024,12]{1,0,2:T(8,128)} copy(f32[512,1024,12]{0,2,1:T(8,128)} %fusion.1) | data formatting | bytes 50331648 | tf_op jit(solution)/shard_map/qkb,bh->hqk/dot_general | solution.py:35
  98.5 16.9 %fusion.116 = (f32[12,512]{1,0:T(8,128)S(1)}, f32[12,512,1024]{2,1,0:T(8,128)}) fusion(f32[512,1024,12]{1,0,2:T(8,128)} %copy.78, bf16[512,12,64]{0,2,1:T(8,128)(2,1)} %bitcast.237, bf16[1024,12,64]{0,2,1:T(8,128)(2,1)S(1)} %bitcast.231, pred[512,1024]{1,0:T(8,128)(4,1)} %get-tuple-element.79), kind=kOutput, calls=%fused_computation.172 | convolution fusion | flops 824174592 | bytes 53239808 | tf_op jit(solution)/shard_map/rqhd,rkhd->rhqk/dot_general | solution.py:63
  115.4 11.1 fusion.5
  128.3 11.2 fusion.66
  144.5 2.6 copy.81
  147.1 13.6 %select_reduce_fusion = (f32[12,512]{1,0:T(8,128)S(1)}, f32[12,512,1024]{2,1,0:T(8,128)}) fusion(pred[512,1024]{1,0:T(8,128)(4,1)S(1)} %get-tuple-element.78, bf16[512,12,64]{0,2,1:T(8,128)(2,1)} %bitcast.235, bf16[1024,12,64]{0,2,1:T(8,128)(2,1)} %bitcast.233), kind=kOutput, calls=%fused_computation.19 | convolution fusion | flops 817883136 | bytes 28073984 | tf_op jit(solution)/shard_map/rqhd,rkhd->rhqk/dot_general | solution.py:63
  160.7 11.5 fusion.6
  172.3 2.7 copy.79
  174.9 11.9 fusion.65
  187.9 5.2 fusion.106
  193.1 9.4 fusion.25
  202.6 3.4 fusion.58
  208.2 2.3 copy.82
  210.4 17.9 %multiply_reduce_fusion.1 = (f32[12,512]{1,0:T(8,128)S(1)}, f32[12,512,1024]{2,1,0:T(8,128)}) fusion(f32[12,512,1024]{2,1,0:T(8,128)} %get-tuple-element.87, f32[12,512]{1,0:T(8,128)S(1)} %log_add_fusion.1, pred[512,1024]{1,0:T(8,128)(4,1)S(1)} %get-tuple-element.78, bf16[512,12,64]{0,2,1:T(8,128)(2,1)} %bitcast.254, bf16[1024,12,64]{0,2,1:T(8,128)(2,1)} %bitcast.246), kind=kOutput, calls=%fused_computation.11 | convolution fusion | flops 830466048 | bytes 53264384 | tf_op jit(solution)/shard_map/rqhd,rkhd->rhqk/dot_general | solution.py:89
  228.4 21.8 %multiply_convert_fusion.1 = bf16[12,512,1024]{2,1,0:T(8,128)(2,1)} fusion(f32[12,512,1024]{2,1,0:T(8,128)} %get-tuple-element.92, f32[12,512,1024]{2,1,0:T(8,128)} %get-tuple-element.87, f32[12,512]{1,0:T(8,128)S(1)} %get-tuple-element.91, f32[12,512]{1,0:T(8,128)S(1)} %log_add_fusion.1, pred[512,1024]{1,0:T(8,128)(4,1)S(1)} %get-tuple-element.78), kind=kLoop, calls=%fused_computation.10 | loop fusion | flops 31457280 | bytes 63488000 | tf_op jit(solution)/shard_map/convert_element_type | solution.py:96
  250.1 8.6 convolution_convert_fusion.21
  265.0 11.6 fusion.44
  276.9 18.3 %multiply_reduce_fusion = (f32[12,512]{1,0:T(8,128)S(1)}, f32[12,512,1024]{2,1,0:T(8,128)}) fusion(f32[12,512,1024]{2,1,0:T(8,128)} %get-tuple-element.83, f32[12,512]{1,0:T(8,128)S(1)} %log_add_fusion, bf16[512,12,64]{0,2,1:T(8,128)(2,1)S(1)} %bitcast.242, bf16[1024,12,64]{0,2,1:T(8,128)(2,1)} %bitcast.244), kind=kOutput, calls=%fused_computation.8 | convolution fusion | flops 824174592 | bytes 52740096 | tf_op jit(solution)/shard_map/rqhd,rkhd->rhqk/dot_general | solution.py:89
  295.2 16.8 %multiply_convert_fusion = bf16[12,512,1024]{2,1,0:T(8,128)(2,1)S(1)} fusion(f32[12,512,1024]{2,1,0:T(8,128)} %get-tuple-element.95, f32[12,512,1024]{2,1,0:T(8,128)} %get-tuple-element.83, f32[12,512]{1,0:T(8,128)S(1)} %get-tuple-element.94, f32[12,512]{1,0:T(8,128)S(1)} %log_add_fusion), kind=kLoop, calls=%fused_computation.7 | loop fusion | flops 25165824 | bytes 62963712 | tf_op jit(solution)/shard_map/convert_element_type | solution.py:96
  312.0 4.1 convolution_convert_fusion.3
  317.0 13.1 %fusion.47 = bf16[12,64,1024]{2,1,0:T(8,128)(2,1)} fusion(bf16[512,12,64]{0,2,1:T(8,128)(2,1)} %bitcast.255, f32[12,512,1024]{2,1,0:T(8,128)} %get-tuple-element.87, f32[12,512]{1,0:T(8,128)S(1)} %log_add_fusion.1, pred[512,1024]{1,0:T(8,128)(4,1)S(1)} %get-tuple-element.78), kind=kOutput, calls=%fused_computation.74 | convolution fusion | flops 824967168 | bytes 28073984 | tf_op jit(solution)/shard_map/rhqk,rqhd->rkhd/dot_general | solution.py:107
  330.3 3.0 convolution_convert_fusion.4
  333.4 3.4 convolution_convert_fusion.7
  336.9 3.3 convolution_convert_fusion.8
  340.6 8.5 convolution_convert_fusion.20
  352.1 8.5 convolution_convert_fusion.2
  360.7 3.2 convolution_convert_fusion.9
  364.0 3.2 convolution_convert_fusion.10
  367.3 5.8 reduce-scatter.49.cloned.1.call-done
  376.6 58.7 %reduce-scatter.65.cloned.1.call-done = bf16[48,768]{1,0:T(8,128)(2,1)} async-done(((bf16[768,768]{1,0:T(8,128)(2,1)}), bf16[48,768]{1,0:T(8,128)(2,1)}) %reduce-scatter.65.cloned.1.call-update) | async-done | bytes 73744 | tf_op jit(solution)/shard_map/reduce_scatter | solution.py:278
  437.0 59.4 %reduce-scatter.59.cloned.1.call-done = bf16[48,768]{1,0:T(8,128)(2,1)} async-done(((bf16[768,768]{1,0:T(8,128)(2,1)}), bf16[48,768]{1,0:T(8,128)(2,1)}) %reduce-scatter.59.cloned.1.call-update) | async-done | bytes 73744 | tf_op jit(solution)/shard_map/reduce_scatter | solution.py:269
  498.2 59.1 %reduce-scatter.57.cloned.1.call-done = bf16[48,768]{1,0:T(8,128)(2,1)} async-done(((bf16[768,768]{1,0:T(8,128)(2,1)}), bf16[48,768]{1,0:T(8,128)(2,1)}) %reduce-scatter.57.cloned.1.call-update) | async-done | bytes 73744 | tf_op jit(solution)/shard_map/reduce_scatter | solution.py:266
  559.1 59.3 %reduce-scatter.51.cloned.1.call-done = bf16[48,768]{1,0:T(8,128)(2,1)} async-done(((bf16[768,768]{1,0:T(8,128)(2,1)}), bf16[48,768]{1,0:T(8,128)(2,1)}) %reduce-scatter.51.cloned.1.call-update) | async-done | bytes 73744 | tf_op jit(solution)/shard_map/reduce_scatter | solution.py:257
  620.1 25.5 %reduce-scatter.47.cloned.1.call-done = bf16[1,512,768]{1,2,0:T(8,128)(2,1)} async-done(((bf16[1,1024,768]{1,2,0:T(8,128)(2,1)}), bf16[1,512,768]{1,2,0:T(8,128)(2,1)}) %reduce-scatter.47.cloned.1.call-update) | async-done | bytes 786448 | tf_op jit(solution)/shard_map/reduce_scatter | solution.py:201
  649.6 8.2 convolution_convert_fusion
  659.3 6.4 convolution_convert_fusion.1
  665.7 23.1 %copy.84 = bf16[12,512,1024]{1,0,2:T(8,128)(2,1)} copy(bf16[12,512,1024]{2,1,0:T(8,128)(2,1)} %copy-done.2) | data formatting | bytes 25165824 | tf_op jit(solution)/shard_map/convert_element_type | solution.py:96
  688.8 18.6 %reduce-scatter.55.cloned.1.call-done = bf16[48,768]{1,0:T(8,128)(2,1)} async-done(((bf16[768,768]{1,0:T(8,128)(2,1)}), bf16[48,768]{1,0:T(8,128)(2,1)}) %reduce-scatter.55.cloned.1.call-update) | async-done | bytes 73744 | tf_op jit(solution)/shard_map/reduce_scatter | solution.py:263
  709.2 13.6 %fusion.68 = f32[32,12]{0,1:T(8,128)} fusion(bf16[12,512,1024]{1,0,2:T(8,128)(2,1)} %copy.84, s32[512,1024]{0,1:T(8,128)} %copy-done.12), kind=kOutput, calls=%fused_computation.123 | convolution fusion | flops 419430400 | bytes 14681600 | tf_op jit(solution)/shard_map/rhqk,qkb->bh/dot_general | solution.py:224
  722.8 45.3 %reduce-scatter.53.cloned.1.call-done = bf16[48,768]{1,0:T(8,128)(2,1)} async-done(((bf16[768,768]{1,0:T(8,128)(2,1)}), bf16[48,768]{1,0:T(8,128)(2,1)}) %reduce-scatter.53.cloned.1.call-update) | async-done | bytes 73744 | tf_op jit(solution)/shard_map/reduce_scatter | solution.py:260
  770.0 8.8 fusion.62
  778.8 49.8 %reduce-scatter.85.cloned.1.call-done = bf16[48,768]{1,0:T(8,128)(2,1)} async-done(((bf16[768,768]{1,0:T(8,128)(2,1)}), bf16[48,768]{1,0:T(8,128)(2,1)}) %reduce-scatter.85.cloned.1.call-update) | async-done | bytes 73744
  832.5 8.2 reduce-scatter.87.cloned.1.call-done
  842.3 11.4 reduce-scatter.81.cloned.1.call-done
  855.4 12.0 %reduce-scatter.79.cloned.1.call-done = bf16[384,48]{1,0:T(8,128)(2,1)} async-done(((bf16[768,48]{1,0:T(8,128)(2,1)}), bf16[384,48]{1,0:T(8,128)(2,1)}) %reduce-scatter.79.cloned.1.call-update) | async-done | bytes 36880
  869.0 12.2 %reduce-scatter.73.cloned.1.call-done = bf16[384,48]{1,0:T(8,128)(2,1)} async-done(((bf16[768,48]{1,0:T(8,128)(2,1)}), bf16[384,48]{1,0:T(8,128)(2,1)}) %reduce-scatter.73.cloned.1.call-update) | async-done | bytes 36880
  882.8 59.9 %reduce-scatter.83.cloned.1.call-done = bf16[48,768]{1,0:T(8,128)(2,1)} async-done(((bf16[768,768]{1,0:T(8,128)(2,1)}), bf16[48,768]{1,0:T(8,128)(2,1)}) %reduce-scatter.83.cloned.1.call-update) | async-done | bytes 73744
  944.5 3.5 fusion.75
  948.1 73.2 %reduce-scatter.71.cloned.1.call-done = bf16[192,768]{1,0:T(8,128)(2,1)} async-done(((bf16[3072,768]{1,0:T(8,128)(2,1)}), bf16[192,768]{1,0:T(8,128)(2,1)}) %reduce-scatter.71.cloned.1.call-update) | async-done | bytes 294928 | tf_op jit(solution)/shard_map/reduce_scatter | solution.py:284
  1023.2 2.5 fusion.80
  1025.7 2.4 fusion.51
  1028.1 72.2 %reduce-scatter.67.cloned.1.call-done = bf16[48,3072]{1,0:T(8,128)(2,1)} async-done(((bf16[768,3072]{1,0:T(8,128)(2,1)}), bf16[48,3072]{1,0:T(8,128)(2,1)}) %reduce-scatter.67.cloned.1.call-update) | async-done | bytes 294928 | tf_op jit(solution)/shard_map/reduce_scatter | solution.py:281
  1100.3 3.8 fusion.67
  1104.2 40.1 %all-reduce = (f32[768]{0:T(1024)}, f32[768]{0:T(1024)}, f32[768]{0:T(1024)}, f32[32,12]{0,1:T(8,128)}) all-reduce(f32[768]{0:T(1024)S(1)} %get-tuple-element.72, f32[768]{0:T(1024)S(1)} %copy-done.44, f32[768]{0:T(1024)S(1)} %copy-done.43, f32[32,12]{0,1:T(8,128)S(1)} %copy-done.42), channel_id=1, replica_groups=mesh['dp'=16,'mem'=2] {'dp','mem'}, use_global_device_ids=true, to_apply=%region_17.18 | all-reduce | flops 2688 | bytes 21504 | tf_op jit(solution)/shard_map/psum | solution.py:253
  1144.3 2.8 fusion.55
  1155.1 13.6 %reduce-scatter.89.cloned.1.call-done = bf16[384,192]{1,0:T(8,128)(2,1)} async-done(((bf16[768,192]{1,0:T(8,128)(2,1)}), bf16[384,192]{1,0:T(8,128)(2,1)}) %reduce-scatter.89.cloned.1.call-update) | async-done | bytes 147472
  1170.5 12.6 %reduce-scatter.69.cloned.1.call-done = bf16[48,1536]{1,0:T(8,128)(2,1)} async-done(((bf16[48,3072]{1,0:T(8,128)(2,1)}), bf16[48,1536]{1,0:T(8,128)(2,1)}) %reduce-scatter.69.cloned.1.call-update) | async-done | bytes 147472 | tf_op jit(solution)/shard_map/reduce_scatter | solution.py:313
  (242 shorter events, 78.6 us)
Async XLA Ops:
  7.2 133.3 %copy-start = (bf16[768,768]{1,0:T(8,128)(2,1)S(1)}, bf16[768,768]{1,0:T(8,128)(2,1)}, u32[]{:S(2)}) copy-start(bf16[768,768]{1,0:T(8,128)(2,1)} %param.35) | copy-start | bytes 3538948
  7.2 89.6 %all-gather.11.cloned.1.call-start = ((), (), s32[]{:S(2)}) async-start(), calls=%async_computation.40 | async-start | bytes 2359296 | tf_op jit(solution)/shard_map/all_gather | solution.py:154
  9.3 21.3 %copy-start.36 = (f32[512]{0:T(512)}, f32[512]{0:T(512)S(1)}, u32[]{:S(2)}) copy-start(f32[512]{0:T(512)S(1)} %fusion.100) | copy-start | bytes 6148
  9.3 3.5 copy-start.15
  9.3 3.5 copy-start.24
  9.3 3.5 copy-start.38
  12.7 113.8 %all-gather.9.cloned.1.call-start = ((), (), s32[]{:S(2)}) async-start(), calls=%async_computation.39 | async-start | bytes 2359296 | tf_op jit(solution)/shard_map/all_gather | solution.py:155
  14.5 130.0 %all-gather.15.cloned.1.call-start = ((), (), s32[]{:S(2)}) async-start(), calls=%async_computation.42 | async-start | bytes 2359296 | tf_op jit(solution)/shard_map/all_gather | solution.py:167
  17.9 8.3 copy-start.47
  17.9 8.3 copy-start.48
  17.9 154.3 %all-gather.13.cloned.1.call-start = ((), (), s32[]{:S(2)}) async-start(), calls=%async_computation.41 | async-start | bytes 2359296 | tf_op jit(solution)/shard_map/all_gather | solution.py:168
  20.9 339.8 %reduce-scatter.45.cloned.1.call-start = ((), (), s32[]{:S(2)}) async-start(), calls=%async_computation.25 | async-start | bytes 2359296 | tf_op jit(solution)/shard_map/reduce_scatter | solution.py:237
  40.9 23.8 %copy-start.12 = (s32[512,1024]{0,1:T(8,128)}, s32[512,1024]{0,1:T(8,128)S(1)}, u32[]{:S(2)}) copy-start(s32[512,1024]{0,1:T(8,128)S(1)} %copy.77) | copy-start | bytes 6291460
  98.5 16.9 %copy-start.3 = (bf16[1024,768]{0,1:T(8,128)(2,1)}, bf16[1024,768]{0,1:T(8,128)(2,1)S(1)}, u32[]{:S(2)}) copy-start(bf16[1024,768]{0,1:T(8,128)(2,1)S(1)} %copy.76) | copy-start | bytes 4718596
  128.3 11.2 copy-start.18
  128.3 11.2 copy-start.16
  128.3 11.2 copy-start.49
  140.5 46.4 %copy-start.7 = (f32[1,512,768]{2,1,0:T(8,128)}, f32[1,512,768]{2,1,0:T(8,128)S(1)}, u32[]{:S(2)}) copy-start(f32[1,512,768]{2,1,0:T(8,128)S(1)} %get-tuple-element.85) | copy-start | bytes 4718596
  174.9 11.9 %copy-start.23 = (bf16[768,768]{1,0:T(8,128)(2,1)S(1)}, bf16[768,768]{1,0:T(8,128)(2,1)}, u32[]{:S(2)}) copy-start(bf16[768,768]{1,0:T(8,128)(2,1)} %param.38) | copy-start | bytes 3538948
  187.8 18.1 %copy-start.9 = (f32[1,512,768]{2,1,0:T(8,128)}, f32[1,512,768]{2,1,0:T(8,128)S(1)}, u32[]{:S(2)}) copy-start(f32[1,512,768]{2,1,0:T(8,128)S(1)} %get-tuple-element.89) | copy-start | bytes 4718596
  187.9 5.2 copy-start.30
  187.9 14.7 %slice-start = ((s8[4718592]{0:T(1024)(128)(4,1)}), s8[4194304]{0:T(1024)(128)(4,1)S(1)}, s32[]{:S(2)}) async-start(s8[4718592]{0:T(1024)(128)(4,1)} %bitcast.248), calls=%async_computation.52 | async-start | bytes 8388608
  193.1 9.5 copy-start.19
  193.1 9.5 slice-start.1
  228.3 21.8 %copy-start.11 = (bf16[1024,768]{0,1:T(8,128)(2,1)S(1)}, bf16[1024,768]{0,1:T(8,128)(2,1)}, u32[]{:S(2)}) copy-start(bf16[1024,768]{0,1:T(8,128)(2,1)} %copy.81) | copy-start | bytes 4718596
  250.1 8.6 copy-start.8
  276.7 87.4 %reduce-scatter.43.cloned.1.call-start = ((), (), s32[]{:S(2)}) async-start(), calls=%async_computation.24 | async-start | bytes 2359296 | tf_op jit(solution)/shard_map/reduce_scatter | solution.py:234
  295.2 16.8 %copy-start.14 = (bf16[512,768]{0,1:T(8,128)(2,1)S(1)}, bf16[512,768]{0,1:T(8,128)(2,1)}, u32[]{:S(2)}) copy-start(bf16[512,768]{0,1:T(8,128)(2,1)} %copy.75) | copy-start | bytes 2359300
  312.0 5.0 copy-start.2
  317.0 56.2 %reduce-scatter.49.cloned.1.call-start = ((), (), s32[]{:S(2)}) async-start(), calls=%async_computation.27 | async-start | bytes 2359296 | tf_op jit(solution)/shard_map/reduce_scatter | solution.py:204
  330.2 105.0 %reduce-scatter.65.cloned.1.call-start = ((), (), s32[]{:S(2)}) async-start(), calls=%async_computation.35 | async-start | bytes 1253376 | tf_op jit(solution)/shard_map/reduce_scatter | solution.py:278
  333.3 3.6 copy-start.29
  333.3 163.1 %reduce-scatter.59.cloned.1.call-start = ((), (), s32[]{:S(2)}) async-start(), calls=%async_computation.32 | async-start | bytes 1253376 | tf_op jit(solution)/shard_map/reduce_scatter | solution.py:269
  336.8 3.7 copy-start.4
  336.8 220.5 %reduce-scatter.57.cloned.1.call-start = ((), (), s32[]{:S(2)}) async-start(), calls=%async_computation.31 | async-start | bytes 1253376 | tf_op jit(solution)/shard_map/reduce_scatter | solution.py:266
  340.3 9.7 copy-start.17
  340.3 9.7 copy-start.37
  340.3 9.7 copy-start.39
  340.3 278.1 %reduce-scatter.51.cloned.1.call-start = ((), (), s32[]{:S(2)}) async-start(), calls=%async_computation.28 | async-start | bytes 1253376 | tf_op jit(solution)/shard_map/reduce_scatter | solution.py:257
  352.0 293.7 %reduce-scatter.47.cloned.1.call-start = ((), (), s32[]{:S(2)}) async-start(), calls=%async_computation.26 | async-start | bytes 2359296 | tf_op jit(solution)/shard_map/reduce_scatter | solution.py:201
  360.6 346.8 %reduce-scatter.55.cloned.1.call-start = ((), (), s32[]{:S(2)}) async-start(), calls=%async_computation.30 | async-start | bytes 1253376 | tf_op jit(solution)/shard_map/reduce_scatter | solution.py:263
  364.0 9.2 copy-start.52
  364.0 404.1 %reduce-scatter.53.cloned.1.call-start = ((), (), s32[]{:S(2)}) async-start(), calls=%async_computation.29 | async-start | bytes 1253376 | tf_op jit(solution)/shard_map/reduce_scatter | solution.py:260
  367.3 461.3 %reduce-scatter.85.cloned.1.call-start = ((), (), s32[]{:S(2)}) async-start(), calls=%async_computation.49 | async-start | bytes 1253376
  376.5 464.2 %reduce-scatter.87.cloned.1.call-start = ((), (), s32[]{:S(2)}) async-start(), calls=%async_computation.50 | async-start | bytes 294912
  437.0 416.8 %reduce-scatter.81.cloned.1.call-start = ((), (), s32[]{:S(2)}) async-start(), calls=%async_computation.47 | async-start | bytes 294912
  498.1 369.3 %reduce-scatter.79.cloned.1.call-start = ((), (), s32[]{:S(2)}) async-start(), calls=%async_computation.46 | async-start | bytes 294912
  559.0 322.2 %reduce-scatter.73.cloned.1.call-start = ((), (), s32[]{:S(2)}) async-start(), calls=%async_computation.43 | async-start | bytes 294912
  620.1 322.7 %reduce-scatter.83.cloned.1.call-start = ((), (), s32[]{:S(2)}) async-start(), calls=%async_computation.48 | async-start | bytes 1253376
  649.1 372.1 %reduce-scatter.71.cloned.1.call-start = ((), (), s32[]{:S(2)}) async-start(), calls=%async_computation.38 | async-start | bytes 5013504 | tf_op jit(solution)/shard_map/reduce_scatter | solution.py:284
  657.8 442.4 %reduce-scatter.67.cloned.1.call-start = ((), (), s32[]{:S(2)}) async-start(), calls=%async_computation.36 | async-start | bytes 5013504 | tf_op jit(solution)/shard_map/reduce_scatter | solution.py:281
  665.7 481.4 %reduce-scatter.77.cloned.1.call-start = ((), (), s32[]{:S(2)}) async-start(), calls=%async_computation.45 | async-start | bytes 294912
  709.1 439.6 %reduce-scatter.75.cloned.1.call-start = ((), (), s32[]{:S(2)}) async-start(), calls=%async_computation.44 | async-start | bytes 294912
  769.8 60.7 %copy-start.27 = (bf16[12,64,512]{2,1,0:T(8,128)(2,1)S(1)}, bf16[12,64,512]{2,1,0:T(8,128)(2,1)}, u32[]{:S(2)}) copy-start(bf16[12,64,512]{2,1,0:T(8,128)(2,1)} %copy-done.26) | copy-start | bytes 2359300
  769.8 380.6 %reduce-scatter.63.cloned.1.call-start = ((), (), s32[]{:S(2)}) async-start(), calls=%async_computation.34 | async-start | bytes 294912 | tf_op jit(solution)/shard_map/reduce_scatter | solution.py:307
  830.4 323.1 %reduce-scatter.61.cloned.1.call-start = ((), (), s32[]{:S(2)}) async-start(), calls=%async_computation.33 | async-start | bytes 294912 | tf_op jit(solution)/shard_map/reduce_scatter | solution.py:304
  944.5 224.2 %reduce-scatter.89.cloned.1.call-start = ((), (), s32[]{:S(2)}) async-start(), calls=%async_computation.51 | async-start | bytes 589824
  1023.2 159.9 %reduce-scatter.69.cloned.1.call-start = ((), (), s32[]{:S(2)}) async-start(), calls=%async_computation.37 | async-start | bytes 442368 | tf_op jit(solution)/shard_map/reduce_scatter | solution.py:313
  1100.3 3.9 copy-start.42
  1100.3 3.9 copy-start.43
  1100.3 3.9 copy-start.44
  1100.3 43.9 %copy-start.35 = (f32[512]{0:T(512)S(1)}, f32[512]{0:T(512)}, u32[]{:S(2)}) copy-start(f32[512]{0:T(512)} %copy-done.34) | copy-start | bytes 6148
  1100.3 43.9 %copy-start.6 = (f32[1,512,768]{2,1,0:T(8,128)S(1)}, f32[1,512,768]{2,1,0:T(8,128)}, u32[]{:S(2)}) copy-start(f32[1,512,768]{2,1,0:T(8,128)} %copy-done.5) | copy-start | bytes 4718596
  1144.3 40.5 %copy-start.1 = (bf16[768,768]{1,0:T(8,128)(2,1)S(1)}, bf16[768,768]{1,0:T(8,128)(2,1)}, u32[]{:S(2)}) copy-start(bf16[768,768]{1,0:T(8,128)(2,1)} %param.35) | copy-start | bytes 3538948
  (20 other events, 38.2 us)
Sparse Core Ops, SparseCore 0:
  12.8 29.9 all-gather.10
  45.0 27.2 all-gather.8
  73.8 27.1 all-gather.14
  102.4 27.1 all-gather.12
  276.8 27.6 reduce-scatter.44
  317.1 27.6 reduce-scatter.42
  347.0 26.0 reduce-scatter.48
  377.2 58.0 reduce-scatter.64
  439.3 57.0 reduce-scatter.58
  500.3 56.9 reduce-scatter.56
  561.4 56.9 reduce-scatter.50
  620.5 25.0 reduce-scatter.46
  649.3 58.0 reduce-scatter.54
  710.9 57.1 reduce-scatter.52
  771.5 57.0 reduce-scatter.84
  830.7 9.9 reduce-scatter.86
  842.8 10.9 reduce-scatter.80
  856.4 10.9 reduce-scatter.78
  870.2 10.9 reduce-scatter.72
  884.7 58.0 reduce-scatter.82
  946.6 74.5 reduce-scatter.70
  1025.6 74.6 reduce-scatter.66
  1102.5 10.3 reduce-scatter.76
  1115.5 10.9 reduce-scatter.74
  1128.7 11.0 reduce-scatter.62
  1142.5 10.9 reduce-scatter.60
  1155.6 13.0 reduce-scatter.88
  1171.0 12.0 reduce-scatter.68
where the time goes:
time: 1200 us; the launch traced here: 1190 us
  waiting for transfers between devices  659 us (55%)
  matrix products  281 us (23%)
  local copies, waits for them, and re-layouts  105 us (9%)
  other arithmetic  79.2 us (7%)
  blocking collectives  49.7 us (4%)
  between operations  15.6 us (1%)
    unnamed x37, waiting for transfers between devices  168 us
    reduce_scatter x1, waiting for transfers between devices, on_device(): lax.psum_scatter(ffn_out_grad.astype(jnp.bfloat16), 'dp', scatter_dimensi...  73.2 us
    reduce_scatter x1, waiting for transfers between devices, on_device(): lax.psum_scatter(ffn_in_grad.astype(jnp.bfloat16), 'dp', scatter_dimensio...  72.2 us
    reduce_scatter x1, waiting for transfers between devices, on_device(): lax.psum_scatter(cross_query_grad.astype(jnp.bfloat16), 'dp', scatter_dim...  59.4 us
    reduce_scatter x1, waiting for transfers between devices, on_device(): lax.psum_scatter(self_query_grad.astype(jnp.bfloat16), 'dp', scatter_dime...  59.3 us
    reduce_scatter x1, waiting for transfers between devices, on_device(): lax.psum_scatter(self_out_grad.astype(jnp.bfloat16), 'dp', scatter_dimens...  59.1 us
    reduce_scatter x1, waiting for transfers between devices, on_device(): lax.psum_scatter(cross_out_grad.astype(jnp.bfloat16), 'dp', scatter_dimen...  58.7 us
    reduce_scatter x1, waiting for transfers between devices, on_device(): lax.psum_scatter(self_key_grad.astype(jnp.bfloat16), 'dp', scatter_dimens...  45.3 us
  transfers between devices with their start and end apart: 28, of which 19 were waited for; matrix products, arithmetic and copies ran while one was open for 29% of the time, Pallas kernels for 0%

commit v1 on v0

v1 whole, which is shorter than its diff:
```python
import copy
import functools
import math

import jax
import jax.numpy as jnp
import numpy as np
from jax import lax
from jax.experimental import pallas as pl
from jax.experimental.pallas import tpu as pltpu
from jax.sharding import PartitionSpec as P

HEADS = 12
HEAD_DIM = 64
BUCKETS = 32
MAX_DIST = 128
PAIRS = HEADS // 2
LANES = 128

EPSILON = 1e-06
NEGATIVE = -(2.0**30)
LOG2E = math.log2(math.e)
LN2 = math.log(2.0)
VMEM_LIMIT = 12 * 1024 * 1024
BF16 = jnp.bfloat16
F32 = jnp.float32


def bucket_edges():
    exact_max = BUCKETS // 2
    return [
        math.ceil(exact_max * (MAX_DIST / exact_max) ** (degree / exact_max))
        for degree in range(1, exact_max)
    ]


def rel_bucket(distance):
    exact_max = BUCKETS // 2
    log_bucket = exact_max + sum(
        (distance >= edge).astype(np.int32) for edge in bucket_edges()
    )
    return np.where(distance < exact_max, distance, log_bucket)


FAR = bucket_edges()[-1]


def near_types(block):
    return (FAR - 1 + block - 1) // block + 1


def group_of(dp, mem, mem_size):
    half = mem_size // 2
    return (dp % 2) * half + mem % half


def row_moves(dp_size, mem_size):
    half = mem_size // 2
    moves = ([], [])
    for dp in range(dp_size):
        for mem in range(mem_size):
            for piece in range(2):
                chunk = 2 * mem + piece
                group = chunk if chunk < mem_size else 2 * mem_size - 1 - chunk
                to_dp = dp - dp % 2 + group // half
                to_mem = (dp % 2) * half + group % half
                moves[piece].append((dp * mem_size + mem, to_dp * mem_size + to_mem))
    return moves


def to_rows(values, axis=0):
    moves = row_moves(lax.axis_size("dp"), lax.axis_size("mem"))
    return tuple(
        lax.ppermute(piece, ("dp", "mem"), move) for piece, move in zip(jnp.split(values, 2, axis=axis), moves)
    )


def arranged(pieces, odd, axis=0):
    first, second = pieces
    return jnp.concatenate(
        [jnp.where(odd, second, first), jnp.where(odd, first, second)], axis=axis
    )


def from_rows(values, odd, axis=0):
    moves = row_moves(lax.axis_size("dp"), lax.axis_size("mem"))
    low, high = jnp.split(values, 2, axis=axis)
    first, second = jnp.where(odd, high, low), jnp.where(odd, low, high)
    back = [[(there, here) for here, there in move] for move in moves]
    first = lax.ppermute(first, ("dp", "mem"), back[0])
    second = lax.ppermute(second, ("dp", "mem"), back[1])
    return jnp.concatenate([first, second], axis=axis)


def group_shift(values, step):
    dp_size, mem_size = lax.axis_size("dp"), lax.axis_size("mem")
    half = mem_size // 2
    moves = []
    for dp in range(dp_size):
        for mem in range(mem_size):
            group = (group_of(dp, mem, mem_size) + step) % mem_size
            to_dp = dp - dp % 2 + group // half
            to_mem = mem - mem % half + group % half
            moves.append((dp * mem_size + mem, to_dp * mem_size + to_mem))
    return lax.ppermute(values, ("dp", "mem"), moves)


def others(values):
    return [group_shift(values, step) for step in range(1, lax.axis_size("mem"))]


def came_parts(parts, rows):
    came = [
        group_shift(parts[:, (step - 1) * rows : step * rows], -step) for step in range(1, lax.axis_size("mem"))
    ]
    return came[0] if len(came) == 1 else sum(part.astype(F32) for part in came)


def block_list(group, mem_size, rows):
    piece = rows // 2
    q_at, k_at, kinds, is_low = [], [], [], []
    for i in range(2 * mem_size + 1):
        low = i <= group
        chunk = jnp.where(low, i, i - (group + 1))
        owner = jnp.where(chunk < mem_size, chunk, 2 * mem_size - 1 - chunk)
        slot = (group - owner) % mem_size
        q_at.append(jnp.where(low, 0, piece))
        k_at.append(slot * rows + jnp.where(chunk < mem_size, 0, piece))
        kinds.append(jnp.where(low, group - i, 2 * mem_size - i))
        is_low.append(low.astype(jnp.int32))
    return jnp.stack([jnp.stack(v).astype(jnp.int32) for v in (q_at, k_at, kinds, is_low)])


def bias_of(distance, rel_bias):
    hot = (rel_bucket(np.maximum(distance, 0))[..., None] == np.arange(BUCKETS)).astype(np.float32)
    values = jnp.einsum(
        "...b,bh->h...", jnp.asarray(hot), rel_bias - rel_bias[BUCKETS - 1], precision=lax.Precision.HIGHEST
    )
    return jnp.where(jnp.asarray(distance >= 0), values * LOG2E, NEGATIVE)


def spread(row, rows):
    width = row.shape[1]
    table = jnp.broadcast_to(row, (8, width))
    place = lax.broadcasted_iota(jnp.int32, (8, width), 0)
    for bit in range(3):
        moved = pltpu.roll(table, 1 << bit, 1)
        table = jnp.where((place >> bit) & 1 == 1, moved, table)
    size = 8
    while size < rows:
        table = jnp.concatenate([table, pltpu.roll(table, size, 1)], axis=0)
        size *= 2
    return table


def small_block(block):
    return min(LANES, block)


def table_kernel(base_ref, base_t_ref, table_ref, table_t_ref):
    heads, kinds, block = table_ref.shape[0], table_ref.shape[1] - 2, table_ref.shape[2]
    for head in range(heads):
        for base, table in ((base_ref, table_ref), (base_t_ref, table_t_ref)):
            table[head, 0] = jnp.full((block, block), NEGATIVE, F32)
            table[head, kinds + 1] = jnp.zeros((block, block), F32)
            for kind in range(kinds):
                table[head, kind + 1] = spread(base[head, kind], block)[:, block:]


def bias_tables(rel_bias, block):
    kinds = near_types(block)
    at = np.arange(2 * block)[None, :] - block
    start = np.arange(kinds)[:, None] * block
    base, base_t = bias_of(start - at, rel_bias), bias_of(start + at, rel_bias)
    if block % LANES:
        step = np.arange(block)[None, :] - np.arange(block)[:, None] + block
        masked = jnp.full((HEADS, 1, block, block), NEGATIVE, F32)
        return [jnp.concatenate([masked, v[:, :, step], jnp.zeros_like(masked)], axis=1) for v in (base, base_t)]
    heads = HEADS // 3
    spec = pl.BlockSpec((heads, kinds, 1, 2 * block), lambda h: (h, 0, 0, 0))
    out = pl.BlockSpec((heads, kinds + 2, block, block), lambda h: (h, 0, 0, 0))
    shape = jax.ShapeDtypeStruct((HEADS, kinds + 2, block, block), F32)
    return pl.pallas_call(
        table_kernel,
        grid=(HEADS // heads,),
        in_specs=[spec, spec],
        out_specs=[out, out],
        out_shape=[pltpu.HBM(shape.shape, shape.dtype)] * 2,
        compiler_params=pltpu.CompilerParams(vmem_limit_bytes=VMEM_LIMIT),
        name="bias_tables",
    )(base[:, :, None, :], base_t[:, :, None, :])


def small_parts(block, small):
    return [(r, c, (r - c) // small) for r in range(0, block, small) for c in range(0, block, small)]


def kind_index(step, kind, block, small, kinds):
    return jnp.clip(kind * (block // small) + step + 1, 0, kinds + 1)


def with_bias(s, table_ref, head, kind, turned=False):
    block, small, kinds = s.shape[0], table_ref.shape[2], table_ref.shape[1] - 2
    fixed = isinstance(kind, int)
    if fixed and (kind - 1) * block >= FAR - 1:
        return s
    pieces = {}
    for r, c, step in small_parts(block, small):
        at = (c, r) if turned else (r, c)
        part = s[at[0] : at[0] + small, at[1] : at[1] + small]
        if fixed:
            step = kind * (block // small) + step
            if step < kinds:
                part = part + table_ref[head, step + 1] if step >= 0 else jnp.full(part.shape, NEGATIVE, F32)
        else:
            part = part + table_ref[head, kind_index(step, kind, block, small, kinds)]
        pieces[at] = part
    starts = range(0, block, small)
    return jnp.concatenate([jnp.concatenate([pieces[a, b] for b in starts], axis=1) for a in starts], axis=0)


def add_grad(ds, grad_ref, head, kind):
    block, small, kinds = ds.shape[0], grad_ref.shape[2], grad_ref.shape[1] - 2
    fixed = isinstance(kind, int)
    for r, c, step in small_parts(block, small):
        part = ds[c : c + small, r : r + small]
        if fixed:
            step = kind * (block // small) + step
            if not 0 <= step < kinds:
                continue
            at = step + 1
        else:
            at = kind_index(step, kind, block, small, kinds)
        grad_ref[head, at] = grad_ref[head, at] + part


def fold(table):
    rows, width = table.shape
    while rows > 1:
        rows //= 2
        table = table[:rows] + pltpu.roll(table[rows:], width - rows, 1)
    return table


def fold_kernel(first_ref, rest_ref, cross_ref, ffn_ref, sums_ref):
    kinds = first_ref.shape[1] - 2
    sums_ref[...] = jnp.zeros_like(sums_ref)
    sums_ref[1:2, :], sums_ref[2:3, :] = cross_ref[...], ffn_ref[...]
    for part, ref in enumerate((first_ref, rest_ref)):
        heads = ref.shape[0]
        for head in range(heads):
            for kind in range(kinds):
                table = ref[head, kind + 1]
                width = 2 * table.shape[1]
                wide = jnp.concatenate([table, jnp.zeros_like(table)], axis=1)
                row = FIRST_HEAD_ROW + part * heads + head
                sums_ref[row : row + 1, kind * width : (kind + 1) * width] = fold(wide)


def table_sums(first, rest, cross_grad, ffn_grad):
    kinds, block = first.shape[1] - 2, first.shape[2]
    shape = (SMALL_ROWS, cross_grad.shape[1])
    if block % LANES:
        grad_t = jnp.pad(jnp.concatenate([first, rest])[:, 1 : kinds + 1], ((0, 0), (0, 0), (0, 0), (0, block)))
        place = (np.arange(block)[:, None] + np.arange(2 * block)[None, :]) % (2 * block)
        sums = jnp.sum(grad_t[:, :, np.arange(block)[:, None], place], axis=2).reshape(HEADS, -1)
        small = jnp.zeros(shape, F32).at[1].set(cross_grad[0]).at[2].set(ffn_grad[0])
        return small.at[FIRST_HEAD_ROW : FIRST_HEAD_ROW + HEADS, : sums.shape[1]].set(sums)
    return run(
        fold_kernel,
        "table_sums",
        (1,),
        [(first, None, pltpu.HBM), (rest, None, pltpu.HBM), (cross_grad, None), (ffn_grad, None)],
        [(shape, F32, None)],
    )[0]


def bucket_hot(block):
    kinds = near_types(block)
    at = np.arange(2 * block)[None, :]
    at = np.where(at < block, at, at - 2 * block) + np.arange(kinds)[:, None] * block
    near = (at >= 0) & (at < FAR)
    hot = (rel_bucket(np.maximum(at, 0))[..., None] == np.arange(BUCKETS)) & near[..., None]
    return hot.reshape(-1, BUCKETS).T.astype(np.float32)


def write_kernel(chunks, *refs):
    counts, chunks = chunks
    totals, at = [], 0
    for count in counts:
        parts = [ref[...].astype(F32) for ref in refs[at : at + count]]
        totals.append(sum(parts[1:], parts[0]))
        at += count
    ffn, rest, own = totals
    small, hot = refs[at][...], refs[at + 1][...]
    refs = refs[at + 2 :]
    gains, table_ref, fo_ref, fi_ref, squares = refs[:3], refs[3], refs[4], refs[5], refs[6:]
    for i in range(3):
        gains[i][...] = small[i : i + 1, :]
    sums = small[FIRST_HEAD_ROW : FIRST_HEAD_ROW + HEADS, : hot.shape[1]]
    near = lax.dot_general(
        hot, sums, (((1,), (1,)), ((), ())), precision=lax.Precision.HIGHEST, preferred_element_type=F32
    )
    last = -jnp.sum(near, axis=0, keepdims=True)
    bucket = lax.broadcasted_iota(jnp.int32, near.shape, 0)
    table_ref[...] = jnp.where(bucket == BUCKETS - 1, last, near)
    rows, cols = fo_ref.shape
    fo_ref[...] = ffn[:rows]
    each = fi_ref.shape[0]
    for i in range(chunks):
        fi_ref[:, i * cols : (i + 1) * cols] = ffn[rows + i * each : rows + (i + 1) * each]
    at = 0
    for total in (rest, own):
        for i in range(total.shape[0] // each):
            squares[at][...] = total[i * each : (i + 1) * each]
            at += 1


def write_grads(ffn, rest, own, small, block, width, hidden):
    dp_size, mem_size = lax.axis_size("dp"), lax.axis_size("mem")
    hot = jnp.asarray(bucket_hot(block))
    square = ((width // dp_size, width // mem_size), F32, None)
    return run(
        functools.partial(write_kernel, ([1 + len(s.came) for s in (ffn, rest, own)], hidden // width)),
        "write_grads",
        (1,),
        [(v.reshape(v.shape[-2:]), None) for s in (ffn, rest, own) for v in (s.keep, *s.came)]
        + [(v, None) for v in (small, hot)],
        [((1, width), F32, None)] * 3
        + [
            ((BUCKETS, HEADS), F32, None),
            ((hidden // dp_size, width // mem_size), F32, None),
            ((width // dp_size, hidden // mem_size), F32, None),
        ]
        + [square] * 8,
    )


def nt(a, b):
    return lax.dot_general(a, b, (((1,), (1,)), ((), ())), preferred_element_type=F32)


def nn(a, b):
    return jnp.dot(a, b, preferred_element_type=F32)


def half_of(values, head):
    lane = lax.broadcasted_iota(jnp.int32, values.shape, 1)
    return jnp.where((lane >= HEAD_DIM) == (head == 1), values, jnp.zeros_like(values))


def join_halves(first, second):
    lane = lax.broadcasted_iota(jnp.int32, first.shape, 1)
    return jnp.where(lane < HEAD_DIM, first, second)


def in_three(values):
    high = values.astype(BF16)
    rest = values - high.astype(F32)
    mid = rest.astype(BF16)
    low = (rest - mid.astype(F32)).astype(BF16)
    return high, mid, low


def put_lanes(base, start, values):
    lane = lax.broadcasted_iota(jnp.int32, base.shape, 1)
    for i, value in enumerate(values):
        base = jnp.where(lane == start + i, value, base)
    return base


def with_log_sum(mask_lanes, log_sum):
    pieces = [piece.astype(F32) for piece in in_three(-log_sum)]
    return put_lanes(mask_lanes.astype(F32), 3, pieces).astype(BF16)


def bit_count(axis):
    return lax.axis_size(axis).bit_length() - 1


def swap(values, axis, bit):
    size = lax.axis_size(axis)
    return lax.ppermute(values, axis, [(i, i ^ (1 << bit)) for i in range(size)])


def swap_many(values, names):
    dp_size, mem_size = lax.axis_size("dp"), lax.axis_size("mem")
    flips = {axis: sum(1 << bit for name, bit in names if name == axis) for axis in ("dp", "mem")}
    moves = [
        (dp * mem_size + mem, (dp ^ flips["dp"]) * mem_size + (mem ^ flips["mem"]))
        for dp in range(dp_size)
        for mem in range(mem_size)
    ]
    return lax.ppermute(values, ("dp", "mem"), moves)


def bit_order(order):
    dp_bits, mem_bits = bit_count("dp"), bit_count("mem")
    z_bits = [("dp", b) for b in range(2, dp_bits)]
    groups = {
        "x": [("mem", b) for b in range(mem_bits)],
        "y": [("dp", b) for b in range(1, min(2, dp_bits))],
        "Z": z_bits[:1],
        "z": z_bits[1:] if "Z" in order else z_bits,
    }
    return [step for name in order for step in groups[name]]


def in_pairs(names):
    return [tuple(names[i : i + 2]) for i in range(0, len(names), 2)]


SMALL_ROWS = 16
FIRST_HEAD_ROW = 4


TILE = 256
LIMITS = {
    "own_project": 12,
    "other_project": 12,
    "encoder_project": 12,
    "self_forward": 18,
    "cross_forward": 18,
    "feed_forward": 34,
    "cross_backward": 18,
    "cross_finish": 30,
    "encoder_finish": 18,
    "self_backward": 18,
    "table_sums": 12,
    "query_grad": 12,
    "key_grads": 18,
    "self_finish_back": 18,
    "advance": 24,
    "write_grads": 16,
}


def tn(a, b):
    return lax.dot_general(a, b, (((0,), (0,)), ((), ())), preferred_element_type=F32)


def normed(hidden, gain):
    return hidden * lax.rsqrt(jnp.mean(hidden * hidden, axis=-1, keepdims=True) + EPSILON) * gain


def norm_back(hidden, gain, grad):
    scale = lax.rsqrt(jnp.mean(hidden * hidden, axis=-1, keepdims=True) + EPSILON)
    unit = hidden * scale
    inner = grad * gain
    out = scale * (inner - unit * jnp.mean(inner * unit, axis=-1, keepdims=True))
    return out, jnp.sum(grad * unit, axis=0, keepdims=True)


def whole(array):
    zeros = (0,) * array.ndim
    return pl.BlockSpec(array.shape, lambda *_: zeros)


def run(kernel, name, grid, ins, outs, scratch=(), scalars=(), after=(), flops=0, aliases=None):
    count = len(scalars) + len(ins)
    in_places = [v[2] if len(v) > 2 else None if v[1] is None or v[1] is ANY else pltpu.HBM for v in ins]
    out_places = [v[3] if len(v) > 3 else None if v[2] is None else pltpu.HBM for v in outs]
    ins, outs = [v[:2] for v in ins], [v[:3] for v in outs]

    def body(*refs):
        kernel(*refs[:count], *refs[count + len(after) :])

    out_shape = [jax.ShapeDtypeStruct(shape, dtype) for shape, dtype, _ in outs]
    placed = [o if p is None else p(o.shape, o.dtype) for o, p in zip(out_shape, out_places)]
    arrays = [a if p is None else pltpu.with_memory_space_constraint(a, p) for (a, _), p in zip(ins, in_places)]
    moved = sum(a.size * a.dtype.itemsize for a, _ in ins) + sum(
        math.prod(s) * jnp.dtype(d).itemsize for s, d, _ in outs
    )
    return pl.pallas_call(
        body,
        grid_spec=pltpu.PrefetchScalarGridSpec(
            num_scalar_prefetch=len(scalars),
            grid=grid,
            in_specs=[whole(a) if s is None else s for a, s in ins]
            + [pl.BlockSpec(memory_space=pl.ANY) for _ in after],
            out_specs=[whole(o) if s is None else s for o, (_, _, s) in zip(out_shape, outs)],
            scratch_shapes=list(scratch),
        ),
        out_shape=placed,
        input_output_aliases=aliases or {},
        compiler_params=pltpu.CompilerParams(vmem_limit_bytes=LIMITS[name] << 20),
        cost_estimate=pl.CostEstimate(flops=flops // 16, bytes_accessed=moved // 16, transcendentals=0),
        name=name,
    )(*scalars, *arrays, *after)


ANY = pl.BlockSpec(memory_space=pl.ANY)


def row_spec(tile, width, shift=0):
    return pl.BlockSpec((tile, width), lambda i, *_: (i + shift, 0))


def fits(rows, cols):
    dp_size, mem_size = lax.axis_size("dp"), lax.axis_size("mem")
    return (rows // dp_size) % 16 == 0 and (cols // mem_size) % LANES == 0


def emit(mine, total_ref, keep_ref, send_ref, at, rows):
    mem_size, pairs, _, cols = keep_ref.shape
    chunks = total_ref.shape[1] // cols // mem_size
    for pair in range(pairs):
        keep_at = pl.multiple_of((2 * pair + mine) * rows, 16)
        send_at = pl.multiple_of((2 * pair + 1 - mine) * rows, 16)
        for mem in range(mem_size):
            for chunk in range(chunks):
                lanes = slice((mem * chunks + chunk) * cols, (mem * chunks + chunk + 1) * cols)
                place = slice(at + chunk * rows, at + (chunk + 1) * rows)
                keep_ref[mem, pair, place, :] = total_ref[pl.ds(keep_at, rows), lanes].astype(BF16)
                send_ref[mem, pair, place, :] = total_ref[pl.ds(send_at, rows), lanes].astype(BF16)


def square_outs(count, width):
    dp_size, mem_size = lax.axis_size("dp"), lax.axis_size("mem")
    if fits(width, width):
        shape = (mem_size, dp_size // 2, count * width // dp_size, width // mem_size)
        return [(shape, BF16, None)] * 2
    return [((width, width), BF16, None)] * count


def write_square(mine, index, total, total_ref, out_refs):
    if len(out_refs[0].shape) == 4:
        keep_ref, send_ref = out_refs
        rows = total.shape[0] // (2 * keep_ref.shape[1])
        total_ref[...] = total
        emit(mine, total_ref, keep_ref, send_ref, index * rows, rows)
    else:
        out_refs[index][...] = total.astype(BF16)


def in_order(grads, chunks=1):
    if grads[0].ndim == 4:
        return grads
    dp_size, mem_size = lax.axis_size("dp"), lax.axis_size("mem")
    cuts = []
    for grad in grads:
        rows, cols = grad.shape[0] // dp_size, grad.shape[1] // mem_size // chunks
        cut = grad.reshape(dp_size // 2, 2, rows, mem_size, chunks, cols).transpose(1, 3, 0, 4, 2, 5)
        cuts.append(cut.reshape(2, mem_size, dp_size // 2, chunks * rows, cols))
    cut = jnp.concatenate(cuts, axis=3)
    mine = lax.axis_index("dp") & 1
    return [lax.dynamic_index_in_dim(cut, which, 0, keepdims=False) for which in (mine, 1 - mine)]


class Scatter:
    def __init__(self, grads, order, chunks=1):
        keep, send = in_order(grads, chunks)
        mem_bits, dp_bits = bit_count("mem"), bit_count("dp")
        self.names = [("mem", b) for b in reversed(range(mem_bits))]
        self.names += [("dp", b) for b in reversed(range(1, dp_bits))]
        self.order = []
        for part in order.split("]"):
            single, _, paired = part.partition("[")
            self.order += [(name,) for name in bit_order(single)] + in_pairs(bit_order(paired))
        shape = (2,) * len(self.names) + keep.shape[2:]
        self.keep, self.came = keep.reshape(shape), [swap(send, "dp", 0).reshape(shape)]
        self.span = (0, shape[-2])

    def parts(self, *orders):
        size = self.span[1] // len(orders)
        shares = []
        for i, order in enumerate(orders):
            share = copy.copy(self)
            share.names, share.span = list(self.names), (i * size, size)
            share.order = [(name,) for name in bit_order(order)]
            shares.append(share)
        return shares


def all_bits():
    return [("mem", b) for b in range(bit_count("mem"))] + [("dp", b) for b in range(bit_count("dp"))]


def bit_values():
    return jnp.stack([((lax.axis_index(axis) >> bit) & 1).astype(jnp.int32) for axis, bit in all_bits()])


def level(*group, bits):
    while any(v.order != group[0].order for v in group):
        longest = max(sum(map(len, v.order)) for v in group)
        advance(bits, *[v for v in group if sum(map(len, v.order)) == longest])


def advance_kernel(moves, bits, *refs):
    outs = refs[sum(parts for _, sources in moves for _, _, parts in sources) :]
    ref_at = out_at = 0
    for names, sources in moves:
        flips = [(0,), (1,)] if len(names) == 1 else [(0, 0), (0, 1), (1, 0), (1, 1)]
        start = 0
        for from_row, size, parts in sources:
            ins = refs[ref_at : ref_at + parts]
            ref_at += parts
            for pre in range(ins[0].shape[0]):
                for mid in range(ins[0].shape[2]):
                    for post in range(ins[0].shape[4]):
                        for out, flip in zip(outs[out_at : out_at + len(flips)], flips):
                            place = [bits[name] if f == 0 else 1 - bits[name] for name, f in zip(names, flip)]
                            place = place + [0] if len(place) == 1 else place
                            rows = slice(from_row, from_row + size)
                            values = [ref[pre, place[0], mid, place[1], post, rows, :].astype(F32) for ref in ins]
                            out[pre, mid, post, start : start + size, :] = sum(values[1:], values[0]).astype(BF16)
            start += size
        out_at += len(flips)


def advance(bits, *groups):
    groups = [group if isinstance(group, tuple) else (group,) for group in groups]
    for group in groups:
        lead = group[0]
        assert all(v.names == lead.names and v.order == lead.order for v in group)
        if not lead.order and len(group) > 1:
            sums = [sum(v.came, v.keep.astype(F32))[..., v.span[0] : sum(v.span), :] for v in group]
            lead.keep = jnp.concatenate(sums, axis=-2)
            lead.came, lead.span = [jnp.zeros_like(lead.keep)], (0, lead.keep.shape[-2])
    groups = [group for group in groups if group[0].order]
    if not groups:
        return
    moves, arrays, heads = [], [], []
    for group in groups:
        lead = group[0]
        names = lead.order.pop(0)
        places = [lead.names.index(name) for name in names]
        if places != sorted(places):
            names, places = names[::-1], places[::-1]
        pre = 2 ** places[0]
        mid = 2 ** (places[1] - places[0] - 1) if len(names) == 2 else 1
        post = 2 ** (len(lead.names) - len(names)) // pre // mid
        second = len(names)
        lead.names = [name for name in lead.names if name not in names]
        rows, cols = [v.span for v in group], lead.keep.shape[-1]
        moves.append(([all_bits().index(name) for name in names], [(*r, 1 + len(v.came)) for r, v in zip(rows, group)]))
        arrays.append(
            [v.reshape(pre, 2, mid, second, post, v.shape[-2], cols) for s in group for v in (s.keep, *s.came)]
        )
        heads.append((names, pre, mid, post, sum(size for _, size in rows), cols))
    total = sum(v.size * 2 for group in arrays for v in group)
    steps = 1
    if total > 8 << 20:
        steps = next(n for n in (4, 2, 1) if all(pre % n == 0 or post % n == 0 for _, pre, _, post, _, _ in heads))
    ins, outs = [], []
    for group, (names, pre, mid, post, rows, cols) in zip(arrays, heads):
        by_pre = pre % steps == 0
        own_pre, own_post = (pre // steps, post) if by_pre else (pre, post // steps)
        for array in group:
            block = (own_pre, 2, mid, array.shape[3], own_post) + array.shape[5:]
            place = (lambda i, *_: (i, 0, 0, 0, 0, 0, 0)) if by_pre else (lambda i, *_: (0, 0, 0, 0, i, 0, 0))
            ins.append((array, None if steps == 1 else pl.BlockSpec(block, place)))
        place = (lambda i, *_: (i, 0, 0, 0, 0)) if by_pre else (lambda i, *_: (0, 0, i, 0, 0))
        spec = None if steps == 1 else pl.BlockSpec((own_pre, mid, own_post, rows, cols), place)
        outs += [((pre, mid, post, rows, cols), BF16, spec)] * 2 ** len(names)
    results = run(
        functools.partial(advance_kernel, moves), "advance", (steps,), ins, outs, scalars=(bits,), flops=total
    )
    for group, (names, pre, mid, post, rows, cols) in zip(groups, heads):
        lead = group[0]
        lead.span = (0, rows)
        lead.keep, *sends = [v.reshape((2,) * len(lead.names) + (rows, cols)) for v in results[: 2 ** len(names)]]
        results = results[2 ** len(names) :]
        partners = [names] if len(names) == 1 else [names[1:], names[:1], names]
        lead.came = [swap_many(send, partner) for send, partner in zip(sends, partners)]


def fence(scatters, *values):
    states = [(v.keep, v.came) for v in scatters]
    states, values = lax.optimization_barrier((states, values))
    for scatter, (keep, came) in zip(scatters, states):
        scatter.keep, scatter.came = keep, came
    return values


def head_norms(rows):
    wide = rows.astype(F32)
    shape = (rows.shape[1], LANES)
    head = lax.broadcasted_iota(jnp.int32, shape, 0) // HEAD_DIM == lax.broadcasted_iota(jnp.int32, shape, 1)
    return jnp.max(nn((wide * wide).astype(BF16), head.astype(F32).astype(BF16)), axis=0, keepdims=True)


def put_norms(norm_ref, rows):
    norms = head_norms(rows)

    @pl.when(pl.program_id(0) == 0)
    def _():
        norm_ref[...] = norms

    @pl.when(pl.program_id(0) > 0)
    def _():
        norm_ref[...] = jnp.maximum(norm_ref[...], norms)


def tag_lanes(tags, first):
    lane = lax.broadcasted_iota(jnp.int32, tags.shape, 1)
    tags = tags.astype(F32)
    kept = (tags[:, first : first + 1] == lane.astype(F32)) & (tags[:, first + 1 : first + 2] > 0)
    lanes = jnp.where(lane < 3, jnp.where(kept, 0.0, NEGATIVE), 0.0)
    return jnp.where((lane >= 3) & (lane < 6), 1.0, lanes).astype(BF16)


def own_project_kernel(
    x_ref,
    gain_ref,
    wq_ref,
    wk_ref,
    wv_ref,
    a_ref,
    q_ref,
    k_ref,
    v_ref,
    dec_ref,
    enc_ref,
    q_lanes_ref,
    q_norm_ref,
    k_norm_ref,
):
    width = gain_ref.shape[1]
    a = normed(x_ref[:, :width].astype(F32), gain_ref[...]).astype(BF16)
    a_ref[...] = a
    q = (nn(a, wq_ref[...]) * LOG2E).astype(BF16)
    k = nn(a, wk_ref[...]).astype(BF16)
    q_ref[...], k_ref[...] = q, k
    v_ref[...] = nn(a, wv_ref[...]).astype(BF16)
    put_norms(q_norm_ref, q), put_norms(k_norm_ref, k)
    tags = x_ref[:, width:]
    dec_ref[...], enc_ref[...] = tag_lanes(tags, 0), tag_lanes(tags, 2)
    lane = lax.broadcasted_iota(jnp.int32, tags.shape, 1)
    q_lanes_ref[...] = ((tags[:, 0:1].astype(F32) == lane.astype(F32)) & (lane < 3)).astype(F32).astype(BF16)


def other_project_kernel(
    x_ref,
    gain_ref,
    wk_ref,
    wv_ref,
    k_old,
    v_old,
    dec_old,
    enc_old,
    k_ref,
    v_ref,
    dec_ref,
    enc_ref,
    k_norm_ref,
):
    width = gain_ref.shape[1]
    a = normed(x_ref[:, :width].astype(F32), gain_ref[...]).astype(BF16)
    k = nn(a, wk_ref[...]).astype(BF16)
    k_ref[...] = k
    v_ref[...] = nn(a, wv_ref[...]).astype(BF16)
    put_norms(k_norm_ref, k)
    tags = x_ref[:, width:]
    dec_ref[...], enc_ref[...] = tag_lanes(tags, 0), tag_lanes(tags, 2)


def encoder_project_kernel(x_ref, wk_ref, wv_ref, *refs):
    k_ref, v_ref, k_norm_ref = refs[-3:]
    k = nn(x_ref[...], wk_ref[...]).astype(BF16)
    k_ref[...] = k
    put_norms(k_norm_ref, k)
    v_ref[...] = nn(x_ref[...], wv_ref[...]).astype(BF16)


def own_project(x, gain, wq, wk, wv, keys):
    rows, width = x.shape[0], gain.shape[1]
    tile = min(TILE, rows)
    spec, lanes = row_spec(tile, width), row_spec(tile, LANES)
    return run(
        own_project_kernel,
        "own_project",
        (rows // tile,),
        [(x, row_spec(tile, x.shape[1]), None), (gain, None), (wq, None), (wk, None), (wv, None)],
        [((n, width), BF16, spec) for n in (rows, rows, keys, keys)]
        + [((n, LANES), BF16, lanes) for n in (keys, keys, rows)]
        + [((1, LANES), F32, None)] * 2,
        flops=6 * rows * width * width,
    )


def other_project(x, gain, wk, wv, *so_far):
    rows, width = x.shape[0], gain.shape[1]
    tile = min(TILE, rows)
    shift = (so_far[0].shape[0] - rows) // tile
    spec, lanes = row_spec(tile, width, shift), row_spec(tile, LANES, shift)
    return run(
        other_project_kernel,
        "other_project",
        (rows // tile,),
        [(x, row_spec(tile, x.shape[1]), None), (gain, None), (wk, None), (wv, None)] + [(v, ANY) for v in so_far],
        [(v.shape, BF16, s) for v, s in zip(so_far, (spec, spec, lanes, lanes))] + [((1, LANES), F32, None)],
        aliases={4: 0, 5: 1, 6: 2, 7: 3},
        flops=4 * rows * width * width,
    )


def encoder_project(x, wk, wv, keys, so_far=()):
    rows, width = x.shape
    tile = min(TILE, rows)
    spec = row_spec(tile, width, (keys - rows) // tile if so_far else 0)
    return run(
        encoder_project_kernel,
        "encoder_project",
        (rows // tile,),
        [(x, row_spec(tile, width), None), (wk, None), (wv, None)] + [(v, ANY) for v in so_far],
        [((keys, width), BF16, spec)] * 2 + [((1, LANES), F32, None)],
        aliases={3: 0, 4: 1} if so_far else None,
        flops=4 * rows * width * width,
    )


def self_finish(mixed_ref, hidden_ref, w_out_ref, gain_ref, w_next_ref, hidden_out, norm_out, next_out, next_norm):
    rows = hidden_ref.shape[0]
    tile = min(TILE, rows)
    for at in range(0, rows, tile):
        o = jnp.concatenate([mixed_ref[p, at : at + tile, :] for p in range(PAIRS)], axis=1)
        hidden = hidden_ref[at : at + tile, :].astype(F32) + nn(o, w_out_ref[...])
        hidden_out[at : at + tile, :] = hidden
        b = normed(hidden, gain_ref[...]).astype(BF16)
        norm_out[at : at + tile, :] = b
        if w_next_ref is not None:
            following = (nn(b, w_next_ref[...]) * LOG2E).astype(BF16)
            next_out[at : at + tile, :] = following
            norms = head_norms(following)
            next_norm[...] = norms if at == 0 else jnp.maximum(next_norm[...], norms)


def ffn_kernel(mine_ref, c_ref, og_ref, wi_ref, wo_ref, h2_ref, gain_ref, wco_ref, *refs):
    layer_ref, dh2_ref, dyc_ref, doc_ref, dgain_ref, *grad_refs, y_sum, dc_sum, total_ref, turned_ref = refs
    step, steps = pl.program_id(0), pl.num_programs(0)
    mine = mine_ref[0]
    c, og, wi, wo = c_ref[...], og_ref[...], wi_ref[...], wo_ref[...]

    @pl.when(step == 0)
    def _():
        turned_ref[...] = c.T

    u = nn(c, wi)
    slope = math.sqrt(2.0 / math.pi)
    square = u * u
    bend = jnp.tanh(u * (slope + (slope * 0.044715) * square))
    half = 0.5 + 0.5 * bend
    wide = u * half
    g = wide.astype(BF16)
    rate = half + wide * ((1.0 - bend) * (slope + (slope * 3.0 * 0.044715) * square))
    y = nn(g, wo)
    du = (nt(og, wo) * rate).astype(BF16)
    dc = nt(du, wi)

    @pl.when(step == 0)
    def _():
        y_sum[...] = y
        dc_sum[...] = dc

    @pl.when(step > 0)
    def _():
        y_sum[...] += y
        dc_sum[...] += dc

    out_total, in_total = tn(g, og), nn(turned_ref[...], du)
    if len(grad_refs) == 4:
        total_ref[...] = out_total
        emit(mine, total_ref, grad_refs[0], grad_refs[1], 0, grad_refs[0].shape[2])
        total_ref[...] = in_total
        rows = grad_refs[2].shape[2] * grad_refs[2].shape[3] // total_ref.shape[1]
        emit(mine, total_ref, grad_refs[2], grad_refs[3], 0, rows)
    else:
        grad_refs[0][...] = out_total.astype(BF16)
        grad_refs[1][...] = in_total.astype(BF16)

    @pl.when(step == steps - 1)
    def _():
        rows = h2_ref.shape[0]
        tile = min(TILE, rows)
        dgain = jnp.zeros(dgain_ref.shape, F32)
        for at in range(0, rows, tile):
            part = slice(at, at + tile)
            hidden = h2_ref[part, :]
            layer_ref[part, :] = (hidden + y_sum[part, :]).astype(BF16)
            back, gain_part = norm_back(hidden, gain_ref[...], dc_sum[part, :])
            dgain = dgain + gain_part
            dh2 = og_ref[part, :].astype(F32) + back
            dh2_ref[part, :] = dh2
            dyc = dh2.astype(BF16)
            dyc_ref[part, :] = dyc
            doc_ref[part, :] = nt(dyc, wco_ref[...]).astype(BF16)
        dgain_ref[...] = dgain


def feed_forward(mine, c, og, wi, wo, h2, gain, wco, after=()):
    rows, width = c.shape
    hidden = wi.shape[1]
    dp_size, mem_size = lax.axis_size("dp"), lax.axis_size("mem")
    chunk = width
    steps = hidden // chunk
    direct = fits(width, width) and steps == 2 * mem_size and (chunk * dp_size) % (2 * hidden) == 0
    if direct:
        pairs, rows_o, cols_o = dp_size // 2, hidden // dp_size, width // mem_size
        chunk_rows = width // dp_size * (chunk // cols_o)
        grads = [
            (
                (mem_size, pairs, rows_o, cols_o),
                BF16,
                pl.BlockSpec((mem_size, pairs // steps, rows_o, cols_o), lambda f, *_: (0, f, 0, 0)),
            )
        ] * 2 + [
            (
                (mem_size, pairs, rows_o, cols_o),
                BF16,
                pl.BlockSpec((1, pairs, chunk_rows, cols_o), lambda f, *_: (f // 2, 0, f % 2, 0)),
            )
        ] * 2
    else:
        grads = [
            ((hidden, width), BF16, pl.BlockSpec((chunk, width), lambda f, *_: (f, 0))),
            ((width, hidden), BF16, pl.BlockSpec((width, chunk), lambda f, *_: (0, f))),
        ]
    outs = run(
        ffn_kernel,
        "feed_forward",
        (steps,),
        [
            (c, None),
            (og, None),
            (wi, pl.BlockSpec((width, chunk), lambda f, *_: (0, f))),
            (wo, pl.BlockSpec((chunk, width), lambda f, *_: (f, 0))),
            (h2, None),
            (gain, None),
            (wco, None),
        ],
        [
            (c.shape, BF16, None),
            (c.shape, F32, None),
            (c.shape, BF16, None),
            (c.shape, BF16, None),
            (gain.shape, F32, None),
        ]
        + grads,
        scratch=[
            pltpu.VMEM(c.shape, F32),
            pltpu.VMEM(c.shape, F32),
            pltpu.VMEM((chunk, width), F32),
            pltpu.VMEM((width, rows), BF16),
        ],
        scalars=(mine,),
        after=after,
        flops=12 * rows * width * hidden,
    )
    grads = outs[5:]
    return outs[:5], [grads[0:2], grads[2:4]] if direct else [grads[0:1], grads[1:2]]


def cross_finish_kernel(
    mine_ref, dq0_ref, dq1_ref, wq_ref, h1_ref, gain_ref, dh2_ref, o_ref, oc_ref, dyc_ref, b_ref, wso_ref, *refs
):
    dh1_ref, do_ref, dgain_ref, *grad_refs, dy_ref, total_ref = refs
    mine = mine_ref[0]
    dq = jnp.concatenate([dq0_ref[...], dq1_ref[...]], axis=1)
    rows = h1_ref.shape[0]
    tile = min(TILE, rows)
    write_square(mine, 0, tn(oc_ref[...], dyc_ref[...]), total_ref, grad_refs)
    write_square(mine, 1, tn(b_ref[...], dq), total_ref, grad_refs)
    dgain = jnp.zeros(dgain_ref.shape, F32)
    for at in range(0, rows, tile):
        part = slice(at, at + tile)
        db = nt(dq[part, :], wq_ref[...])
        back, gain_part = norm_back(h1_ref[part, :], gain_ref[...], db)
        dgain = dgain + gain_part
        dh1 = dh2_ref[part, :] + back
        dh1_ref[part, :] = dh1
        dy = dh1.astype(BF16)
        dy_ref[part, :] = dy
        do_ref[part, :] = nt(dy, wso_ref[...]).astype(BF16)
    dgain_ref[...] = dgain
    write_square(mine, 2, tn(o_ref[...], dy_ref[...]), total_ref, grad_refs)


def cross_finish(mine, dq, wq, h1, gain, dh2, o, oc, dyc, b, wso, after=()):
    rows, width = h1.shape
    outs = run(
        cross_finish_kernel,
        "cross_finish",
        (1,),
        [(v, None) for v in (*dq, wq, h1, gain, dh2, o, oc, dyc, b, wso)],
        [(h1.shape, F32, None, pltpu.HBM), (h1.shape, BF16, None), (gain.shape, F32, None)] + square_outs(3, width),
        scratch=[pltpu.VMEM(h1.shape, BF16), pltpu.VMEM((width, width), F32)],
        scalars=(mine,),
        after=after,
        flops=10 * rows * width * width,
    )
    return outs[:3], outs[3:]


def summed(own_refs, came_refs, index):
    return jnp.concatenate(
        [
            (own[index].astype(F32) + came[index].astype(F32)).astype(BF16)
            for own, came in zip(own_refs, came_refs)
        ],
        axis=1,
    )


def encoder_finish_kernel(mine_ref, own0_ref, own1_ref, came0_ref, came1_ref, x_ref, wk_ref, wv_ref, *refs):
    dx_ref, *grad_refs, total_ref = refs
    mine = mine_ref[0]
    dk = summed((own0_ref, own1_ref), (came0_ref, came1_ref), 0)
    dv = summed((own0_ref, own1_ref), (came0_ref, came1_ref), 1)
    x = x_ref[...]
    dx_ref[...] = (nt(dk, wk_ref[...]) + nt(dv, wv_ref[...])).astype(BF16)
    write_square(mine, 0, tn(x, dk), total_ref, grad_refs)
    write_square(mine, 1, tn(x, dv), total_ref, grad_refs)


def encoder_finish(mine, own, came, x, wk, wv, after=()):
    rows, width = x.shape
    outs = run(
        encoder_finish_kernel,
        "encoder_finish",
        (1,),
        [(v, None) for v in (*own, *came, x, wk, wv)],
        [(x.shape, BF16, None)] + square_outs(2, width),
        scratch=[pltpu.VMEM((width, width), F32)],
        scalars=(mine,),
        after=after,
        flops=8 * rows * width * width,
    )
    return outs[0], outs[1:]


def query_grad_kernel(mine_ref, dq0_ref, dq1_ref, a_ref, *refs):
    *grad_refs, total_ref = refs
    dq = jnp.concatenate([dq0_ref[...], dq1_ref[...]], axis=1)
    write_square(mine_ref[0], 0, tn(a_ref[...], dq), total_ref, grad_refs)


def query_grad(mine, dq, a):
    rows, width = a.shape
    return run(
        query_grad_kernel,
        "query_grad",
        (1,),
        [(v, None) for v in (*dq, a)],
        square_outs(1, width),
        scratch=[pltpu.VMEM((width, width), F32)],
        scalars=(mine,),
        flops=2 * rows * width * width,
    )


def key_grads_kernel(mine_ref, own0_ref, own1_ref, came0_ref, came1_ref, a_ref, *refs):
    sums_ref, *grad_refs, total_ref = refs
    a = a_ref[...]
    for i in range(2):
        total = summed((own0_ref, own1_ref), (came0_ref, came1_ref), i)
        sums_ref[i] = total
        write_square(mine_ref[0], i, tn(a, total), total_ref, grad_refs)


def key_grads(mine, own, came, a, after=()):
    rows, width = a.shape
    outs = run(
        key_grads_kernel,
        "key_grads",
        (1,),
        [(v, None) for v in (*own, *came, a)],
        [((2, rows, width), BF16, None)] + square_outs(2, width),
        scratch=[pltpu.VMEM((width, width), F32)],
        scalars=(mine,),
        after=after,
        flops=4 * rows * width * width,
    )
    return outs[0], outs[1:]


def self_finish_back_kernel(
    dq0_ref, dq1_ref, sums_ref, x_ref, gain_ref, dh1_ref, wq_ref, wk_ref, wv_ref, small_ref, dx_ref, small_out
):
    @pl.when(pl.program_id(0) == 0)
    def _():
        small_out[...] = small_ref[...]

    dq = jnp.concatenate([dq0_ref[...], dq1_ref[...]], axis=1)
    da = nt(dq, wq_ref[...]) + nt(sums_ref[0], wk_ref[...]) + nt(sums_ref[1], wv_ref[...])
    back, gain_part = norm_back(x_ref[...].astype(F32), gain_ref[...], da)
    small_out[0:1, :] += gain_part
    dx_ref[...] = (dh1_ref[...] + back).astype(BF16)


def self_finish_back(dq, sums, x, gain, dh1, wq, wk, wv, small):
    rows, width = dh1.shape
    tile = min(TILE, rows)
    spec = row_spec(tile, width)
    return run(
        self_finish_back_kernel,
        "self_finish_back",
        (rows // tile,),
        [
            (dq[0], row_spec(tile, dq[0].shape[1])),
            (dq[1], row_spec(tile, dq[1].shape[1])),
            (sums, pl.BlockSpec((2, tile, width), lambda i, *_: (0, i, 0)), None),
            (x, spec),
            (gain, None),
            (dh1, spec),
            (wq, None),
            (wk, None),
            (wv, None),
            (small, None),
        ],
        [((rows, width), BF16, spec), (small.shape, F32, None)],
        flops=6 * rows * width * width,
    )


SCORE_BOUND = 80.0


def mark_small(small_ref, q_norm_ref, *k_norm_refs):
    @pl.when(pl.program_id(0) == 0)
    def _():
        k_norm = k_norm_refs[0][...]
        for ref in k_norm_refs[1:]:
            k_norm = jnp.maximum(k_norm, ref[...])
        largest = jnp.max(q_norm_ref[...] * k_norm)
        small_ref[0] = (largest <= 0.95 * SCORE_BOUND**2).astype(jnp.int32)


def self_scores(i, head, blocks, q_ref, k_ref, table_ref, q_lanes_ref, k_lanes_ref):
    piece = q_ref.shape[0] // 2
    mem_size = k_ref.shape[0] // q_ref.shape[0]
    q_at = pl.multiple_of(blocks[0, i], piece)
    k_at = pl.multiple_of(blocks[1, i], piece)
    q = half_of(q_ref[pl.ds(q_at, piece), :], head)
    q = jnp.concatenate([q, q_lanes_ref[pl.ds(q_at, piece), :]], axis=1)
    k = jnp.concatenate([k_ref[pl.ds(k_at, piece), :], k_lanes_ref[pl.ds(k_at, piece), :]], axis=1)
    return with_bias(nt(q, k), table_ref, head, 2 * mem_size - i if i >= mem_size else blocks[2, i])


def add_mixed(sums, i, mixed, low, mem_size):
    if i == 0:
        sums[0] = mixed
    elif i < mem_size:
        part = jnp.where(low, mixed, 0.0)
        sums[0] = sums[0] + part
        sums[1] = mixed - part if sums[1] is None else sums[1] + (mixed - part)
    else:
        sums[1] = mixed if sums[1] is None else sums[1] + mixed


def self_forward_kernel(
    blocks,
    q_ref,
    k_ref,
    v_ref,
    table_ref,
    q_lanes_ref,
    k_lanes_ref,
    hidden_ref,
    w_out_ref,
    gain_ref,
    w_next_ref,
    q_norm_ref,
    k_norm0_ref,
    k_norm1_ref,
    o_ref,
    back_lanes_ref,
    hidden_out,
    norm_out,
    next_out,
    next_norm,
    s_ref,
    mixed_ref,
    small_ref,
):
    rows = q_ref.shape[0]
    piece = rows // 2
    mem_size = k_ref.shape[0] // rows
    count = 2 * mem_size + 1
    ones = jnp.ones((piece, LANES), BF16)
    scores = functools.partial(
        self_scores,
        blocks=blocks,
        q_ref=q_ref,
        k_ref=k_ref,
        table_ref=table_ref,
        q_lanes_ref=q_lanes_ref,
        k_lanes_ref=k_lanes_ref,
    )
    mark_small(small_ref, q_norm_ref, k_norm0_ref, k_norm1_ref)

    def mix(i, p):
        k_at = pl.multiple_of(blocks[1, i], piece)
        return nn(p.astype(BF16), jnp.concatenate([v_ref[pl.ds(k_at, piece), :], ones], axis=1))

    def put(outs):
        for i in range(2):
            mixed = join_halves(outs[0][i], outs[1][i]).astype(BF16)
            o_ref[i * piece : (i + 1) * piece, :] = mixed
            mixed_ref[pl.program_id(0), i * piece : (i + 1) * piece, :] = mixed

    def close(head, sums, tops):
        mixed = []
        for at, total, top in ((0, sums[0], tops[0]), (piece, sums[1], tops[1])):
            weight = total[:, LANES:]
            mixed.append(total[:, :LANES] / weight)
            log_sum = jnp.log2(weight) if top is None else top + jnp.log2(weight)
            back_lanes_ref[head, at : at + piece, :] = with_log_sum(q_lanes_ref[at : at + piece, :], log_sum)
        return mixed

    @pl.when(small_ref[0] == 1)
    def _():
        outs = []
        for head in range(2):
            sums = [None, None]
            for i in range(count):
                add_mixed(sums, i, mix(i, jnp.exp2(scores(i, head))), blocks[3, i] == 1, mem_size)
            outs.append(close(head, sums, (None, None)))
        put(outs)

    @pl.when(small_ref[0] == 0)
    def _():
        outs = []
        for head in range(2):
            tops = []
            for i in range(count):
                s = scores(i, head)
                s_ref[i] = s
                tops.append(jnp.max(s, axis=1, keepdims=True))
            top_low, top_high = tops[0], tops[mem_size]
            for i in range(mem_size + 1, count):
                top_high = jnp.maximum(top_high, tops[i])
            for i in range(1, mem_size):
                low = blocks[3, i] == 1
                top_low = jnp.maximum(top_low, jnp.where(low, tops[i], NEGATIVE))
                top_high = jnp.maximum(top_high, jnp.where(low, NEGATIVE, tops[i]))
            sums = [None, None]
            for i in range(count):
                low = blocks[3, i] == 1
                top = top_low if i == 0 else top_high if i >= mem_size else jnp.where(low, top_low, top_high)
                add_mixed(sums, i, mix(i, jnp.exp2(s_ref[i] - top)), low, mem_size)
            outs.append(close(head, sums, (top_low, top_high)))
        put(outs)

    @pl.when(pl.program_id(0) == PAIRS - 1)
    def _():
        self_finish(
            mixed_ref, hidden_ref, w_out_ref, gain_ref, w_next_ref, hidden_out, norm_out, next_out, next_norm
        )


def pair_spec(rows):
    return pl.BlockSpec((rows, LANES), lambda p, *_: (0, p))


def whole_spec(rows):
    return pl.BlockSpec((rows, LANES), lambda p, *_: (0, 0))


def lanes_spec(rows):
    return pl.BlockSpec((2, rows, LANES), lambda p, *_: (p, 0, 0))


def cross_forward_kernel(
    q_ref,
    k_ref,
    v_ref,
    q_lanes_ref,
    k_lanes_ref,
    hidden_ref,
    w_out_ref,
    gain_ref,
    q_norm_ref,
    k_norm0_ref,
    k_norm1_ref,
    o_ref,
    back_lanes_ref,
    hidden_out,
    norm_out,
    mixed_ref,
    small_ref,
):
    rows, keys = q_ref.shape[0], k_ref.shape[0]
    tile, key_tile = min(256, rows), min(256, keys)
    mark_small(small_ref, q_norm_ref, k_norm0_ref, k_norm1_ref)

    def put(part, outs):
        mixed = join_halves(outs[0], outs[1]).astype(BF16)
        o_ref[part, :] = mixed
        mixed_ref[pl.program_id(0), part, :] = mixed

    @pl.when(small_ref[0] == 1)
    def _():
        ones = jnp.ones((key_tile, LANES), BF16)
        outs = []
        for head in range(2):
            q = jnp.concatenate([half_of(q_ref[...], head), q_lanes_ref[...]], axis=1)
            total = None
            for at in range(0, keys, key_tile):
                part = slice(at, at + key_tile)
                k = jnp.concatenate([k_ref[part, :], k_lanes_ref[part, :]], axis=1)
                v = jnp.concatenate([v_ref[part, :], ones], axis=1)
                mixed = nn(jnp.exp2(nt(q, k)).astype(BF16), v)
                total = mixed if total is None else total + mixed
            weight = total[:, LANES:]
            outs.append(total[:, :LANES] / weight)
            back_lanes_ref[head] = with_log_sum(q_lanes_ref[...], jnp.log2(weight))
        put(slice(0, rows), outs)

    @pl.when(small_ref[0] == 0)
    def _():
        k = jnp.concatenate([k_ref[...], k_lanes_ref[...]], axis=1)
        v = jnp.concatenate([v_ref[...], jnp.ones((keys, LANES), BF16)], axis=1)
        for at in range(0, rows, tile):
            part = slice(at, at + tile)
            outs = []
            for head in range(2):
                q = jnp.concatenate([half_of(q_ref[part, :], head), q_lanes_ref[part, :]], axis=1)
                s = nt(q, k)
                top = jnp.max(s, axis=1, keepdims=True)
                total = nn(jnp.exp2(s - top).astype(BF16), v)
                weight = total[:, LANES:]
                outs.append(total[:, :LANES] / weight)
                back_lanes_ref[head, part, :] = with_log_sum(q_lanes_ref[part, :], top + jnp.log2(weight))
            put(part, outs)

    @pl.when(pl.program_id(0) == PAIRS - 1)
    def _():
        self_finish(mixed_ref, hidden_ref, w_out_ref, gain_ref, None, hidden_out, norm_out, None, None)


def grad_lanes(o, do):
    inner = jnp.sum(o.astype(F32) * do.astype(F32), axis=1, keepdims=True)
    pieces = [piece.astype(F32) for piece in in_three(-inner)]
    return put_lanes(jnp.zeros(do.shape, F32), 0, pieces).astype(BF16)


def put_parts(at, dk, dv, own_ref, other_ref):
    rows = own_ref.shape[1]
    ref, start = (own_ref, at) if at < rows else (other_ref, at - rows)
    ref[0, start : start + dk.shape[0], :] = (dk * LN2).astype(BF16)
    ref[1, start : start + dv.shape[0], :] = dv.astype(BF16)


def cross_backward_kernel(
    q_ref, k_ref, v_ref, o_ref, do_ref, back_lanes_ref, k_lanes_ref, dq_ref, own_ref, other_ref
):
    rows, keys = q_ref.shape[0], k_ref.shape[0]
    tile = min(256, rows)
    k_turned = k_ref[...].T
    k_wide = jnp.concatenate([k_ref[...], k_lanes_ref[...]], axis=1)
    v_wide = jnp.concatenate([v_ref[...], jnp.ones((keys, LANES), BF16)], axis=1)
    dk = dv = None
    for at in range(0, rows, tile):
        part = slice(at, at + tile)
        dqs = []
        for head in range(2):
            q, do = half_of(q_ref[part, :], head), half_of(do_ref[part, :], head)
            q_wide = jnp.concatenate([q, back_lanes_ref[head, part, :]], axis=1)
            do_wide = jnp.concatenate([do, grad_lanes(o_ref[part, :], do)], axis=1)
            p = jnp.exp2(nt(k_wide, q_wide))
            ds = (p * nt(v_wide, do_wide)).astype(BF16)
            dv_part, dk_part = nn(p.astype(BF16), do), nn(ds, q)
            dv = dv_part if dv is None else dv + dv_part
            dk = dk_part if dk is None else dk + dk_part
            dqs.append(nn(k_turned[head * HEAD_DIM : (head + 1) * HEAD_DIM, :], ds))
        dq_ref[part, :] = jnp.concatenate(dqs, axis=0).T.astype(BF16)
    for at, size in ((0, rows), (rows, keys - rows)):
        put_parts(at, dk[at : at + size], dv[at : at + size], own_ref, other_ref)


def self_backward_kernel(
    blocks,
    q_ref,
    k_ref,
    v_ref,
    o_ref,
    do_ref,
    back_lanes_ref,
    k_lanes_ref,
    table_ref,
    dq_ref,
    own_ref,
    other_ref,
    grad_ref,
    do_lanes_ref,
    dq_sum,
    dk_sum,
    dv_sum,
):
    rows = q_ref.shape[0]
    piece = rows // 2
    mem_size = k_ref.shape[0] // rows
    count = 2 * mem_size + 1
    ones = jnp.ones((piece, LANES), BF16)
    for head in range(2):
        do_lanes_ref[head] = grad_lanes(o_ref[...], half_of(do_ref[...], head))
    dq_sum[...] = jnp.zeros_like(dq_sum)
    dk_sum[...] = jnp.zeros_like(dk_sum)
    dv_sum[...] = jnp.zeros_like(dv_sum)
    grad_ref[...] = jnp.zeros_like(grad_ref)
    for i in reversed(range(count)):
        q_at = pl.multiple_of(blocks[0, i], piece)
        k_at = pl.multiple_of(blocks[1, i], piece)
        k, v = k_ref[pl.ds(k_at, piece), :], v_ref[pl.ds(k_at, piece), :]
        k_turned = k.T
        k_wide = jnp.concatenate([k, k_lanes_ref[pl.ds(k_at, piece), :]], axis=1)
        v_wide = jnp.concatenate([v, ones], axis=1)
        dk = dv = None
        dqs = []
        for head in range(2):
            q = half_of(q_ref[pl.ds(q_at, piece), :], head)
            do = half_of(do_ref[pl.ds(q_at, piece), :], head)
            q_wide = jnp.concatenate([q, back_lanes_ref[head, pl.ds(q_at, piece), :]], axis=1)
            do_wide = jnp.concatenate([do, do_lanes_ref[head, pl.ds(q_at, piece), :]], axis=1)
            s = nt(k_wide, q_wide)
            kind = 2 * mem_size - i if i >= mem_size else blocks[2, i]
            p = jnp.exp2(with_bias(s, table_ref, head, kind, turned=True))
            ds = p * nt(v_wide, do_wide)
            add_grad(ds, grad_ref, head, kind)
            ds = ds.astype(BF16)
            dv_part, dk_part = nn(p.astype(BF16), do), nn(ds, q)
            dv = dv_part if dv is None else dv + dv_part
            dk = dk_part if dk is None else dk + dk_part
            dqs.append(nn(k_turned[head * HEAD_DIM : (head + 1) * HEAD_DIM, :], ds))
        which = 1 - blocks[3, i]
        dq_sum[which] = dq_sum[which] + jnp.concatenate(dqs, axis=0)
        dk_sum[pl.ds(k_at, piece), :] = dk_sum[pl.ds(k_at, piece), :] + dk
        dv_sum[pl.ds(k_at, piece), :] = dv_sum[pl.ds(k_at, piece), :] + dv
    for i in range(2):
        dq_ref[i * piece : (i + 1) * piece, :] = dq_sum[i].T.astype(BF16)
    for at in (0, rows):
        size = rows if at == 0 else k_ref.shape[0] - rows
        put_parts(at, dk_sum[at : at + size, :], dv_sum[at : at + size, :], own_ref, other_ref)


def table_spec(table):
    return pl.BlockSpec((2,) + table.shape[1:], lambda p, *_: (p, 0, 0, 0))


def attention_flops(scores, matmuls):
    return 2 * HEADS * scores * 256 * matmuls


def self_forward(blocks, q, k, v, table, q_lanes, k_lanes, hidden, w_out, gain, w_next, norms, after=()):
    rows, keys = q.shape[0], k.shape[0]
    piece = rows // 2
    return run(
        self_forward_kernel,
        "self_forward",
        (PAIRS,),
        [
            (q, pair_spec(rows)),
            (k, pair_spec(keys)),
            (v, pair_spec(keys)),
            (table, table_spec(table)),
            (q_lanes, None),
            (k_lanes, None, pltpu.HBM),
            (hidden, pl.BlockSpec((rows, gain.shape[1]), lambda *_: (0, 0))),
            (w_out, None),
            (gain, None),
            (w_next, None),
        ]
        + [(norm, None) for norm in norms],
        [
            (q.shape, BF16, pair_spec(rows)),
            ((HEADS, rows, LANES), BF16, lanes_spec(rows)),
            (q.shape, F32, None),
            (q.shape, BF16, None),
            (q.shape, BF16, None),
            ((1, LANES), F32, None),
        ],
        scratch=[
            pltpu.VMEM((blocks.shape[1], piece, piece), F32),
            pltpu.VMEM((PAIRS, rows, LANES), BF16),
            pltpu.SMEM((1,), jnp.int32),
        ],
        scalars=(blocks,),
        after=after,
        flops=attention_flops(blocks.shape[1] * piece * piece, 2),
    )


def cross_forward(q, k, v, q_lanes, k_lanes, hidden, w_out, gain, norms, after=()):
    rows, keys = q.shape[0], k.shape[0]
    return run(
        cross_forward_kernel,
        "cross_forward",
        (PAIRS,),
        [
            (q, pair_spec(rows)),
            (k, pair_spec(keys)),
            (v, pair_spec(keys)),
            (q_lanes, None),
            (k_lanes, None, pltpu.HBM),
            (hidden, None),
            (w_out, None),
            (gain, None),
        ]
        + [(norm, None) for norm in norms],
        [
            (q.shape, BF16, pair_spec(rows)),
            ((HEADS, rows, LANES), BF16, lanes_spec(rows)),
            (q.shape, F32, None),
            (q.shape, BF16, None),
        ],
        scratch=[pltpu.VMEM((PAIRS, rows, LANES), BF16), pltpu.SMEM((1,), jnp.int32)],
        after=after,
        flops=attention_flops(rows * keys, 2),
    )


def half_spec(rows, start):
    return pl.BlockSpec((rows, LANES), lambda p, *_: (0, p + start))


def cross_backward(q, k, v, o, do, back_lanes, k_lanes, start, count, after=()):
    rows, keys = q.shape[0], k.shape[0]
    width = count * LANES
    parts = pl.BlockSpec((2, rows, LANES), lambda p, *_: (0, 0, p))
    others_spec = pl.BlockSpec((2, keys - rows, LANES), lambda p, *_: (0, 0, p))
    return run(
        cross_backward_kernel,
        "cross_backward",
        (count,),
        [
            (q, half_spec(rows, start)),
            (k, half_spec(keys, start)),
            (v, half_spec(keys, start)),
            (o, half_spec(rows, start)),
            (do, half_spec(rows, start), None),
            (back_lanes, pl.BlockSpec((2, rows, LANES), lambda p, *_: (p + start, 0, 0))),
            (k_lanes, None, pltpu.HBM),
        ],
        [
            ((rows, width), BF16, pair_spec(rows)),
            ((2, rows, width), BF16, parts),
            ((2, keys - rows, width), BF16, others_spec),
        ],
        after=after,
        flops=attention_flops(rows * keys, 5) * count // PAIRS,
    )


def self_backward(blocks, q, k, v, o, do, back_lanes, k_lanes, table_t, start, count, after=()):
    rows, keys = q.shape[0], k.shape[0]
    piece = rows // 2
    width = count * LANES
    parts = pl.BlockSpec((2, rows, LANES), lambda p, *_: (0, 0, p))
    others_spec = pl.BlockSpec((2, keys - rows, LANES), lambda p, *_: (0, 0, p))
    return run(
        self_backward_kernel,
        "self_backward",
        (count,),
        [
            (q, half_spec(rows, start)),
            (k, half_spec(keys, start)),
            (v, half_spec(keys, start)),
            (o, half_spec(rows, start)),
            (do, half_spec(rows, start), None),
            (back_lanes, pl.BlockSpec((2, rows, LANES), lambda p, *_: (p + start, 0, 0))),
            (k_lanes, None, pltpu.HBM),
            (table_t, pl.BlockSpec((2,) + table_t.shape[1:], lambda p, *_: (p + start, 0, 0, 0))),
        ],
        [
            ((rows, width), BF16, pair_spec(rows)),
            ((2, rows, width), BF16, parts),
            ((2, keys - rows, width), BF16, others_spec),
            ((2 * count,) + table_t.shape[1:], F32, table_spec(table_t)),
        ],
        scratch=[
            pltpu.VMEM((2, rows, LANES), BF16),
            pltpu.VMEM((2, LANES, piece), F32),
            pltpu.VMEM((keys, LANES), F32),
            pltpu.VMEM((keys, LANES), F32),
        ],
        scalars=(blocks,),
        after=after,
        flops=attention_flops(blocks.shape[1] * piece * piece, 5) * count // PAIRS,
    )


def on_device(
    decoder_in,
    encoder_out,
    dec_segments,
    dec_mask,
    enc_segments,
    enc_mask,
    self_gain,
    cross_gain,
    ffn_gain,
    rel_bias,
    self_query,
    self_key,
    self_value,
    self_out,
    cross_query,
    cross_key,
    cross_value,
    cross_out,
    ffn_in,
    ffn_out,
    out_grad,
):
    mem_size = lax.axis_size("mem")
    rows, width = decoder_in.shape[1:]
    keys = rows * mem_size
    dp_index = lax.axis_index("dp")
    mine = (dp_index % 2).astype(jnp.int32)[None]
    group = group_of(dp_index, lax.axis_index("mem"), mem_size)
    odd = group % 2 == 1
    blocks = block_list(group, mem_size, rows)
    bits = bit_values()
    gain_self, gain_cross, gain_ffn = (g[None, :] for g in (self_gain, cross_gain, ffn_gain))
    first, rest = PAIRS // 2, PAIRS - PAIRS // 2

    lane = jnp.arange(LANES, dtype=jnp.int32)[None, :]
    tags = jnp.zeros((rows, LANES), jnp.int32)
    for i, tag in enumerate((dec_segments, dec_mask, enc_segments, enc_mask)):
        tags = jnp.where(lane == i, tag[0][:, None], tags)
    pieces = to_rows(jnp.concatenate([decoder_in[0], tags.astype(BF16)], axis=1))
    table, table_t = bias_tables(rel_bias, small_block(rows // 2))
    pair_in = jnp.stack([encoder_out[0], out_grad[0]])
    pieces, table, table_t, pair_in = fence([], pieces, table, table_t, pair_in)
    hidden_own = arranged(pieces, odd)

    hidden_others = jnp.concatenate(others(hidden_own))
    pair_pieces = to_rows(pair_in, axis=1)
    self_in, query_rows, *so_far, q_lanes, q_norm, k_norm0 = own_project(
        hidden_own, gain_self, self_query, self_key, self_value, keys
    )
    hidden_others, so_far = fence([], hidden_others, so_far)
    key_all, value_all, dec_lanes, enc_lanes, k_norm1 = other_project(hidden_others, gain_self, self_key, self_value, *so_far)
    self_mixed, self_lanes, hidden_one, cross_in, cross_rows, cross_norm = self_forward(
        blocks,
        query_rows,
        key_all,
        value_all,
        table,
        q_lanes,
        dec_lanes,
        hidden_own,
        self_out,
        gain_cross,
        cross_query,
        (q_norm, k_norm0, k_norm1),
    )
    pair_pieces, cross_rows = fence([], pair_pieces, cross_rows)

    encoder_own, cotangent = arranged(pair_pieces, odd, axis=1)
    encoder_others = jnp.concatenate(others(encoder_own))
    *so_far, k_norm0 = encoder_project(encoder_own, cross_key, cross_value, keys)
    encoder_others, so_far = fence([], encoder_others, so_far)

    cross_key_all, cross_value_all, k_norm1 = encoder_project(encoder_others, cross_key, cross_value, keys, so_far)
    cross_mixed, cross_lanes, hidden_two, ffn_input = cross_forward(
        cross_rows,
        cross_key_all,
        cross_value_all,
        q_lanes,
        enc_lanes,
        hidden_one,
        cross_out,
        gain_ffn,
        (cross_norm, k_norm0, k_norm1),
    )
    (layer_out, hidden_two_grad, cross_branch_grad, cross_mixed_grad, ffn_gain_grad), ffn_grads = feed_forward(
        mine, ffn_input, cotangent, ffn_in, ffn_out, hidden_two, gain_ffn, cross_out
    )

    ffn_a, ffn_b = Scatter(ffn_grads[0], "xyz"), Scatter(ffn_grads[1], "yxz", ffn_in.shape[1] // width)
    layer_out = from_rows(layer_out, odd)

    def cross_half(start, count, do):
        return cross_backward(
            cross_rows, cross_key_all, cross_value_all, cross_mixed, do, cross_lanes, enc_lanes, start, count
        )

    cross_q0, cross_own0, cross_other0 = cross_half(0, first, cross_mixed_grad)
    layer_out, cross_q0, cross_own0, cross_other0, cross_mixed_grad = fence(
        [ffn_a, ffn_b], layer_out, cross_q0, cross_own0, cross_other0, cross_mixed_grad
    )

    advance(bits, ffn_a, ffn_b)
    came0 = came_parts(cross_other0, rows)
    cross_q1, cross_own1, cross_other1 = cross_half(first, rest, cross_mixed_grad)
    came0, cross_q1, cross_own1, cross_other1 = fence([], came0, cross_q1, cross_own1, cross_other1)

    came1 = came_parts(cross_other1, rows)
    (hidden_one_grad, self_mixed_grad, cross_gain_grad), grads = cross_finish(
        mine,
        (cross_q0, cross_q1),
        cross_query,
        hidden_one,
        gain_cross,
        hidden_two_grad,
        self_mixed,
        cross_mixed,
        cross_branch_grad,
        cross_in,
        self_out,
    )
    came1, hidden_one_grad, self_mixed_grad, grads = fence(
        [ffn_a, ffn_b], came1, hidden_one_grad, self_mixed_grad, grads
    )

    advance(bits, ffn_a, ffn_b)
    rest_a = Scatter(grads, "xyz")
    encoder_out_grad, grads = encoder_finish(
        mine, (cross_own0, cross_own1), (came0, came1), encoder_own, cross_key, cross_value, after=[ffn_a.keep]
    )
    encoder_out_grad, grads, self_mixed_grad = fence([rest_a], encoder_out_grad, grads, self_mixed_grad)

    rest_b = Scatter(grads, "yxz")
    encoder_out_grad = from_rows(encoder_out_grad, odd)

    def self_half(start, count, do):
        return self_backward(
            blocks, query_rows, key_all, value_all, self_mixed, do, self_lanes, dec_lanes, table_t, start, count
        )

    self_q0, self_own0, self_other0, table_grad0 = self_half(0, first, self_mixed_grad)
    encoder_out_grad, self_q0, self_own0, self_other0, self_mixed_grad = fence(
        [ffn_a, ffn_b, rest_a, rest_b], encoder_out_grad, self_q0, self_own0, self_other0, self_mixed_grad
    )

    level(ffn_a, ffn_b, bits=bits)
    advance(bits, (ffn_a, ffn_b), rest_a, rest_b)
    came0 = came_parts(self_other0, rows)
    self_q1, self_own1, self_other1, table_grad1 = self_half(first, rest, self_mixed_grad)
    came0, self_q1, self_own1, self_other1, table_grad1 = fence(
        [ffn_a, rest_b], came0, self_q1, self_own1, self_other1, table_grad1
    )

    came1 = came_parts(self_other1, rows)
    query_grads = query_grad(mine, (self_q0, self_q1), self_in)
    (query_grads,) = fence([], query_grads)

    own_q = Scatter(query_grads, "yxz")
    small = table_sums(table_grad0, table_grad1, cross_gain_grad, ffn_gain_grad)
    came1, small = fence([ffn_a, rest_a, rest_b, own_q], came1, small)

    advance(bits, ffn_a, rest_a, rest_b, own_q)
    sums, grads = key_grads(mine, (self_own0, self_own1), (came0, came1), self_in, after=[rest_a.keep])
    sums, grads = fence([], sums, grads)

    own = Scatter(grads, "yxz")
    decoder_in_grad, small = self_finish_back(
        (self_q0, self_q1),
        sums,
        hidden_own,
        gain_self,
        hidden_one_grad,
        self_query,
        self_key,
        self_value,
        small,
    )
    decoder_in_grad, small = fence([ffn_a, rest_a, rest_b, own_q, own], decoder_in_grad, small)

    small_bits = [("dp", 0), ("dp", 2), ("mem", 0), ("dp", 1), ("dp", 3)]
    small_bits = [name for name in small_bits if name in all_bits()]
    small_bits += [name for name in all_bits() if name not in small_bits]

    def add_small(small, rounds=1):
        for _ in range(min(rounds, len(small_bits))):
            small = small + swap_many(small, (small_bits.pop(0),))
        return small

    own_k, own_v = own.parts("yxz", "xyz")
    level(rest_a, rest_b, bits=bits)
    advance(bits, own_k, own_v, own_q, (rest_a, rest_b))
    (small,) = fence([own_k, own_v, own_q, rest_a], add_small(small, 2))

    advance(bits, own_k, own_v)
    decoder_in_grad = from_rows(decoder_in_grad, odd)
    (small,) = fence([own_k, own_v], add_small(small))

    level(own_k, own_v, own_q, bits=bits)
    advance(bits, (own_k, own_v, own_q), rest_a)
    (small,) = fence([own_k], add_small(small))
    small = add_small(small, len(small_bits))
    for scatter in (own_k, ffn_a, rest_a):
        while scatter.order:
            advance(bits, scatter)
    parts = small
    self_gain_sum, cross_gain_sum, ffn_gain_sum, table_sum, grad_fo, grad_fi, *squares = write_grads(
        ffn_a, rest_a, own_k, parts, small_block(rows // 2), width, ffn_in.shape[1]
    )
    self_gain_sum, cross_gain_sum, ffn_gain_sum = self_gain_sum[0], cross_gain_sum[0], ffn_gain_sum[0]
    grad_co, grad_cq, grad_so, grad_ck, grad_cv, grad_sk, grad_sv, grad_sq = squares
    return (
        layer_out[None],
        decoder_in_grad[None],
        encoder_out_grad[None],
        self_gain_sum,
        cross_gain_sum,
        ffn_gain_sum,
        table_sum,
        grad_sq,
        grad_sk,
        grad_sv,
        grad_so,
        grad_cq,
        grad_ck,
        grad_cv,
        grad_co,
        grad_fi,
        grad_fo,
    )


def solution(mesh):
    in_specs = (
        P("dp", "mem", None),
        P("dp", "mem", None),
        P("dp", "mem"),
        P("dp", "mem"),
        P("dp", "mem"),
        P("dp", "mem"),
        P(),
        P(),
        P(),
        P(),
        P(),
        P(),
        P(),
        P(),
        P(),
        P(),
        P(),
        P(),
        P(),
        P(),
        P("dp", "mem", None),
    )
    out_specs = (
        P("dp", "mem", None),
        P("dp", "mem", None),
        P("dp", "mem", None),
        P(),
        P(),
        P(),
        P(),
        P("dp", "mem"),
        P("dp", "mem"),
        P("dp", "mem"),
        P("dp", "mem"),
        P("dp", "mem"),
        P("dp", "mem"),
        P("dp", "mem"),
        P("dp", "mem"),
        P("dp", "mem"),
        P("dp", "mem"),
    )
    return jax.shard_map(
        on_device, mesh=mesh, in_specs=in_specs, out_specs=out_specs, check_vma=False
    )
```

time: 1200 us -> 296 us (0.25)
  waiting for transfers between devices: 659 us -> 48.8 us
  matrix products: 281 us -> 0.44 us
  Pallas kernels: 0 us -> 163 us
  local copies, waits for them, and re-layouts: 105 us -> 8.64 us
  other arithmetic: 79.2 us -> 10.3 us
  starting transfers between devices: 2.13 us -> 59.3 us
  blocking collectives: 49.7 us -> 0 us
  between operations: 15.6 us -> 2.09 us
    reduce_scatter x15 -> x0, waiting for transfers between devices: 491 us -> none  [the longest x1 73.2 us: on_device(): lax.psum_scatter(ffn_out_grad.astype(jnp.bfloat16), 'dp', scatter_dimensi...]
    dot_general x44 -> x2, matrix products: 281 us -> 0.44 us  [bias_of(): jnp.einsum('...b,bh->h...', jnp.asarray(hot), rel_bias - rel_bias[BUCKETS...]
    unnamed x37 -> x0, waiting for transfers between devices: 168 us -> none
    pallas_call x0 -> x27, Pallas kernels: none -> 163 us  [the longest x26 155 us: run(): pl.pallas_call(body, grid_spec=pltpu.PrefetchScalarGridSpec(num_scalar_pr...]
    ppermute x0 -> x47, starting transfers between devices: none -> 59.3 us  [the longest x25 33.6 us: swap_many(): return lax.ppermute(values, ('dp', 'mem'), moves)]
    ppermute x0 -> x47, waiting for transfers between devices: none -> 48.8 us  [the longest x25 43.9 us: swap_many(): return lax.ppermute(values, ('dp', 'mem'), moves)]
    convert_element_type x15 -> x1, other arithmetic: 47.7 us -> 1.19 us  [on_device(): tags.astype(BF16)]
    psum x1 -> x0, blocking collectives: 40.1 us -> none  [on_device(): lax.psum((self_gain_grad, cross_gain_grad, ffn_gain_grad, table_grad), ('...]
  transfers between devices with their start and end apart: 28 -> 47, of which waited for: 19 -> 12; matrix products, arithmetic and copies ran while one was open for 29% -> 2% of each run, Pallas kernels for 0% -> 39%
where the time goes in v1:
time: 296 us; the launch traced here: 292 us
  Pallas kernels  163 us (55%)
  starting transfers between devices  59.3 us (20%)
  waiting for transfers between devices  48.8 us (16%)
  other arithmetic  10.3 us (3%)
  local copies, waits for them, and re-layouts  8.64 us (3%)
    pallas_call x26, Pallas kernels, run(): pl.pallas_call(body, grid_spec=pltpu.PrefetchScalarGridSpec(num_scalar_pr...  155 us
    ppermute x25, waiting for transfers between devices, swap_many(): return lax.ppermute(values, ('dp', 'mem'), moves)  43.9 us
    ppermute x25, starting transfers between devices, swap_many(): return lax.ppermute(values, ('dp', 'mem'), moves)  33.6 us
    ppermute x4, starting transfers between devices, to_rows(): lax.ppermute(piece, ('dp', 'mem'), move)  9.05 us
    pallas_call x1, Pallas kernels, bias_tables(): pl.pallas_call(table_kernel, grid=(HEADS // heads,), in_specs=[spec, spec...  7.26 us
    ppermute x3, starting transfers between devices, from_rows(): second = lax.ppermute(second, ('dp', 'mem'), back[1])  6.67 us
    unnamed x105, local copies, waits for them, and re-layouts  6.64 us
    ppermute x6, starting transfers between devices, group_shift(): return lax.ppermute(values, ('dp', 'mem'), moves)  6.13 us
  transfers between devices with their start and end apart: 47, of which 12 were waited for; matrix products, arithmetic and copies ran while one was open for 2% of the time, Pallas kernels for 39%

profile of v1, /device:TPU:0, one launch (start us, length us, event | category | flops | bytes accessed | tf_op | source)
XLA Modules:
  0.0 292.3 jit_solution(10100445369283901285)
XLA Ops:
  0.8 1.2 select_convert_fusion
  2.0 1.2 pad_maximum_fusion.5
  5.2 7.3 %bias_tables.1 = (f32[12,4,128,128]{3,2,1,0:T(8,128)}, f32[12,4,128,128]{3,2,1,0:T(8,128)}) custom-call(f32[12,2,1,256]{3,2,1,0:T(1,128)S(1)} %copy.55.base_ref, f32[12,2,1,256]{3,2,1,0:T(1,128)S(1)} %broadcast_in_dim.115.base_t_ref), custom_call_target="tpu_custom_call" | custom-call | tf_op jit(solution)/shard_map/bias_tables/pallas_call | solution.py:183
  12.8 4.8 %collective-permute-start.4 = (bf16[512,896]{1,0:T(8,128)(2,1)S(1)}, bf16[512,896]{1,0:T(8,128)(2,1)}, u32[]{:S(2)}, u32[]{:S(2)}) collective-permute-start(bf16[512,896]{1,0:T(8,128)(2,1)S(1)} %pad_maximum_fusion.1.refs_0_.refs_7_.refs_3_), channel_id=1, source_target_pairs={{0,2},{1,3},{2,0},{3,1},{4,6},{5,7},{6,4},{7,5},{8,10},{9,11},{10,... | collective-permute-start | bytes 2752520 | tf_op jit(solution)/shard_map/ppermute | solution.py:105
  17.6 1.3 fusion.15
  18.9 7.9 %collective-permute-start.2 = (bf16[2,256,768]{2,1,0:T(8,128)(2,1)}, bf16[2,256,768]{2,1,0:T(8,128)(2,1)}, u32[]{:S(2)}, u32[]{:S(2)}) collective-permute-start(bf16[2,256,768]{2,1,0:T(8,128)(2,1)} %get-tuple-element.514), channel_id=1, source_target_pairs={{0,0},{1,2},{2,1},{3,3},{4,4},{5,6},{6,5},{7,7},{8,8},{9,10},{10,9... | collective-permute-start | bytes 2359304 | tf_op jit(solution)/shard_map/ppermute | solution.py:74
  27.5 1.3 copy-done.13
  28.8 4.6 %own_project.1 = (bf16[512,768]{1,0:T(8,128)(2,1)}, bf16[512,768]{1,0:T(8,128)(2,1)}, bf16[1024,768]{1,0:T(8,128)(2,1)}, bf16[1024,768]{1,0:T(8,128)(2,1)}, bf16...) custom-call(bf16[512,896]{1,0:T(8,128)(2,1)S(1)} %pad_maximum_fusion, ...), custom_call_target="tpu_custom_call" | custom-call | flops 113246208 | bytes 614656 | tf_op jit(solution)/shard_map/own_project/pallas_call | solution.py:474
  33.4 4.3 %other_project.1 = (bf16[1024,768]{1,0:T(8,128)(2,1)}, bf16[1024,768]{1,0:T(8,128)(2,1)}, bf16[1024,128]{1,0:T(8,128)(2,1)}, bf16[1024,128]{1,0:T(8,128)(2,1)}, f32[1,128]{1,0:T(1,128)S(1)}) custom-call(bf16[512,896]{1,0:T(8,128)(2,1)} %collective-permute-done.4.refs_0_, ...), custom_call_target="tpu_custom_call", output_to_operand_aliasing={{0}: (4, {}), {1}: (5, {}), {2}: (6, {}), {3}: (7, {})} | custom-call | flops 75497472 | bytes 663776 | tf_op jit(solution)/shard_map/other_project/pallas_call | solution.py:474
  37.7 14.0 %self_forward.1 = (bf16[512,768]{1,0:T(8,128)(2,1)}, bf16[12,512,128]{2,1,0:T(8,128)(2,1)}, f32[512,768]{1,0:T(8,128)S(1)}, bf16[512,768]{1,0:T(8,128)(2,1)S(1)}...) custom-call(s32[4,5]{1,0:T(4,128)S(1)} %pad_add_fusion.refs_0_, bf16[512,768]{1,0:T(8,128)(2,1)} %get-tuple-element.251.refs_1_, ...), custom_call_target="tpu_custom_call" | custom-call | flops 251658240 | bytes 1016128 | tf_op jit(solution)/shard_map/self_forward/pallas_call | solution.py:474
  51.8 2.6 broadcast_select_fusion
  56.1 3.3 %encoder_project.2 = (bf16[1024,768]{1,0:T(8,128)(2,1)}, bf16[1024,768]{1,0:T(8,128)(2,1)}, f32[1,128]{1,0:T(1,128)S(1)}) custom-call(bf16[512,768]{1,0:T(8,128)(2,1)S(1)} %get-tuple-element.510.refs_0_.refs_5_, bf16[768,768]{1,0:T(8,128)(2,1)S(1)} %copy-done.3, bf16[768,768]{1,0:T(8,128)(2,1)S(1)} %copy-done.5), custom_call_target="tpu_custom_call" | custom-call | flops 75497472 | bytes 393248 | tf_op jit(solution)/shard_map/encoder_project/pallas_call | solution.py:474
  59.4 3.3 %encoder_project.3 = (bf16[1024,768]{1,0:T(8,128)(2,1)}, bf16[1024,768]{1,0:T(8,128)(2,1)}, f32[1,128]{1,0:T(1,128)S(1)}) custom-call(bf16[512,768]{1,0:T(8,128)(2,1)S(1)} %collective-permute-done.5.refs_0_, bf16[768,768]{1,0:T(8,128)(2,1)S(1)} %copy-done.3, bf16[768,768]{1,0:T(8,128)(2,1)S(1)} %copy-done.5, ...), custom_call_target="tpu_custom_call", output_to_operand_aliasing={{0}: (3, {}), {1}: (4, {})} | custom-call | flops 75497472 | bytes 589856 | tf_op jit(solution)/shard_map/encoder_project/pallas_call | solution.py:474
  62.7 13.3 %cross_forward.1 = (bf16[512,768]{1,0:T(8,128)(2,1)}, bf16[12,512,128]{2,1,0:T(8,128)(2,1)}, f32[512,768]{1,0:T(8,128)S(1)}, bf16[512,768]{1,0:T(8,128)(2,1)S(1)}) custom-call(bf16[512,768]{1,0:T(8,128)(2,1)} %copy-done.8, bf16[1024,768]{1,0:T(8,128)(2,1)} %get-tuple-element.278.refs_1_, bf16[1024,768]{1,0:T(8,128)(2,1)} %get-tuple-element.279.refs_2_, ...), custom_call_target="tpu_custom_call" | custom-call | flops 402653184 | bytes 737568 | tf_op jit(solution)/shard_map/cross_forward/pallas_call | solution.py:474
  76.0 25.8 %feed_forward.1 = (bf16[512,768]{1,0:T(8,128)(2,1)S(1)}, f32[512,768]{1,0:T(8,128)S(1)}, bf16[512,768]{1,0:T(8,128)(2,1)S(1)}, bf16[512,768]{1,0:T(8,128)(2,1)S(...) custom-call(s32[1]{0:T(128)} %bitcast.refs_0_, ...), custom_call_target="tpu_custom_call" | custom-call | flops 905969664 | bytes 1696128 | tf_op jit(solution)/shard_map/feed_forward/pallas_call | solution.py:474
  103.2 3.4 %collective-permute-start.9 = (bf16[256,768]{1,0:T(8,128)(2,1)S(1)}, bf16[256,768]{1,0:T(8,128)(2,1)S(1)}, u32[]{:S(2)}, u32[]{:S(2)}) collective-permute-start(bf16[256,768]{1,0:T(8,128)(2,1)S(1)} %get-tuple-element.524), channel_id=1, source_target_pairs={{2,0},{0,1},{3,2},{1,3},{6,4},{4,5},{7,6},{5,7},{10,8},{8,9},{11,1... | collective-permute-start | bytes 1179656 | tf_op jit(solution)/shard_map/ppermute | solution.py:91
  106.6 11.3 %cross_backward.2 = (bf16[512,384]{1,0:T(8,128)(2,1)}, bf16[2,512,384]{2,1,0:T(8,128)(2,1)}, bf16[2,512,384]{2,1,0:T(8,128)(2,1)}) custom-call(bf16[512,768]{1,0:T(8,128)(2,1)} %copy-done.8, bf16[1024,768]{1,0:T(8,128)(2,1)} %get-tuple-element.278.refs_1_, bf16[1024,768]{1,0:T(8,128)(2,1)} %get-tuple-element.279.refs_2_, ...), custom_call_target="tpu_custom_call" | custom-call | flops 503316480 | bytes 581632 | tf_op jit(solution)/shard_map/cross_backward/pallas_call | solution.py:474
  119.1 7.1 %advance.8 = (bf16[1,1,8,192,384]{4,3,2,1,0:T(8,128)(2,1)}, bf16[1,1,8,192,384]{4,3,2,1,0:T(8,128)(2,1)}, bf16[8,1,1,192,384]{4,3,2,1,0:T(8,128)(2,1)}, bf16[8,1,1,192,384]{4,3,2,1,0:T(8,128)(2,1)}) custom-call(s32[5]{0:T(128)S(1)} %stack.153.refs_0_, bf16[1,2,1,1,8,192,384]{6,5,4,3,2,1,0:T(8,128)(2,1)} %bitcast.220, ...), custom_call_target="tpu_custom_call" | custom-call | flops 589824 | bytes 884736 | tf_op jit(solution)/shard_map/advance/pallas_call | solution.py:474
  126.2 1.7 collective-permute-start.10
  127.9 0.9 collective-permute-start.11
  128.9 11.4 %cross_backward.3 = (bf16[512,384]{1,0:T(8,128)(2,1)}, bf16[2,512,384]{2,1,0:T(8,128)(2,1)}, bf16[2,512,384]{2,1,0:T(8,128)(2,1)}) custom-call(bf16[512,768]{1,0:T(8,128)(2,1)} %copy-done.8, bf16[1024,768]{1,0:T(8,128)(2,1)} %get-tuple-element.278.refs_1_, bf16[1024,768]{1,0:T(8,128)(2,1)} %get-tuple-element.279.refs_2_, ...), custom_call_target="tpu_custom_call" | custom-call | flops 503316480 | bytes 581632 | tf_op jit(solution)/shard_map/cross_backward/pallas_call | solution.py:474
  140.7 1.0 copy-done.38
  141.7 5.8 %cross_finish.1 = (f32[512,768]{1,0:T(8,128)}, bf16[512,768]{1,0:T(8,128)(2,1)S(1)}, f32[1,768]{1,0:T(1,128)S(1)}, bf16[2,8,144,384]{3,2,1,0:T(8,128)(2,1)S(1)}, bf16[2,8,144,384]{3,2,1,0:T(8,128)(2,1)S(1)}) custom-call(s32[1]{0:T(128)} %bitcast.refs_0_, bf16[512,384]{1,0:T(8,128)(2,1)S(1)} %copy-done.37, bf16[512,384]{1,0:T(8,128)(2,1)S(1)} %copy-done.38, ...), custom_call_target="tpu_custom_call" | custom-call | flops 188743680 | bytes 958848 | tf_op jit(solution)/shard_map/cross_finish/pallas_call | solution.py:474
  147.5 7.2 %collective-permute-done.10 = bf16[2,2,2,192,384]{4,3,2,1,0:T(8,128)(2,1)S(1)} collective-permute-done((bf16[2,2,2,192,384]{4,3,2,1,0:T(8,128)(2,1)}, bf16[2,2,2,192,384]{4,3,2,1,0:T(8,128)(2,1)S(1)}, u32[]{:S(2)}, u32[]{:S(2)}) %collective-permute-start.10) | collective-permute-done | bytes 1179680 | tf_op jit(solution)/shard_map/ppermute | solution.py:394
  154.7 1.2 collective-permute-done.11
  155.9 1.1 advance.9
  157.9 4.1 %encoder_finish.1 = (bf16[512,768]{1,0:T(8,128)(2,1)S(1)}, bf16[2,8,96,384]{3,2,1,0:T(8,128)(2,1)S(1)}, bf16[2,8,96,384]{3,2,1,0:T(8,128)(2,1)S(1)}) custom-call(s32[1]{0:T(128)} %bitcast.refs_0_, bf16[2,512,384]{2,1,0:T(8,128)(2,1)S(1)} %copy-done.34, bf16[2,512,384]{2,1,0:T(8,128)(2,1)S(1)} %copy-done.35, ...), custom_call_target="tpu_custom_call" | custom-call | flops 150994944 | bytes 589824 | tf_op jit(solution)/shard_map/encoder_finish/pallas_call | solution.py:474
  162.6 1.6 collective-permute-start.14
  164.2 1.7 collective-permute-start.15
  166.6 2.4 collective-permute-start.19
  169.0 13.0 %self_backward.2 = (bf16[512,384]{1,0:T(8,128)(2,1)}, bf16[2,512,384]{2,1,0:T(8,128)(2,1)}, bf16[2,512,384]{2,1,0:T(8,128)(2,1)}, f32[6,4,128,128]{3,2,1,0:T(8,128)}) custom-call(s32[4,5]{1,0:T(4,128)S(1)} %pad_add_fusion.refs_0_, bf16[512,768]{1,0:T(8,128)(2,1)} %get-tuple-element.251.refs_1_, bf16[1024,768]{1,0:T(8,128)(2,1)} %get-tuple-element.261.refs_2_, ...), custom_call_target="tpu_custom_call" | custom-call | flops 314572800 | bytes 876544 | tf_op jit(solution)/shard_map/self_backward/pallas_call | solution.py:474
  182.0 4.8 %collective-permute-done.19 = bf16[256,768]{1,0:T(8,128)(2,1)S(1)} collective-permute-done((bf16[256,768]{1,0:T(8,128)(2,1)S(1)}, bf16[256,768]{1,0:T(8,128)(2,1)S(1)}, u32[]{:S(2)}, u32[]{:S(2)}) %collective-permute-start.19) | collective-permute-done | bytes 393248 | tf_op jit(solution)/shard_map/ppermute | solution.py:91
  188.5 1.5 advance.10
  191.1 1.9 collective-permute-start.23
  193.0 12.8 %self_backward.3 = (bf16[512,384]{1,0:T(8,128)(2,1)}, bf16[2,512,384]{2,1,0:T(8,128)(2,1)}, bf16[2,512,384]{2,1,0:T(8,128)(2,1)}, f32[6,4,128,128]{3,2,1,0:T(8,128)}) custom-call(s32[4,5]{1,0:T(4,128)S(1)} %pad_add_fusion.refs_0_, bf16[512,768]{1,0:T(8,128)(2,1)} %get-tuple-element.251.refs_1_, bf16[1024,768]{1,0:T(8,128)(2,1)} %get-tuple-element.261.refs_2_, ...), custom_call_target="tpu_custom_call" | custom-call | flops 314572800 | bytes 876544 | tf_op jit(solution)/shard_map/self_backward/pallas_call | solution.py:474
  206.0 1.0 copy-done.23
  207.0 0.9 query_grad.1
  208.5 5.6 %table_sums.1.refs_9_ = f32[16,768]{1,0:T(8,128)S(1)} custom-call(f32[6,4,128,128]{3,2,1,0:T(8,128)} %get-tuple-element.382.refs_0_, f32[6,4,128,128]{3,2,1,0:T(8,128)} %get-tuple-element.383.refs_1_, f32[1,768]{1,0:T(1,128)S(1)} %get-tuple-element.384.refs_2_, f32[1,768]{1,0:T(1,128)S(1)} %get-tuple-element.385.refs_3_), custom_call_target="tpu_custom_call" | custom-call | bytes 200064 | tf_op jit(solution)/shard_map/table_sums/pallas_call | solution.py:474
  214.1 1.2 advance.11
  215.4 1.7 key_grads.1
  217.2 1.6 collective-permute-start.27
  218.8 3.6 %collective-permute-start.26 = (bf16[384,384]{1,0:T(8,128)(2,1)S(1)}, bf16[384,384]{1,0:T(8,128)(2,1)S(1)}, u32[]{:S(2)}, u32[]{:S(2)}) collective-permute-start(bf16[384,384]{1,0:T(8,128)(2,1)S(1)} %bitcast.213), channel_id=1, source_target_pairs={{0,16},{1,17},{2,18},{3,19},{4,20},{5,21},{6,22},{7,23},{8,24},{9,... | collective-permute-start | bytes 884744 | tf_op jit(solution)/shard_map/ppermute | solution.py:394
  222.4 1.0 collective-permute-start.28
  223.4 1.5 collective-permute-start.29
  225.0 5.1 %self_finish_back.1 = (bf16[512,768]{1,0:T(8,128)(2,1)}, f32[16,768]{1,0:T(8,128)S(1)}) custom-call(bf16[512,384]{1,0:T(8,128)(2,1)} %get-tuple-element.376.refs_1_.refs_0_, bf16[512,384]{1,0:T(8,128)(2,1)} %get-tuple-element.377.refs_2_.refs_1_, bf16[2,512,768]{2,1,0:T(8,128)(2,1)S(1)} %get-tuple-element.408.refs_2_, bf16[512,896]{1,0:T(8,128)(2,1)} %copy-done, ...), custom_call_target="tpu_custom_call" | custom-call | flops 113246208 | bytes 579776 | tf_op jit(solution)/shard_map/self_finish_back/pallas_call | solution.py:474
  230.1 6.0 %collective-permute-done.26.refs_1_ = bf16[384,384]{1,0:T(8,128)(2,1)S(1)} collective-permute-done((bf16[384,384]{1,0:T(8,128)(2,1)S(1)}, bf16[384,384]{1,0:T(8,128)(2,1)S(1)}, u32[]{:S(2)}, u32[]{:S(2)}) %collective-permute-start.26) | collective-permute-done | bytes 294944 | tf_op jit(solution)/shard_map/ppermute | solution.py:394
  236.1 1.1 advance.12
  237.2 1.4 collective-permute-start.36
  238.6 1.7 collective-permute-start.33
  241.2 1.2 collective-permute-start.35
  243.0 5.8 %collective-permute-done.38 = f32[16,768]{1,0:T(8,128)S(1)} collective-permute-done((f32[16,768]{1,0:T(8,128)S(1)}, f32[16,768]{1,0:T(8,128)S(1)}, u32[]{:S(2)}, u32[]{:S(2)}) %collective-permute-start.38) | collective-permute-done | bytes 49184 | tf_op jit(solution)/shard_map/ppermute | solution.py:394
  249.5 3.1 %collective-permute-done.35 = bf16[2,2,48,384]{3,2,1,0:T(8,128)(2,1)S(1)} collective-permute-done((bf16[2,2,48,384]{3,2,1,0:T(8,128)(2,1)S(1)}, bf16[2,2,48,384]{3,2,1,0:T(8,128)(2,1)S(1)}, u32[]{:S(2)}, u32[]{:S(2)}) %collective-permute-start.35) | collective-permute-done | bytes 147488 | tf_op jit(solution)/shard_map/ppermute | solution.py:394
  254.3 1.7 collective-permute-start.40
  256.0 1.9 collective-permute-start.41
  257.9 7.6 %collective-permute-done.41 = f32[16,768]{1,0:T(8,128)S(1)} collective-permute-done((f32[16,768]{1,0:T(8,128)S(1)}, f32[16,768]{1,0:T(8,128)S(1)}, u32[]{:S(2)}, u32[]{:S(2)}) %collective-permute-start.41) | collective-permute-done | bytes 49184 | tf_op jit(solution)/shard_map/ppermute | solution.py:394
  266.3 1.5 collective-permute-start.43
  267.9 2.6 collective-permute-start.42
  270.9 3.7 %collective-permute-done.44 = f32[16,768]{1,0:T(8,128)S(1)} collective-permute-done((f32[16,768]{1,0:T(8,128)S(1)}, f32[16,768]{1,0:T(8,128)S(1)}, u32[]{:S(2)}, u32[]{:S(2)}) %collective-permute-start.44) | collective-permute-done | bytes 49184 | tf_op jit(solution)/shard_map/ppermute | solution.py:394
  274.6 4.0 %collective-permute-done.43 = bf16[2,144,384]{2,1,0:T(8,128)(2,1)S(1)} collective-permute-done((bf16[2,144,384]{2,1,0:T(8,128)(2,1)S(1)}, bf16[2,144,384]{2,1,0:T(8,128)(2,1)S(1)}, u32[]{:S(2)}, u32[]{:S(2)}) %collective-permute-start.43) | collective-permute-done | bytes 221216 | tf_op jit(solution)/shard_map/ppermute | solution.py:394
  279.2 3.0 %collective-permute-start.45 = (bf16[144,384]{1,0:T(8,128)(2,1)S(1)}, bf16[144,384]{1,0:T(8,128)(2,1)S(1)}, u32[]{:S(2)}, u32[]{:S(2)}) collective-permute-start(bf16[144,384]{1,0:T(8,128)(2,1)S(1)} %bitcast.219), channel_id=1, source_target_pairs={{0,16},{1,17},{2,18},{3,19},{4,20},{5,21},{6,22},{7,23},{8,24},{9,... | collective-permute-start | bytes 331784 | tf_op jit(solution)/shard_map/ppermute | solution.py:394
  282.2 0.9 maximum_bitcast_fusion
  283.1 1.0 collective-permute-done.46
  284.1 4.4 %collective-permute-done.45.refs_5_ = bf16[144,384]{1,0:T(8,128)(2,1)S(1)} collective-permute-done((bf16[144,384]{1,0:T(8,128)(2,1)S(1)}, bf16[144,384]{1,0:T(8,128)(2,1)S(1)}, u32[]{:S(2)}, u32[]{:S(2)}) %collective-permute-start.45) | collective-permute-done | bytes 110624 | tf_op jit(solution)/shard_map/ppermute | solution.py:394
  288.5 1.1 write_grads.1
  (203 shorter events, 21.5 us)
Async XLA Ops:
  3.1 9.4 %collective-permute-start.1 = (bf16[256,896]{1,0:T(8,128)(2,1)S(1)}, bf16[256,896]{1,0:T(8,128)(2,1)S(1)}, u32[]{:S(2)}, u32[]{:S(2)}) collective-permute-start(bf16[256,896]{1,0:T(8,128)(2,1)S(1)} %get-tuple-element.517), channel_id=1, source_target_pairs={{0,2},{1,0},{2,3},{3,1},{4,6},{5,4},{6,7},{7,5},{8,10},{9,8},{10,1... | collective-permute-start | bytes 1376264 | tf_op jit(solution)/shard_map/ppermute | solution.py:74
  3.6 9.0 %collective-permute-start = (bf16[256,896]{1,0:T(8,128)(2,1)S(1)}, bf16[256,896]{1,0:T(8,128)(2,1)S(1)}, u32[]{:S(2)}, u32[]{:S(2)}) collective-permute-start(bf16[256,896]{1,0:T(8,128)(2,1)S(1)} %get-tuple-element.518), channel_id=1, source_target_pairs={{0,0},{1,2},{2,1},{3,3},{4,4},{5,6},{6,5},{7,7},{8,8},{9,10},{10,9... | collective-permute-start | bytes 1376264 | tf_op jit(solution)/shard_map/ppermute | solution.py:74
  12.8 14.7 %copy-start = (bf16[512,896]{1,0:T(8,128)(2,1)}, bf16[512,896]{1,0:T(8,128)(2,1)S(1)}, u32[]{:S(2)}) copy-start(bf16[512,896]{1,0:T(8,128)(2,1)S(1)} %pad_maximum_fusion.1.refs_0_.refs_7_.refs_3_) | copy-start | bytes 2752516
  12.8 14.2 %copy-start.46 = (f32[768]{0:T(1024)S(1)}, f32[768]{0:T(1024)}, u32[]{:S(2)}) copy-start(f32[768]{0:T(1024)} %param.32) | copy-start | bytes 9220
  12.8 14.3 %copy-start.47 = (f32[768]{0:T(1024)S(1)}, f32[768]{0:T(1024)}, u32[]{:S(2)}) copy-start(f32[768]{0:T(1024)} %param.33) | copy-start | bytes 9220
  12.8 14.7 %copy-start.1 = (bf16[768,768]{1,0:T(8,128)(2,1)S(1)}, bf16[768,768]{1,0:T(8,128)(2,1)}, u32[]{:S(2)}) copy-start(bf16[768,768]{1,0:T(8,128)(2,1)} %refs_7_.6) | copy-start | bytes 3538948
  12.8 14.7 %copy-start.2 = (bf16[768,768]{1,0:T(8,128)(2,1)S(1)}, bf16[768,768]{1,0:T(8,128)(2,1)}, u32[]{:S(2)}) copy-start(bf16[768,768]{1,0:T(8,128)(2,1)} %refs_8_.3) | copy-start | bytes 3538948
  12.8 20.6 %collective-permute-start.4 = (bf16[512,896]{1,0:T(8,128)(2,1)S(1)}, bf16[512,896]{1,0:T(8,128)(2,1)}, u32[]{:S(2)}, u32[]{:S(2)}) collective-permute-start(bf16[512,896]{1,0:T(8,128)(2,1)S(1)} %pad_maximum_fusion.1.refs_0_.refs_7_.refs_3_), channel_id=1, source_target_pairs={{0,2},{1,3},{2,0},{3,1},{4,6},{5,7},{6,4},{7,5},{8,10},{9,11},{10,... | collective-permute-start | bytes 2752520 | tf_op jit(solution)/shard_map/ppermute | solution.py:105
  18.9 32.9 %collective-permute-start.3 = (bf16[2,256,768]{2,1,0:T(8,128)(2,1)}, bf16[2,256,768]{2,1,0:T(8,128)(2,1)}, u32[]{:S(2)}, u32[]{:S(2)}) collective-permute-start(bf16[2,256,768]{2,1,0:T(8,128)(2,1)} %get-tuple-element.513), channel_id=1, source_target_pairs={{0,2},{1,0},{2,3},{3,1},{4,6},{5,4},{6,7},{7,5},{8,10},{9,8},{10,1... | collective-permute-start | bytes 2359304 | tf_op jit(solution)/shard_map/ppermute | solution.py:74
  18.9 32.9 %collective-permute-start.2 = (bf16[2,256,768]{2,1,0:T(8,128)(2,1)}, bf16[2,256,768]{2,1,0:T(8,128)(2,1)}, u32[]{:S(2)}, u32[]{:S(2)}) collective-permute-start(bf16[2,256,768]{2,1,0:T(8,128)(2,1)} %get-tuple-element.514), channel_id=1, source_target_pairs={{0,0},{1,2},{2,1},{3,3},{4,4},{5,6},{6,5},{7,7},{8,8},{9,10},{10,9... | collective-permute-start | bytes 2359304 | tf_op jit(solution)/shard_map/ppermute | solution.py:74
  54.6 4.8 %collective-permute-start.5 = (bf16[512,768]{1,0:T(8,128)(2,1)S(1)}, bf16[512,768]{1,0:T(8,128)(2,1)S(1)}, u32[]{:S(2)}, u32[]{:S(2)}) collective-permute-start(bf16[512,768]{1,0:T(8,128)(2,1)S(1)} %get-tuple-element.510.refs_0_.refs_5_), channel_id=1, source_target_pairs={{0,2},{1,3},{2,0},{3,1},{4,6},{5,7},{6,4},{7,5},{8,10},{9,11},{10,... | collective-permute-start | bytes 2359304 | tf_op jit(solution)/shard_map/ppermute | solution.py:105
  101.8 16.0 %copy-start.19 = (bf16[512,768]{1,0:T(8,128)(2,1)}, bf16[512,768]{1,0:T(8,128)(2,1)S(1)}, u32[]{:S(2)}) copy-start(bf16[512,768]{1,0:T(8,128)(2,1)S(1)} %get-tuple-element.308.refs_4_) | copy-start | bytes 2359300
  101.9 16.0 %copy-start.24 = (f32[512,768]{1,0:T(8,128)}, f32[512,768]{1,0:T(8,128)S(1)}, u32[]{:S(2)}) copy-start(f32[512,768]{1,0:T(8,128)S(1)} %get-tuple-element.315.refs_6_) | copy-start | bytes 4718596
  101.9 16.0 %copy-start.31 = (bf16[512,768]{1,0:T(8,128)(2,1)}, bf16[512,768]{1,0:T(8,128)(2,1)S(1)}, u32[]{:S(2)}) copy-start(bf16[512,768]{1,0:T(8,128)(2,1)S(1)} %get-tuple-element.317.refs_9_) | copy-start | bytes 2359300
  101.9 17.0 %collective-permute-start.6 = (bf16[2,8,192,384]{3,2,1,0:T(8,128)(2,1)}, bf16[2,8,192,384]{3,2,1,0:T(8,128)(2,1)}, u32[]{:S(2)}, u32[]{:S(2)}) collective-permute-start(bf16[2,8,192,384]{3,2,1,0:T(8,128)(2,1)} %get-tuple-element.288), channel_id=1, source_target_pairs={{0,2},{2,0},{4,6},{6,4},{8,10},{10,8},{12,14},{14,12},{16,18},{18,... | collective-permute-start | bytes 7077896 | tf_op jit(solution)/shard_map/ppermute | solution.py:383
  101.9 16.9 %collective-permute-start.7 = (bf16[2,8,192,384]{3,2,1,0:T(8,128)(2,1)}, bf16[2,8,192,384]{3,2,1,0:T(8,128)(2,1)}, u32[]{:S(2)}, u32[]{:S(2)}) collective-permute-start(bf16[2,8,192,384]{3,2,1,0:T(8,128)(2,1)} %get-tuple-element.290), channel_id=1, source_target_pairs={{0,2},{2,0},{4,6},{6,4},{8,10},{10,8},{12,14},{14,12},{16,18},{18,... | collective-permute-start | bytes 7077896 | tf_op jit(solution)/shard_map/ppermute | solution.py:383
  102.5 15.4 %collective-permute-start.8 = (bf16[256,768]{1,0:T(8,128)(2,1)S(1)}, bf16[256,768]{1,0:T(8,128)(2,1)S(1)}, u32[]{:S(2)}, u32[]{:S(2)}) collective-permute-start(bf16[256,768]{1,0:T(8,128)(2,1)S(1)} %get-tuple-element.523), channel_id=1, source_target_pairs={{0,0},{2,1},{1,2},{3,3},{4,4},{6,5},{5,6},{7,7},{8,8},{10,9},{9,10... | collective-permute-start | bytes 1179656 | tf_op jit(solution)/shard_map/ppermute | solution.py:90
  103.2 14.7 %collective-permute-start.9 = (bf16[256,768]{1,0:T(8,128)(2,1)S(1)}, bf16[256,768]{1,0:T(8,128)(2,1)S(1)}, u32[]{:S(2)}, u32[]{:S(2)}) collective-permute-start(bf16[256,768]{1,0:T(8,128)(2,1)S(1)} %get-tuple-element.524), channel_id=1, source_target_pairs={{2,0},{0,1},{3,2},{1,3},{6,4},{4,5},{7,6},{5,7},{10,8},{8,9},{11,1... | collective-permute-start | bytes 1179656 | tf_op jit(solution)/shard_map/ppermute | solution.py:91
  118.9 21.4 %collective-permute-start.12 = (bf16[2,512,384]{2,1,0:T(8,128)(2,1)}, bf16[2,512,384]{2,1,0:T(8,128)(2,1)}, u32[]{:S(2)}, u32[]{:S(2)}) collective-permute-start(bf16[2,512,384]{2,1,0:T(8,128)(2,1)} %get-tuple-element.307), channel_id=1, source_target_pairs={{0,2},{1,3},{2,0},{3,1},{4,6},{5,7},{6,4},{7,5},{8,10},{9,11},{10,... | collective-permute-start | bytes 2359304 | tf_op jit(solution)/shard_map/ppermute | solution.py:105
  119.1 21.6 %copy-start.29 = (bf16[512,768]{1,0:T(8,128)(2,1)S(1)}, bf16[512,768]{1,0:T(8,128)(2,1)}, u32[]{:S(2)}) copy-start(bf16[512,768]{1,0:T(8,128)(2,1)} %copy-done.28) | copy-start | bytes 2359300
  119.1 21.6 %copy-start.32 = (bf16[512,768]{1,0:T(8,128)(2,1)S(1)}, bf16[512,768]{1,0:T(8,128)(2,1)}, u32[]{:S(2)}) copy-start(bf16[512,768]{1,0:T(8,128)(2,1)} %copy-done.31) | copy-start | bytes 2359300
  119.1 21.6 %copy-start.37 = (bf16[512,384]{1,0:T(8,128)(2,1)S(1)}, bf16[512,384]{1,0:T(8,128)(2,1)}, u32[]{:S(2)}) copy-start(bf16[512,384]{1,0:T(8,128)(2,1)} %get-tuple-element.313.refs_1_) | copy-start | bytes 1179652
  126.2 28.4 %collective-permute-start.10 = (bf16[2,2,2,192,384]{4,3,2,1,0:T(8,128)(2,1)}, bf16[2,2,2,192,384]{4,3,2,1,0:T(8,128)(2,1)S(1)}, u32[]{:S(2)}, u32[]{:S(2)}) collective-permute-start(bf16[2,2,2,192,384]{4,3,2,1,0:T(8,128)(2,1)} %bitcast.233), channel_id=1, source_target_pairs={{0,1},{1,0},{2,3},{3,2},{4,5},{5,4},{6,7},{7,6},{8,9},{9,8},{10,11... | collective-permute-start | bytes 3538952 | tf_op jit(solution)/shard_map/ppermute | solution.py:394
  127.9 12.8 %copy-start.18 = (bf16[768,768]{1,0:T(8,128)(2,1)S(1)}, bf16[768,768]{1,0:T(8,128)(2,1)}, u32[]{:S(2)}) copy-start(bf16[768,768]{1,0:T(8,128)(2,1)} %refs_3_.7) | copy-start | bytes 3538948
  127.9 27.9 %collective-permute-start.11 = (bf16[2,2,2,192,384]{4,3,2,1,0:T(8,128)(2,1)}, bf16[2,2,2,192,384]{4,3,2,1,0:T(8,128)(2,1)S(1)}, u32[]{:S(2)}, u32[]{:S(2)}) collective-permute-start(bf16[2,2,2,192,384]{4,3,2,1,0:T(8,128)(2,1)} %bitcast.232), channel_id=1, source_target_pairs={{0,4},{1,5},{2,6},{3,7},{4,0},{5,1},{6,2},{7,3},{8,12},{9,13},{10,... | collective-permute-start | bytes 3538952 | tf_op jit(solution)/shard_map/ppermute | solution.py:394
  140.3 15.6 %collective-permute-start.13 = (bf16[2,512,384]{2,1,0:T(8,128)(2,1)}, bf16[2,512,384]{2,1,0:T(8,128)(2,1)S(1)}, u32[]{:S(2)}, u32[]{:S(2)}) collective-permute-start(bf16[2,512,384]{2,1,0:T(8,128)(2,1)} %get-tuple-element.312), channel_id=1, source_target_pairs={{0,2},{1,3},{2,0},{3,1},{4,6},{5,7},{6,4},{7,5},{8,10},{9,11},{10,... | collective-permute-start | bytes 2359304 | tf_op jit(solution)/shard_map/ppermute | solution.py:105
  141.7 14.1 %copy-start.26 = (bf16[1,1,8,192,384]{4,3,2,1,0:T(8,128)(2,1)S(1)}, bf16[1,1,8,192,384]{4,3,2,1,0:T(8,128)(2,1)}, u32[]{:S(2)}) copy-start(bf16[1,1,8,192,384]{4,3,2,1,0:T(8,128)(2,1)} %get-tuple-element.303) | copy-start | bytes 3538948
  141.7 14.1 %copy-start.27 = (bf16[8,1,1,192,384]{4,3,2,1,0:T(8,128)(2,1)S(1)}, bf16[8,1,1,192,384]{4,3,2,1,0:T(8,128)(2,1)}, u32[]{:S(2)}) copy-start(bf16[8,1,1,192,384]{4,3,2,1,0:T(8,128)(2,1)} %get-tuple-element.305) | copy-start | bytes 3538948
  155.8 6.2 %collective-permute-start.16 = (bf16[2,8,144,384]{3,2,1,0:T(8,128)(2,1)S(1)}, bf16[2,8,144,384]{3,2,1,0:T(8,128)(2,1)S(1)}, u32[]{:S(2)}, u32[]{:S(2)}) collective-permute-start(bf16[2,8,144,384]{3,2,1,0:T(8,128)(2,1)S(1)} %get-tuple-element.332), channel_id=1, source_target_pairs={{0,2},{2,0},{4,6},{6,4},{8,10},{10,8},{12,14},{14,12},{16,18},{18,... | collective-permute-start | bytes 5308424 | tf_op jit(solution)/shard_map/ppermute | solution.py:383
  162.0 25.7 %collective-permute-start.17 = (bf16[2,8,96,384]{3,2,1,0:T(8,128)(2,1)S(1)}, bf16[2,8,96,384]{3,2,1,0:T(8,128)(2,1)S(1)}, u32[]{:S(2)}, u32[]{:S(2)}) collective-permute-start(bf16[2,8,96,384]{3,2,1,0:T(8,128)(2,1)S(1)} %get-tuple-element.344), channel_id=1, source_target_pairs={{0,2},{2,0},{4,6},{6,4},{8,10},{10,8},{12,14},{14,12},{16,18},{18,... | collective-permute-start | bytes 3538952 | tf_op jit(solution)/shard_map/ppermute | solution.py:383
  162.6 25.2 %collective-permute-start.14 = (bf16[2,2,192,384]{3,2,1,0:T(8,128)(2,1)S(1)}, bf16[2,2,192,384]{3,2,1,0:T(8,128)(2,1)S(1)}, u32[]{:S(2)}, u32[]{:S(2)}) collective-permute-start(bf16[2,2,192,384]{3,2,1,0:T(8,128)(2,1)S(1)} %bitcast.204), channel_id=1, source_target_pairs={{0,4},{1,5},{2,6},{3,7},{4,0},{5,1},{6,2},{7,3},{8,12},{9,13},{10,... | collective-permute-start | bytes 1769480 | tf_op jit(solution)/shard_map/ppermute | solution.py:394
  164.2 23.6 %collective-permute-start.15 = (bf16[2,2,192,384]{3,2,1,0:T(8,128)(2,1)S(1)}, bf16[2,2,192,384]{3,2,1,0:T(8,128)(2,1)S(1)}, u32[]{:S(2)}, u32[]{:S(2)}) collective-permute-start(bf16[2,2,192,384]{3,2,1,0:T(8,128)(2,1)S(1)} %bitcast.203), channel_id=1, source_target_pairs={{0,1},{1,0},{2,3},{3,2},{4,5},{5,4},{6,7},{7,6},{8,9},{9,8},{10,11... | collective-permute-start | bytes 1769480 | tf_op jit(solution)/shard_map/ppermute | solution.py:394
  165.9 16.1 %collective-permute-start.18 = (bf16[256,768]{1,0:T(8,128)(2,1)S(1)}, bf16[256,768]{1,0:T(8,128)(2,1)S(1)}, u32[]{:S(2)}, u32[]{:S(2)}) collective-permute-start(bf16[256,768]{1,0:T(8,128)(2,1)S(1)} %get-tuple-element.521), channel_id=1, source_target_pairs={{0,0},{2,1},{1,2},{3,3},{4,4},{6,5},{5,6},{7,7},{8,8},{10,9},{9,10... | collective-permute-start | bytes 1179656 | tf_op jit(solution)/shard_map/ppermute | solution.py:90
  166.6 20.2 %collective-permute-start.19 = (bf16[256,768]{1,0:T(8,128)(2,1)S(1)}, bf16[256,768]{1,0:T(8,128)(2,1)S(1)}, u32[]{:S(2)}, u32[]{:S(2)}) collective-permute-start(bf16[256,768]{1,0:T(8,128)(2,1)S(1)} %get-tuple-element.522), channel_id=1, source_target_pairs={{2,0},{0,1},{3,2},{1,3},{6,4},{4,5},{7,6},{5,7},{10,8},{8,9},{11,1... | collective-permute-start | bytes 1179656 | tf_op jit(solution)/shard_map/ppermute | solution.py:91
  187.8 18.1 %collective-permute-start.22 = (bf16[2,512,384]{2,1,0:T(8,128)(2,1)S(1)}, bf16[2,512,384]{2,1,0:T(8,128)(2,1)S(1)}, u32[]{:S(2)}, u32[]{:S(2)}) collective-permute-start(bf16[2,512,384]{2,1,0:T(8,128)(2,1)S(1)} %copy-done.51), channel_id=1, source_target_pairs={{0,2},{1,3},{2,0},{3,1},{4,6},{5,7},{6,4},{7,5},{8,10},{9,11},{10,... | collective-permute-start | bytes 2359304 | tf_op jit(solution)/shard_map/ppermute | solution.py:105
  190.0 15.8 %collective-permute-start.20 = (bf16[2,384,384]{2,1,0:T(8,128)(2,1)S(1)}, bf16[2,384,384]{2,1,0:T(8,128)(2,1)S(1)}, u32[]{:S(2)}, u32[]{:S(2)}) collective-permute-start(bf16[2,384,384]{2,1,0:T(8,128)(2,1)S(1)} %bitcast.206), channel_id=1, source_target_pairs={{0,8},{1,9},{2,10},{3,11},{4,12},{5,13},{6,14},{7,15},{8,0},{9,1},... | collective-permute-start | bytes 1769480 | tf_op jit(solution)/shard_map/ppermute | solution.py:394
  190.6 15.2 %collective-permute-start.21 = (bf16[2,2,2,96,384]{4,3,2,1,0:T(8,128)(2,1)S(1)}, bf16[2,2,2,96,384]{4,3,2,1,0:T(8,128)(2,1)S(1)}, u32[]{:S(2)}, u32[]{:S(2)}) collective-permute-start(bf16[2,2,2,96,384]{4,3,2,1,0:T(8,128)(2,1)S(1)} %bitcast.205), channel_id=1, source_target_pairs={{0,4},{1,5},{2,6},{3,7},{4,0},{5,1},{6,2},{7,3},{8,12},{9,13},{10,... | collective-permute-start | bytes 1769480 | tf_op jit(solution)/shard_map/ppermute | solution.py:394
  191.1 14.8 %copy-start.21 = (bf16[512,768]{1,0:T(8,128)(2,1)S(1)}, bf16[512,768]{1,0:T(8,128)(2,1)}, u32[]{:S(2)}) copy-start(bf16[512,768]{1,0:T(8,128)(2,1)} %get-tuple-element.378.refs_3_.refs_5_) | copy-start | bytes 2359300
  191.1 14.8 %copy-start.22 = (bf16[512,384]{1,0:T(8,128)(2,1)S(1)}, bf16[512,384]{1,0:T(8,128)(2,1)}, u32[]{:S(2)}) copy-start(bf16[512,384]{1,0:T(8,128)(2,1)} %get-tuple-element.376.refs_1_.refs_0_) | copy-start | bytes 1179652
  191.1 22.9 %collective-permute-start.23 = (bf16[2,2,2,144,384]{4,3,2,1,0:T(8,128)(2,1)S(1)}, bf16[2,2,2,144,384]{4,3,2,1,0:T(8,128)(2,1)S(1)}, u32[]{:S(2)}, u32[]{:S(2)}) collective-permute-start(bf16[2,2,2,144,384]{4,3,2,1,0:T(8,128)(2,1)S(1)} %bitcast.202), channel_id=1, source_target_pairs={{0,1},{1,0},{2,3},{3,2},{4,5},{5,4},{6,7},{7,6},{8,9},{9,8},{10,11... | collective-permute-start | bytes 2654216 | tf_op jit(solution)/shard_map/ppermute | solution.py:394
  205.9 8.2 %collective-permute-start.25 = (bf16[2,512,384]{2,1,0:T(8,128)(2,1)}, bf16[2,512,384]{2,1,0:T(8,128)(2,1)S(1)}, u32[]{:S(2)}, u32[]{:S(2)}) collective-permute-start(bf16[2,512,384]{2,1,0:T(8,128)(2,1)} %get-tuple-element.381), channel_id=1, source_target_pairs={{0,2},{1,3},{2,0},{3,1},{4,6},{5,7},{6,4},{7,5},{8,10},{9,11},{10,... | collective-permute-start | bytes 2359304 | tf_op jit(solution)/shard_map/ppermute | solution.py:105
  207.9 6.1 %collective-permute-start.24 = (bf16[2,8,48,384]{3,2,1,0:T(8,128)(2,1)S(1)}, bf16[2,8,48,384]{3,2,1,0:T(8,128)(2,1)S(1)}, u32[]{:S(2)}, u32[]{:S(2)}) collective-permute-start(bf16[2,8,48,384]{3,2,1,0:T(8,128)(2,1)S(1)} %get-tuple-element.380), channel_id=1, source_target_pairs={{0,2},{2,0},{4,6},{6,4},{8,10},{10,8},{12,14},{14,12},{16,18},{18,... | collective-permute-start | bytes 1769480 | tf_op jit(solution)/shard_map/ppermute | solution.py:383
  217.1 19.0 %collective-permute-start.30 = (bf16[2,8,96,384]{3,2,1,0:T(8,128)(2,1)S(1)}, bf16[2,8,96,384]{3,2,1,0:T(8,128)(2,1)S(1)}, u32[]{:S(2)}, u32[]{:S(2)}) collective-permute-start(bf16[2,8,96,384]{3,2,1,0:T(8,128)(2,1)S(1)} %get-tuple-element.407), channel_id=1, source_target_pairs={{0,2},{2,0},{4,6},{6,4},{8,10},{10,8},{12,14},{14,12},{16,18},{18,... | collective-permute-start | bytes 3538952 | tf_op jit(solution)/shard_map/ppermute | solution.py:383
  217.2 18.9 %collective-permute-start.27 = (bf16[2,2,144,384]{3,2,1,0:T(8,128)(2,1)S(1)}, bf16[2,2,144,384]{3,2,1,0:T(8,128)(2,1)S(1)}, u32[]{:S(2)}, u32[]{:S(2)}) collective-permute-start(bf16[2,2,144,384]{3,2,1,0:T(8,128)(2,1)S(1)} %bitcast.207), channel_id=1, source_target_pairs={{0,4},{1,5},{2,6},{3,7},{4,0},{5,1},{6,2},{7,3},{8,12},{9,13},{10,... | collective-permute-start | bytes 1327112 | tf_op jit(solution)/shard_map/ppermute | solution.py:394
  218.8 17.2 %collective-permute-start.26 = (bf16[384,384]{1,0:T(8,128)(2,1)S(1)}, bf16[384,384]{1,0:T(8,128)(2,1)S(1)}, u32[]{:S(2)}, u32[]{:S(2)}) collective-permute-start(bf16[384,384]{1,0:T(8,128)(2,1)S(1)} %bitcast.213), channel_id=1, source_target_pairs={{0,16},{1,17},{2,18},{3,19},{4,20},{5,21},{6,22},{7,23},{8,24},{9,... | collective-permute-start | bytes 884744 | tf_op jit(solution)/shard_map/ppermute | solution.py:394
  222.4 13.6 %collective-permute-start.28 = (bf16[2,2,96,384]{3,2,1,0:T(8,128)(2,1)S(1)}, bf16[2,2,96,384]{3,2,1,0:T(8,128)(2,1)S(1)}, u32[]{:S(2)}, u32[]{:S(2)}) collective-permute-start(bf16[2,2,96,384]{3,2,1,0:T(8,128)(2,1)S(1)} %bitcast.212), channel_id=1, source_target_pairs={{0,1},{1,0},{2,3},{3,2},{4,5},{5,4},{6,7},{7,6},{8,9},{9,8},{10,11... | collective-permute-start | bytes 884744 | tf_op jit(solution)/shard_map/ppermute | solution.py:394
  223.4 12.7 %collective-permute-start.29 = (bf16[2,2,2,48,384]{4,3,2,1,0:T(8,128)(2,1)S(1)}, bf16[2,2,2,48,384]{4,3,2,1,0:T(8,128)(2,1)S(1)}, u32[]{:S(2)}, u32[]{:S(2)}) collective-permute-start(bf16[2,2,2,48,384]{4,3,2,1,0:T(8,128)(2,1)S(1)} %bitcast.211), channel_id=1, source_target_pairs={{0,4},{1,5},{2,6},{3,7},{4,0},{5,1},{6,2},{7,3},{8,12},{9,13},{10,... | collective-permute-start | bytes 884744 | tf_op jit(solution)/shard_map/ppermute | solution.py:394
  237.2 16.2 %collective-permute-start.36 = (bf16[2,240,384]{2,1,0:T(8,128)(2,1)S(1)}, bf16[2,240,384]{2,1,0:T(8,128)(2,1)S(1)}, u32[]{:S(2)}, u32[]{:S(2)}) collective-permute-start(bf16[2,240,384]{2,1,0:T(8,128)(2,1)S(1)} %bitcast.208), channel_id=1, source_target_pairs={{0,8},{1,9},{2,10},{3,11},{4,12},{5,13},{6,14},{7,15},{8,0},{9,1},... | collective-permute-start | bytes 1105928 | tf_op jit(solution)/shard_map/ppermute | solution.py:394
  238.6 3.7 %collective-permute-start.37 = (f32[16,768]{1,0:T(8,128)S(1)}, f32[16,768]{1,0:T(8,128)S(1)}, u32[]{:S(2)}, u32[]{:S(2)}) collective-permute-start(f32[16,768]{1,0:T(8,128)S(1)} %get-tuple-element.433), channel_id=1, source_target_pairs={{0,2},{1,3},{2,0},{3,1},{4,6},{5,7},{6,4},{7,5},{8,10},{9,11},{10,... | collective-permute-start | bytes 147464 | tf_op jit(solution)/shard_map/ppermute | solution.py:394
  238.6 14.8 %collective-permute-start.33 = (bf16[2,2,2,48,384]{4,3,2,1,0:T(8,128)(2,1)S(1)}, bf16[2,2,2,48,384]{4,3,2,1,0:T(8,128)(2,1)S(1)}, u32[]{:S(2)}, u32[]{:S(2)}) collective-permute-start(bf16[2,2,2,48,384]{4,3,2,1,0:T(8,128)(2,1)S(1)} %bitcast.210), channel_id=1, source_target_pairs={{0,4},{1,5},{2,6},{3,7},{4,0},{5,1},{6,2},{7,3},{8,12},{9,13},{10,... | collective-permute-start | bytes 884744 | tf_op jit(solution)/shard_map/ppermute | solution.py:394
  240.3 13.2 %collective-permute-start.34 = (bf16[2,2,2,48,384]{4,3,2,1,0:T(8,128)(2,1)S(1)}, bf16[2,2,2,48,384]{4,3,2,1,0:T(8,128)(2,1)S(1)}, u32[]{:S(2)}, u32[]{:S(2)}) collective-permute-start(bf16[2,2,2,48,384]{4,3,2,1,0:T(8,128)(2,1)S(1)} %bitcast.209), channel_id=1, source_target_pairs={{0,1},{1,0},{2,3},{3,2},{4,5},{5,4},{6,7},{7,6},{8,9},{9,8},{10,11... | collective-permute-start | bytes 884744 | tf_op jit(solution)/shard_map/ppermute | solution.py:394
  241.2 11.4 %collective-permute-start.35 = (bf16[2,2,48,384]{3,2,1,0:T(8,128)(2,1)S(1)}, bf16[2,2,48,384]{3,2,1,0:T(8,128)(2,1)S(1)}, u32[]{:S(2)}, u32[]{:S(2)}) collective-permute-start(bf16[2,2,48,384]{3,2,1,0:T(8,128)(2,1)S(1)} %bitcast.216), channel_id=1, source_target_pairs={{0,1},{1,0},{2,3},{3,2},{4,5},{5,4},{6,7},{7,6},{8,9},{9,8},{10,11... | collective-permute-start | bytes 442376 | tf_op jit(solution)/shard_map/ppermute | solution.py:394
  242.3 6.5 %collective-permute-start.38 = (f32[16,768]{1,0:T(8,128)S(1)}, f32[16,768]{1,0:T(8,128)S(1)}, u32[]{:S(2)}, u32[]{:S(2)}) collective-permute-start(f32[16,768]{1,0:T(8,128)S(1)} %add.79), channel_id=1, source_target_pairs={{0,8},{1,9},{2,10},{3,11},{4,12},{5,13},{6,14},{7,15},{8,0},{9,1},... | collective-permute-start | bytes 147464 | tf_op jit(solution)/shard_map/ppermute | solution.py:394
  248.8 33.3 %collective-permute-start.31 = (bf16[256,768]{1,0:T(8,128)(2,1)S(1)}, bf16[256,768]{1,0:T(8,128)(2,1)S(1)}, u32[]{:S(2)}, u32[]{:S(2)}) collective-permute-start(bf16[256,768]{1,0:T(8,128)(2,1)S(1)} %get-tuple-element.519), channel_id=1, source_target_pairs={{0,0},{2,1},{1,2},{3,3},{4,4},{6,5},{5,6},{7,7},{8,8},{10,9},{9,10... | collective-permute-start | bytes 1179656 | tf_op jit(solution)/shard_map/ppermute | solution.py:90
  252.6 29.6 %collective-permute-start.32 = (bf16[256,768]{1,0:T(8,128)(2,1)S(1)}, bf16[256,768]{1,0:T(8,128)(2,1)S(1)}, u32[]{:S(2)}, u32[]{:S(2)}) collective-permute-start(bf16[256,768]{1,0:T(8,128)(2,1)S(1)} %get-tuple-element.520), channel_id=1, source_target_pairs={{2,0},{0,1},{3,2},{1,3},{6,4},{4,5},{7,6},{5,7},{10,8},{8,9},{11,1... | collective-permute-start | bytes 1179656 | tf_op jit(solution)/shard_map/ppermute | solution.py:91
  254.2 11.4 %collective-permute-start.39 = (bf16[2,2,48,384]{3,2,1,0:T(8,128)(2,1)S(1)}, bf16[2,2,48,384]{3,2,1,0:T(8,128)(2,1)S(1)}, u32[]{:S(2)}, u32[]{:S(2)}) collective-permute-start(bf16[2,2,48,384]{3,2,1,0:T(8,128)(2,1)S(1)} %bitcast.218), channel_id=1, source_target_pairs={{0,1},{1,0},{2,3},{3,2},{4,5},{5,4},{6,7},{7,6},{8,9},{9,8},{10,11... | collective-permute-start | bytes 442376 | tf_op jit(solution)/shard_map/ppermute | solution.py:394
  254.3 11.3 %collective-permute-start.40 = (bf16[2,2,48,384]{3,2,1,0:T(8,128)(2,1)S(1)}, bf16[2,2,48,384]{3,2,1,0:T(8,128)(2,1)S(1)}, u32[]{:S(2)}, u32[]{:S(2)}) collective-permute-start(bf16[2,2,48,384]{3,2,1,0:T(8,128)(2,1)S(1)} %bitcast.217), channel_id=1, source_target_pairs={{0,4},{1,5},{2,6},{3,7},{4,0},{5,1},{6,2},{7,3},{8,12},{9,13},{10,... | collective-permute-start | bytes 442376 | tf_op jit(solution)/shard_map/ppermute | solution.py:394
  256.0 9.6 %collective-permute-start.41 = (f32[16,768]{1,0:T(8,128)S(1)}, f32[16,768]{1,0:T(8,128)S(1)}, u32[]{:S(2)}, u32[]{:S(2)}) collective-permute-start(f32[16,768]{1,0:T(8,128)S(1)} %add.80), channel_id=1, source_target_pairs={{0,1},{1,0},{2,3},{3,2},{4,5},{5,4},{6,7},{7,6},{8,9},{9,8},{10,11... | collective-permute-start | bytes 147464 | tf_op jit(solution)/shard_map/ppermute | solution.py:394
  266.3 22.1 %copy-start.39 = (f32[32,512]{1,0:T(8,128)S(1)}, f32[32,512]{1,0:T(8,128)}, u32[]{:S(2)}) copy-start(f32[32,512]{1,0:T(8,128)} %constant.96.clone.refs_7_) | copy-start | bytes 196612
  266.3 12.2 %collective-permute-start.43 = (bf16[2,144,384]{2,1,0:T(8,128)(2,1)S(1)}, bf16[2,144,384]{2,1,0:T(8,128)(2,1)S(1)}, u32[]{:S(2)}, u32[]{:S(2)}) collective-permute-start(bf16[2,144,384]{2,1,0:T(8,128)(2,1)S(1)} %bitcast.214), channel_id=1, source_target_pairs={{0,8},{1,9},{2,10},{3,11},{4,12},{5,13},{6,14},{7,15},{8,0},{9,1},... | collective-permute-start | bytes 663560 | tf_op jit(solution)/shard_map/ppermute | solution.py:394
  267.9 16.2 %collective-permute-start.42 = (bf16[240,384]{1,0:T(8,128)(2,1)S(1)}, bf16[240,384]{1,0:T(8,128)(2,1)S(1)}, u32[]{:S(2)}, u32[]{:S(2)}) collective-permute-start(bf16[240,384]{1,0:T(8,128)(2,1)S(1)} %bitcast.215), channel_id=1, source_target_pairs={{0,16},{1,17},{2,18},{3,19},{4,20},{5,21},{6,22},{7,23},{8,24},{9,... | collective-permute-start | bytes 552968 | tf_op jit(solution)/shard_map/ppermute | solution.py:394
  270.5 4.1 %collective-permute-start.44 = (f32[16,768]{1,0:T(8,128)S(1)}, f32[16,768]{1,0:T(8,128)S(1)}, u32[]{:S(2)}, u32[]{:S(2)}) collective-permute-start(f32[16,768]{1,0:T(8,128)S(1)} %add.81), channel_id=1, source_target_pairs={{0,4},{1,5},{2,6},{3,7},{4,0},{5,1},{6,2},{7,3},{8,12},{9,13},{10,... | collective-permute-start | bytes 147464 | tf_op jit(solution)/shard_map/ppermute | solution.py:394
  278.6 5.5 %collective-permute-start.46 = (f32[16,768]{1,0:T(8,128)S(1)}, f32[16,768]{1,0:T(8,128)S(1)}, u32[]{:S(2)}, u32[]{:S(2)}) collective-permute-start(f32[16,768]{1,0:T(8,128)S(1)} %add.82), channel_id=1, source_target_pairs={{0,16},{1,17},{2,18},{3,19},{4,20},{5,21},{6,22},{7,23},{8,24},{9,... | collective-permute-start | bytes 147464 | tf_op jit(solution)/shard_map/ppermute | solution.py:394
  279.2 9.3 %collective-permute-start.45 = (bf16[144,384]{1,0:T(8,128)(2,1)S(1)}, bf16[144,384]{1,0:T(8,128)(2,1)S(1)}, u32[]{:S(2)}, u32[]{:S(2)}) collective-permute-start(bf16[144,384]{1,0:T(8,128)(2,1)S(1)} %bitcast.219), channel_id=1, source_target_pairs={{0,16},{1,17},{2,18},{3,19},{4,20},{5,21},{6,22},{7,23},{8,24},{9,... | collective-permute-start | bytes 331784 | tf_op jit(solution)/shard_map/ppermute | solution.py:394
  (35 other events, 188.1 us)

commit v2 on v1

--- a/solution.py
+++ b/solution.py
@@ -291,7 +291,8 @@
         parts = [ref[...].astype(F32) for ref in refs[at : at + count]]
         totals.append(sum(parts[1:], parts[0]))
         at += count
-    ffn, rest, own = totals
+    first, second, rest, own = totals
+    ffn = jnp.concatenate([first, second], axis=0)
     small, hot = refs[at][...], refs[at + 1][...]
     refs = refs[at + 2 :]
     gains, table_ref, fo_ref, fi_ref, squares = refs[:3], refs[3], refs[4], refs[5], refs[6:]
@@ -321,10 +322,10 @@
     hot = jnp.asarray(bucket_hot(block))
     square = ((width // dp_size, width // mem_size), F32, None)
     return run(
-        functools.partial(write_kernel, ([1 + len(s.came) for s in (ffn, rest, own)], hidden // width)),
+        functools.partial(write_kernel, ([1 + len(s.came) for s in (*ffn, rest, own)], hidden // width)),
         "write_grads",
         (1,),
-        [(v.reshape(v.shape[-2:]), None) for s in (ffn, rest, own) for v in (s.keep, *s.came)]
+        [(v.reshape(v.shape[-2:]), None) for s in (*ffn, rest, own) for v in (s.keep, *s.came)]
         + [(v, None) for v in (small, hot)],
         [((1, width), F32, None)] * 3
         + [
@@ -561,15 +562,11 @@
         self.keep, self.came = keep.reshape(shape), [swap(send, "dp", 0).reshape(shape)]
         self.span = (0, shape[-2])
 
-    def parts(self, *orders):
-        size = self.span[1] // len(orders)
-        shares = []
-        for i, order in enumerate(orders):
-            share = copy.copy(self)
-            share.names, share.span = list(self.names), (i * size, size)
-            share.order = [(name,) for name in bit_order(order)]
-            shares.append(share)
-        return shares
+    def part(self, start, size, order):
+        share = copy.copy(self)
+        share.names, share.span = list(self.names), (self.span[0] + start, size)
+        share.order = [(name,) for name in bit_order(order)]
+        return share
 
 
 def all_bits():
@@ -1682,7 +1679,11 @@
         [ffn_a, ffn_b], layer_out, cross_q0, cross_own0, cross_other0, cross_mixed_grad
     )
 
-    advance(bits, ffn_a, ffn_b)
+    third = (ffn_a.span[1] + ffn_b.span[1]) // 3
+    left = ffn_a.span[1] - third
+    ffn_mid = (ffn_a.part(third, left, "yxz"), ffn_b.part(0, third - left, "yxz"))
+    ffn_a, ffn_b, ffn_c = ffn_a.part(0, third, "xyz"), ffn_mid[0], ffn_b.part(third - left, third, "zxy")
+    advance(bits, ffn_a, ffn_mid, ffn_c)
     came0 = came_parts(cross_other0, rows)
     cross_q1, cross_own1, cross_other1 = cross_half(first, rest, cross_mixed_grad)
     came0, cross_q1, cross_own1, cross_other1 = fence([], came0, cross_q1, cross_own1, cross_other1)
@@ -1702,7 +1703,7 @@
         self_out,
     )
     came1, hidden_one_grad, self_mixed_grad, grads = fence(
-        [ffn_a, ffn_b], came1, hidden_one_grad, self_mixed_grad, grads
+        [ffn_a, ffn_b, ffn_c], came1, hidden_one_grad, self_mixed_grad, grads
     )
 
     advance(bits, ffn_a, ffn_b)
@@ -1726,22 +1727,22 @@
     )
 
     level(ffn_a, ffn_b, bits=bits)
-    advance(bits, (ffn_a, ffn_b), rest_a, rest_b)
+    advance(bits, (ffn_a, ffn_b), ffn_c, rest_a, rest_b)
     came0 = came_parts(self_other0, rows)
     self_q1, self_own1, self_other1, table_grad1 = self_half(first, rest, self_mixed_grad)
     came0, self_q1, self_own1, self_other1, table_grad1 = fence(
-        [ffn_a, rest_b], came0, self_q1, self_own1, self_other1, table_grad1
+        [ffn_a, ffn_c, rest_b], came0, self_q1, self_own1, self_other1, table_grad1
     )
 
     came1 = came_parts(self_other1, rows)
     query_grads = query_grad(mine, (self_q0, self_q1), self_in)
     (query_grads,) = fence([], query_grads)
 
-    own_q = Scatter(query_grads, "yxz")
+    own_q = Scatter(query_grads, "xyz")
     small = table_sums(table_grad0, table_grad1, cross_gain_grad, ffn_gain_grad)
     came1, small = fence([ffn_a, rest_a, rest_b, own_q], came1, small)
 
-    advance(bits, ffn_a, rest_a, rest_b, own_q)
+    advance(bits, ffn_a, ffn_c, rest_a, rest_b, own_q)
     sums, grads = key_grads(mine, (self_own0, self_own1), (came0, came1), self_in, after=[rest_a.keep])
     sums, grads = fence([], sums, grads)
 
@@ -1757,9 +1758,9 @@
         self_value,
         small,
     )
-    decoder_in_grad, small = fence([ffn_a, rest_a, rest_b, own_q, own], decoder_in_grad, small)
-
-    small_bits = [("dp", 0), ("dp", 2), ("mem", 0), ("dp", 1), ("dp", 3)]
+    decoder_in_grad, small = fence([ffn_a, ffn_c, rest_a, rest_b, own_q, own], decoder_in_grad, small)
+
+    small_bits = [("dp", 0), ("dp", 2), ("dp", 1), ("mem", 0), ("dp", 3)]
     small_bits = [name for name in small_bits if name in all_bits()]
     small_bits += [name for name in all_bits() if name not in small_bits]
 
@@ -1768,12 +1769,13 @@
             small = small + swap_many(small, (small_bits.pop(0),))
         return small
 
-    own_k, own_v = own.parts("yxz", "xyz")
+    half = own.span[1] // 2
+    own_k, own_v = own.part(0, half, "yxz"), own.part(half, half, "xyz")
     level(rest_a, rest_b, bits=bits)
     advance(bits, own_k, own_v, own_q, (rest_a, rest_b))
     (small,) = fence([own_k, own_v, own_q, rest_a], add_small(small, 2))
 
-    advance(bits, own_k, own_v)
+    advance(bits, own_k, own_v, ffn_c)
     decoder_in_grad = from_rows(decoder_in_grad, odd)
     (small,) = fence([own_k, own_v], add_small(small))
 
@@ -1781,12 +1783,12 @@
     advance(bits, (own_k, own_v, own_q), rest_a)
     (small,) = fence([own_k], add_small(small))
     small = add_small(small, len(small_bits))
-    for scatter in (own_k, ffn_a, rest_a):
+    for scatter in (own_k, ffn_a, ffn_c, rest_a):
         while scatter.order:
             advance(bits, scatter)
     parts = small
     self_gain_sum, cross_gain_sum, ffn_gain_sum, table_sum, grad_fo, grad_fi, *squares = write_grads(
-        ffn_a, rest_a, own_k, parts, small_block(rows // 2), width, ffn_in.shape[1]
+        (ffn_a, ffn_c), rest_a, own_k, parts, small_block(rows // 2), width, ffn_in.shape[1]
     )
     self_gain_sum, cross_gain_sum, ffn_gain_sum = self_gain_sum[0], cross_gain_sum[0], ffn_gain_sum[0]
     grad_co, grad_cq, grad_so, grad_ck, grad_cv, grad_sk, grad_sv, grad_sq = squares

time: 296 us -> 301 us (1.017)
  Pallas kernels: 163 us -> 172 us
  waiting for transfers between devices: 48.8 us -> 43.3 us
    pallas_call x26, Pallas kernels: 155 us -> 164 us  [run(): pl.pallas_call(body, grid_spec=pltpu.PrefetchScalarGridSpec(num_scalar_pr...]
    ppermute x3, waiting for transfers between devices: 4.85 us -> 0.01 us  [from_rows(): second = lax.ppermute(second, ('dp', 'mem'), back[1])]
    unnamed x105 -> x131, local copies, waits for them, and re-layouts: 6.64 us -> 7.42 us
    ppermute x25 -> x29, waiting for transfers between devices: 43.9 us -> 43.3 us  [swap_many(): return lax.ppermute(values, ('dp', 'mem'), moves)]
    ppermute x25 -> x29, starting transfers between devices: 33.6 us -> 33.8 us  [swap_many(): return lax.ppermute(values, ('dp', 'mem'), moves)]
  transfers between devices with their start and end apart: 47 -> 51, of which waited for: 12 -> 12; matrix products, arithmetic and copies ran while one was open for 2% -> 2% of each run, Pallas kernels for 39% -> 41%
where the time goes in v2:
time: 301 us; the launch traced here: 297 us
  Pallas kernels  172 us (57%)
  starting transfers between devices  60.1 us (20%)
  waiting for transfers between devices  43.3 us (14%)
  other arithmetic  10.3 us (3%)
  local copies, waits for them, and re-layouts  9.37 us (3%)
    pallas_call x26, Pallas kernels, run(): pl.pallas_call(body, grid_spec=pltpu.PrefetchScalarGridSpec(num_scalar_pr...  164 us
    ppermute x29, waiting for transfers between devices, swap_many(): return lax.ppermute(values, ('dp', 'mem'), moves)  43.3 us
    ppermute x29, starting transfers between devices, swap_many(): return lax.ppermute(values, ('dp', 'mem'), moves)  33.8 us
    ppermute x4, starting transfers between devices, to_rows(): lax.ppermute(piece, ('dp', 'mem'), move)  9.1 us
    unnamed x131, local copies, waits for them, and re-layouts  7.42 us
    pallas_call x1, Pallas kernels, bias_tables(): pl.pallas_call(table_kernel, grid=(HEADS // heads,), in_specs=[spec, spec...  7.29 us
    ppermute x3, starting transfers between devices, from_rows(): second = lax.ppermute(second, ('dp', 'mem'), back[1])  6.99 us
  transfers between devices with their start and end apart: 51, of which 12 were waited for; matrix products, arithmetic and copies ran while one was open for 2% of the time, Pallas kernels for 41%

profile of v2, /device:TPU:0, one launch (start us, length us, event | category | flops | bytes accessed | tf_op | source)
XLA Modules:
  0.0 297.3 jit_solution(12203328691245275523)
XLA Ops:
  0.8 1.2 select_convert_fusion
  2.0 1.2 pad_maximum_fusion.5
  5.2 7.3 %bias_tables.1 = (f32[12,4,128,128]{3,2,1,0:T(8,128)}, f32[12,4,128,128]{3,2,1,0:T(8,128)}) custom-call(f32[12,2,1,256]{3,2,1,0:T(1,128)S(1)} %copy.55.base_ref, f32[12,2,1,256]{3,2,1,0:T(1,128)S(1)} %broadcast_in_dim.115.base_t_ref), custom_call_target="tpu_custom_call" | custom-call | tf_op jit(solution)/shard_map/bias_tables/pallas_call | solution.py:183
  12.9 4.7 %collective-permute-start.4 = (bf16[512,896]{1,0:T(8,128)(2,1)S(1)}, bf16[512,896]{1,0:T(8,128)(2,1)}, u32[]{:S(2)}, u32[]{:S(2)}) collective-permute-start(bf16[512,896]{1,0:T(8,128)(2,1)S(1)} %pad_maximum_fusion.1.refs_0_.refs_7_.refs_3_), channel_id=1, source_target_pairs={{0,2},{1,3},{2,0},{3,1},{4,6},{5,7},{6,4},{7,5},{8,10},{9,11},{10,... | collective-permute-start | bytes 2752520 | tf_op jit(solution)/shard_map/ppermute | solution.py:105
  17.6 1.3 fusion.15
  18.9 7.9 %collective-permute-start.2 = (bf16[2,256,768]{2,1,0:T(8,128)(2,1)}, bf16[2,256,768]{2,1,0:T(8,128)(2,1)}, u32[]{:S(2)}, u32[]{:S(2)}) collective-permute-start(bf16[2,256,768]{2,1,0:T(8,128)(2,1)} %get-tuple-element.542), channel_id=1, source_target_pairs={{0,0},{1,2},{2,1},{3,3},{4,4},{5,6},{6,5},{7,7},{8,8},{9,10},{10,9... | collective-permute-start | bytes 2359304 | tf_op jit(solution)/shard_map/ppermute | solution.py:74
  27.5 1.3 copy-done.13
  28.8 4.6 %own_project.1 = (bf16[512,768]{1,0:T(8,128)(2,1)}, bf16[512,768]{1,0:T(8,128)(2,1)}, bf16[1024,768]{1,0:T(8,128)(2,1)}, bf16[1024,768]{1,0:T(8,128)(2,1)}, bf16...) custom-call(bf16[512,896]{1,0:T(8,128)(2,1)S(1)} %pad_maximum_fusion, ...), custom_call_target="tpu_custom_call" | custom-call | flops 113246208 | bytes 614656 | tf_op jit(solution)/shard_map/own_project/pallas_call | solution.py:475
  33.4 4.3 %other_project.1 = (bf16[1024,768]{1,0:T(8,128)(2,1)}, bf16[1024,768]{1,0:T(8,128)(2,1)}, bf16[1024,128]{1,0:T(8,128)(2,1)}, bf16[1024,128]{1,0:T(8,128)(2,1)}, f32[1,128]{1,0:T(1,128)S(1)}) custom-call(bf16[512,896]{1,0:T(8,128)(2,1)} %collective-permute-done.4.refs_0_, ...), custom_call_target="tpu_custom_call", output_to_operand_aliasing={{0}: (4, {}), {1}: (5, {}), {2}: (6, {}), {3}: (7, {})} | custom-call | flops 75497472 | bytes 663776 | tf_op jit(solution)/shard_map/other_project/pallas_call | solution.py:475
  37.7 14.1 %self_forward.1 = (bf16[512,768]{1,0:T(8,128)(2,1)}, bf16[12,512,128]{2,1,0:T(8,128)(2,1)}, f32[512,768]{1,0:T(8,128)S(1)}, bf16[512,768]{1,0:T(8,128)(2,1)S(1)}...) custom-call(s32[4,5]{1,0:T(4,128)S(1)} %pad_add_fusion.refs_0_, bf16[512,768]{1,0:T(8,128)(2,1)} %get-tuple-element.265.refs_1_, ...), custom_call_target="tpu_custom_call" | custom-call | flops 251658240 | bytes 1016128 | tf_op jit(solution)/shard_map/self_forward/pallas_call | solution.py:475
  51.8 2.6 broadcast_select_fusion
  56.1 3.3 %encoder_project.2 = (bf16[1024,768]{1,0:T(8,128)(2,1)}, bf16[1024,768]{1,0:T(8,128)(2,1)}, f32[1,128]{1,0:T(1,128)S(1)}) custom-call(bf16[512,768]{1,0:T(8,128)(2,1)S(1)} %get-tuple-element.538.refs_0_.refs_5_, bf16[768,768]{1,0:T(8,128)(2,1)S(1)} %copy-done.3, bf16[768,768]{1,0:T(8,128)(2,1)S(1)} %copy-done.5), custom_call_target="tpu_custom_call" | custom-call | flops 75497472 | bytes 393248 | tf_op jit(solution)/shard_map/encoder_project/pallas_call | solution.py:475
  59.4 3.3 %encoder_project.3 = (bf16[1024,768]{1,0:T(8,128)(2,1)}, bf16[1024,768]{1,0:T(8,128)(2,1)}, f32[1,128]{1,0:T(1,128)S(1)}) custom-call(bf16[512,768]{1,0:T(8,128)(2,1)S(1)} %collective-permute-done.5.refs_0_, bf16[768,768]{1,0:T(8,128)(2,1)S(1)} %copy-done.3, bf16[768,768]{1,0:T(8,128)(2,1)S(1)} %copy-done.5, ...), custom_call_target="tpu_custom_call", output_to_operand_aliasing={{0}: (3, {}), {1}: (4, {})} | custom-call | flops 75497472 | bytes 589856 | tf_op jit(solution)/shard_map/encoder_project/pallas_call | solution.py:475
  62.7 14.2 %cross_forward.1 = (bf16[512,768]{1,0:T(8,128)(2,1)}, bf16[12,512,128]{2,1,0:T(8,128)(2,1)}, f32[512,768]{1,0:T(8,128)S(1)}, bf16[512,768]{1,0:T(8,128)(2,1)S(1)}) custom-call(bf16[512,768]{1,0:T(8,128)(2,1)} %copy-done.8, bf16[1024,768]{1,0:T(8,128)(2,1)} %get-tuple-element.292.refs_1_, bf16[1024,768]{1,0:T(8,128)(2,1)} %get-tuple-element.293.refs_2_, ...), custom_call_target="tpu_custom_call" | custom-call | flops 402653184 | bytes 737568 | tf_op jit(solution)/shard_map/cross_forward/pallas_call | solution.py:475
  76.9 25.8 %feed_forward.1 = (bf16[512,768]{1,0:T(8,128)(2,1)S(1)}, f32[512,768]{1,0:T(8,128)S(1)}, bf16[512,768]{1,0:T(8,128)(2,1)S(1)}, bf16[512,768]{1,0:T(8,128)(2,1)S(...) custom-call(s32[1]{0:T(128)} %bitcast.refs_0_, ...), custom_call_target="tpu_custom_call" | custom-call | flops 905969664 | bytes 1696128 | tf_op jit(solution)/shard_map/feed_forward/pallas_call | solution.py:475
  104.1 2.9 collective-permute-start.9
  107.0 11.3 %cross_backward.2 = (bf16[512,384]{1,0:T(8,128)(2,1)}, bf16[2,512,384]{2,1,0:T(8,128)(2,1)}, bf16[2,512,384]{2,1,0:T(8,128)(2,1)}) custom-call(bf16[512,768]{1,0:T(8,128)(2,1)} %copy-done.8, bf16[1024,768]{1,0:T(8,128)(2,1)} %get-tuple-element.292.refs_1_, bf16[1024,768]{1,0:T(8,128)(2,1)} %get-tuple-element.293.refs_2_, ...), custom_call_target="tpu_custom_call" | custom-call | flops 503316480 | bytes 581632 | tf_op jit(solution)/shard_map/cross_backward/pallas_call | solution.py:475
  118.4 0.9 pad_maximum_fusion.3
  119.4 10.4 %advance.8 = (bf16[1,1,8,128,384]{4,3,2,1,0:T(8,128)(2,1)}, bf16[1,1,8,128,384]{4,3,2,1,0:T(8,128)(2,1)}, bf16[8,1,1,128,384]{4,3,2,1,0:T(8,128)(2,1)}, bf16[8,1...) custom-call(s32[5]{0:T(128)S(1)} %stack.153.refs_0_, ...), custom_call_target="tpu_custom_call" | custom-call | flops 1179648 | bytes 1474560 | tf_op jit(solution)/shard_map/advance/pallas_call | solution.py:475
  130.1 2.5 collective-permute-start.11
  132.7 1.0 collective-permute-start.12
  133.7 11.4 %cross_backward.3 = (bf16[512,384]{1,0:T(8,128)(2,1)}, bf16[2,512,384]{2,1,0:T(8,128)(2,1)}, bf16[2,512,384]{2,1,0:T(8,128)(2,1)}) custom-call(bf16[512,768]{1,0:T(8,128)(2,1)} %copy-done.8, bf16[1024,768]{1,0:T(8,128)(2,1)} %get-tuple-element.292.refs_1_, bf16[1024,768]{1,0:T(8,128)(2,1)} %get-tuple-element.293.refs_2_, ...), custom_call_target="tpu_custom_call" | custom-call | flops 503316480 | bytes 581632 | tf_op jit(solution)/shard_map/cross_backward/pallas_call | solution.py:475
  145.3 1.0 copy-done.44
  146.3 5.7 %cross_finish.1 = (f32[512,768]{1,0:T(8,128)}, bf16[512,768]{1,0:T(8,128)(2,1)S(1)}, f32[1,768]{1,0:T(1,128)S(1)}, bf16[2,8,144,384]{3,2,1,0:T(8,128)(2,1)S(1)}, bf16[2,8,144,384]{3,2,1,0:T(8,128)(2,1)S(1)}) custom-call(s32[1]{0:T(128)} %bitcast.refs_0_, bf16[512,384]{1,0:T(8,128)(2,1)S(1)} %copy-done.42, bf16[512,384]{1,0:T(8,128)(2,1)S(1)} %copy-done.44, ...), custom_call_target="tpu_custom_call" | custom-call | flops 188743680 | bytes 958848 | tf_op jit(solution)/shard_map/cross_finish/pallas_call | solution.py:475
  155.1 4.1 %encoder_finish.1 = (bf16[512,768]{1,0:T(8,128)(2,1)S(1)}, bf16[2,8,96,384]{3,2,1,0:T(8,128)(2,1)S(1)}, bf16[2,8,96,384]{3,2,1,0:T(8,128)(2,1)S(1)}) custom-call(s32[1]{0:T(128)} %bitcast.refs_0_, bf16[2,512,384]{2,1,0:T(8,128)(2,1)S(1)} %copy-done.36, bf16[2,512,384]{2,1,0:T(8,128)(2,1)S(1)} %copy-done.39, ...), custom_call_target="tpu_custom_call" | custom-call | flops 150994944 | bytes 589824 | tf_op jit(solution)/shard_map/encoder_finish/pallas_call | solution.py:475
  160.5 2.9 collective-permute-start.20
  163.7 13.0 %self_backward.2 = (bf16[512,384]{1,0:T(8,128)(2,1)}, bf16[2,512,384]{2,1,0:T(8,128)(2,1)}, bf16[2,512,384]{2,1,0:T(8,128)(2,1)}, f32[6,4,128,128]{3,2,1,0:T(8,128)}) custom-call(s32[4,5]{1,0:T(4,128)S(1)} %pad_add_fusion.refs_0_, bf16[512,768]{1,0:T(8,128)(2,1)} %get-tuple-element.265.refs_1_, bf16[1024,768]{1,0:T(8,128)(2,1)} %get-tuple-element.275.refs_2_, ...), custom_call_target="tpu_custom_call" | custom-call | flops 314572800 | bytes 876544 | tf_op jit(solution)/shard_map/self_backward/pallas_call | solution.py:475
  177.7 3.1 %collective-permute-done.16 = bf16[2,2,128,384]{3,2,1,0:T(8,128)(2,1)S(1)} collective-permute-done((bf16[2,2,128,384]{3,2,1,0:T(8,128)(2,1)S(1)}, bf16[2,2,128,384]{3,2,1,0:T(8,128)(2,1)S(1)}, u32[]{:S(2)}, u32[]{:S(2)}) %collective-permute-start.16) | collective-permute-done | bytes 393248 | tf_op jit(solution)/shard_map/ppermute | solution.py:395
  181.9 6.1 %advance.10 = (bf16[2,1,1,256,384]{4,3,2,1,0:T(8,128)(2,1)}, bf16[2,1,1,256,384]{4,3,2,1,0:T(8,128)(2,1)}, bf16[2,1,2,128,384]{4,3,2,1,0:T(8,128)(2,1)}, bf16[2,...) custom-call(s32[5]{0:T(128)S(1)} %stack.153.refs_0_, ...), custom_call_target="tpu_custom_call" | custom-call | flops 565248 | bytes 847872 | tf_op jit(solution)/shard_map/advance/pallas_call | solution.py:475
  188.2 1.7 collective-permute-start.21
  189.9 2.6 collective-permute-start.22
  192.5 1.6 collective-permute-start.25
  194.1 12.8 %self_backward.3 = (bf16[512,384]{1,0:T(8,128)(2,1)}, bf16[2,512,384]{2,1,0:T(8,128)(2,1)}, bf16[2,512,384]{2,1,0:T(8,128)(2,1)}, f32[6,4,128,128]{3,2,1,0:T(8,128)}) custom-call(s32[4,5]{1,0:T(4,128)S(1)} %pad_add_fusion.refs_0_, bf16[512,768]{1,0:T(8,128)(2,1)} %get-tuple-element.265.refs_1_, bf16[1024,768]{1,0:T(8,128)(2,1)} %get-tuple-element.275.refs_2_, ...), custom_call_target="tpu_custom_call" | custom-call | flops 314572800 | bytes 876544 | tf_op jit(solution)/shard_map/self_backward/pallas_call | solution.py:475
  206.8 1.8 collective-permute-done.21
  208.8 1.0 copy-done.24
  209.7 0.9 query_grad.1
  211.3 5.7 %table_sums.1.refs_9_ = f32[16,768]{1,0:T(8,128)S(1)} custom-call(f32[6,4,128,128]{3,2,1,0:T(8,128)} %get-tuple-element.402.refs_0_, f32[6,4,128,128]{3,2,1,0:T(8,128)} %get-tuple-element.403.refs_1_, f32[1,768]{1,0:T(1,128)S(1)} %get-tuple-element.404.refs_2_, f32[1,768]{1,0:T(1,128)S(1)} %get-tuple-element.405.refs_3_), custom_call_target="tpu_custom_call" | custom-call | bytes 200064 | tf_op jit(solution)/shard_map/table_sums/pallas_call | solution.py:475
  217.1 1.2 advance.11
  218.4 1.7 key_grads.1
  220.2 1.7 collective-permute-start.30
  221.9 2.1 collective-permute-start.28
  224.4 1.7 collective-permute-start.32
  226.0 8.0 %collective-permute-done.28.refs_1_ = bf16[256,384]{1,0:T(8,128)(2,1)S(1)} collective-permute-done((bf16[256,384]{1,0:T(8,128)(2,1)S(1)}, bf16[256,384]{1,0:T(8,128)(2,1)S(1)}, u32[]{:S(2)}, u32[]{:S(2)}) %collective-permute-start.28) | collective-permute-done | bytes 196640 | tf_op jit(solution)/shard_map/ppermute | solution.py:395
  234.9 5.1 %self_finish_back.1 = (bf16[512,768]{1,0:T(8,128)(2,1)}, f32[16,768]{1,0:T(8,128)S(1)}) custom-call(bf16[512,384]{1,0:T(8,128)(2,1)} %get-tuple-element.396.refs_1_.refs_0_, bf16[512,384]{1,0:T(8,128)(2,1)} %get-tuple-element.397.refs_2_.refs_1_, bf16[2,512,768]{2,1,0:T(8,128)(2,1)S(1)} %get-tuple-element.432.refs_2_, bf16[512,896]{1,0:T(8,128)(2,1)} %copy-done, ...), custom_call_target="tpu_custom_call" | custom-call | flops 113246208 | bytes 579776 | tf_op jit(solution)/shard_map/self_finish_back/pallas_call | solution.py:475
  240.0 3.4 %collective-permute-done.29 = bf16[2,128,384]{2,1,0:T(8,128)(2,1)S(1)} collective-permute-done((bf16[2,128,384]{2,1,0:T(8,128)(2,1)S(1)}, bf16[2,128,384]{2,1,0:T(8,128)(2,1)S(1)}, u32[]{:S(2)}, u32[]{:S(2)}) %collective-permute-start.29) | collective-permute-done | bytes 196640 | tf_op jit(solution)/shard_map/ppermute | solution.py:395
  243.4 1.1 advance.12
  244.5 3.4 %collective-permute-start.39 = (bf16[2,240,384]{2,1,0:T(8,128)(2,1)S(1)}, bf16[2,240,384]{2,1,0:T(8,128)(2,1)S(1)}, u32[]{:S(2)}, u32[]{:S(2)}) collective-permute-start(bf16[2,240,384]{2,1,0:T(8,128)(2,1)S(1)} %bitcast.224), channel_id=1, source_target_pairs={{0,8},{1,9},{2,10},{3,11},{4,12},{5,13},{6,14},{7,15},{8,0},{9,1},... | collective-permute-start | bytes 1105928 | tf_op jit(solution)/shard_map/ppermute | solution.py:395
  248.2 1.2 collective-permute-start.37
  249.4 1.7 collective-permute-start.38
  251.3 5.3 %collective-permute-done.41 = f32[16,768]{1,0:T(8,128)S(1)} collective-permute-done((f32[16,768]{1,0:T(8,128)S(1)}, f32[16,768]{1,0:T(8,128)S(1)}, u32[]{:S(2)}, u32[]{:S(2)}) %collective-permute-start.41) | collective-permute-done | bytes 49184 | tf_op jit(solution)/shard_map/ppermute | solution.py:395
  257.4 3.1 %collective-permute-done.38 = bf16[2,2,48,384]{3,2,1,0:T(8,128)(2,1)S(1)} collective-permute-done((bf16[2,2,48,384]{3,2,1,0:T(8,128)(2,1)S(1)}, bf16[2,2,48,384]{3,2,1,0:T(8,128)(2,1)S(1)}, u32[]{:S(2)}, u32[]{:S(2)}) %collective-permute-start.38) | collective-permute-done | bytes 147488 | tf_op jit(solution)/shard_map/ppermute | solution.py:395
  260.4 1.2 collective-permute-start.35
  262.9 1.7 collective-permute-start.45
  264.5 4.7 %collective-permute-done.45 = f32[16,768]{1,0:T(8,128)S(1)} collective-permute-done((f32[16,768]{1,0:T(8,128)S(1)}, f32[16,768]{1,0:T(8,128)S(1)}, u32[]{:S(2)}, u32[]{:S(2)}) %collective-permute-start.45) | collective-permute-done | bytes 49184 | tf_op jit(solution)/shard_map/ppermute | solution.py:395
  269.3 2.5 collective-permute-done.43
  272.6 1.8 collective-permute-start.47
  274.7 2.5 collective-permute-start.48
  277.2 2.1 collective-permute-done.48
  279.6 3.4 %collective-permute-done.47 = bf16[2,144,384]{2,1,0:T(8,128)(2,1)S(1)} collective-permute-done((bf16[2,144,384]{2,1,0:T(8,128)(2,1)S(1)}, bf16[2,144,384]{2,1,0:T(8,128)(2,1)S(1)}, u32[]{:S(2)}, u32[]{:S(2)}) %collective-permute-start.47) | collective-permute-done | bytes 221216 | tf_op jit(solution)/shard_map/ppermute | solution.py:395
  283.0 1.3 collective-permute-start.50
  285.0 1.6 collective-permute-start.49
  287.6 1.5 collective-permute-done.50
  289.1 4.3 %collective-permute-done.49.refs_7_ = bf16[144,384]{1,0:T(8,128)(2,1)S(1)} collective-permute-done((bf16[144,384]{1,0:T(8,128)(2,1)S(1)}, bf16[144,384]{1,0:T(8,128)(2,1)S(1)}, u32[]{:S(2)}, u32[]{:S(2)}) %collective-permute-start.49) | collective-permute-done | bytes 110624 | tf_op jit(solution)/shard_map/ppermute | solution.py:395
  293.5 1.1 write_grads.1
  (237 shorter events, 23.2 us)
Async XLA Ops:
  3.1 9.5 %collective-permute-start.1 = (bf16[256,896]{1,0:T(8,128)(2,1)S(1)}, bf16[256,896]{1,0:T(8,128)(2,1)S(1)}, u32[]{:S(2)}, u32[]{:S(2)}) collective-permute-start(bf16[256,896]{1,0:T(8,128)(2,1)S(1)} %get-tuple-element.545), channel_id=1, source_target_pairs={{0,2},{1,0},{2,3},{3,1},{4,6},{5,4},{6,7},{7,5},{8,10},{9,8},{10,1... | collective-permute-start | bytes 1376264 | tf_op jit(solution)/shard_map/ppermute | solution.py:74
  3.6 9.0 %collective-permute-start = (bf16[256,896]{1,0:T(8,128)(2,1)S(1)}, bf16[256,896]{1,0:T(8,128)(2,1)S(1)}, u32[]{:S(2)}, u32[]{:S(2)}) collective-permute-start(bf16[256,896]{1,0:T(8,128)(2,1)S(1)} %get-tuple-element.546), channel_id=1, source_target_pairs={{0,0},{1,2},{2,1},{3,3},{4,4},{5,6},{6,5},{7,7},{8,8},{9,10},{10,9... | collective-permute-start | bytes 1376264 | tf_op jit(solution)/shard_map/ppermute | solution.py:74
  12.8 14.7 %copy-start = (bf16[512,896]{1,0:T(8,128)(2,1)}, bf16[512,896]{1,0:T(8,128)(2,1)S(1)}, u32[]{:S(2)}) copy-start(bf16[512,896]{1,0:T(8,128)(2,1)S(1)} %pad_maximum_fusion.1.refs_0_.refs_7_.refs_3_) | copy-start | bytes 2752516
  12.9 20.5 %collective-permute-start.4 = (bf16[512,896]{1,0:T(8,128)(2,1)S(1)}, bf16[512,896]{1,0:T(8,128)(2,1)}, u32[]{:S(2)}, u32[]{:S(2)}) collective-permute-start(bf16[512,896]{1,0:T(8,128)(2,1)S(1)} %pad_maximum_fusion.1.refs_0_.refs_7_.refs_3_), channel_id=1, source_target_pairs={{0,2},{1,3},{2,0},{3,1},{4,6},{5,7},{6,4},{7,5},{8,10},{9,11},{10,... | collective-permute-start | bytes 2752520 | tf_op jit(solution)/shard_map/ppermute | solution.py:105
  18.9 32.9 %collective-permute-start.3 = (bf16[2,256,768]{2,1,0:T(8,128)(2,1)}, bf16[2,256,768]{2,1,0:T(8,128)(2,1)}, u32[]{:S(2)}, u32[]{:S(2)}) collective-permute-start(bf16[2,256,768]{2,1,0:T(8,128)(2,1)} %get-tuple-element.541), channel_id=1, source_target_pairs={{0,2},{1,0},{2,3},{3,1},{4,6},{5,4},{6,7},{7,5},{8,10},{9,8},{10,1... | collective-permute-start | bytes 2359304 | tf_op jit(solution)/shard_map/ppermute | solution.py:74
  18.9 32.9 %collective-permute-start.2 = (bf16[2,256,768]{2,1,0:T(8,128)(2,1)}, bf16[2,256,768]{2,1,0:T(8,128)(2,1)}, u32[]{:S(2)}, u32[]{:S(2)}) collective-permute-start(bf16[2,256,768]{2,1,0:T(8,128)(2,1)} %get-tuple-element.542), channel_id=1, source_target_pairs={{0,0},{1,2},{2,1},{3,3},{4,4},{5,6},{6,5},{7,7},{8,8},{9,10},{10,9... | collective-permute-start | bytes 2359304 | tf_op jit(solution)/shard_map/ppermute | solution.py:74
  54.6 4.8 %collective-permute-start.5 = (bf16[512,768]{1,0:T(8,128)(2,1)S(1)}, bf16[512,768]{1,0:T(8,128)(2,1)S(1)}, u32[]{:S(2)}, u32[]{:S(2)}) collective-permute-start(bf16[512,768]{1,0:T(8,128)(2,1)S(1)} %get-tuple-element.538.refs_0_.refs_5_), channel_id=1, source_target_pairs={{0,2},{1,3},{2,0},{3,1},{4,6},{5,7},{6,4},{7,5},{8,10},{9,11},{10,... | collective-permute-start | bytes 2359304 | tf_op jit(solution)/shard_map/ppermute | solution.py:105
  102.7 15.6 %copy-start.19 = (bf16[512,768]{1,0:T(8,128)(2,1)}, bf16[512,768]{1,0:T(8,128)(2,1)S(1)}, u32[]{:S(2)}) copy-start(bf16[512,768]{1,0:T(8,128)(2,1)S(1)} %get-tuple-element.324.refs_4_) | copy-start | bytes 2359300
  102.7 15.6 %copy-start.26 = (f32[512,768]{1,0:T(8,128)}, f32[512,768]{1,0:T(8,128)S(1)}, u32[]{:S(2)}) copy-start(f32[512,768]{1,0:T(8,128)S(1)} %get-tuple-element.331.refs_6_) | copy-start | bytes 4718596
  102.7 15.6 %copy-start.33 = (bf16[512,768]{1,0:T(8,128)(2,1)}, bf16[512,768]{1,0:T(8,128)(2,1)S(1)}, u32[]{:S(2)}) copy-start(bf16[512,768]{1,0:T(8,128)(2,1)S(1)} %get-tuple-element.333.refs_9_) | copy-start | bytes 2359300
  102.7 16.6 %collective-permute-start.6 = (bf16[2,8,192,384]{3,2,1,0:T(8,128)(2,1)}, bf16[2,8,192,384]{3,2,1,0:T(8,128)(2,1)}, u32[]{:S(2)}, u32[]{:S(2)}) collective-permute-start(bf16[2,8,192,384]{3,2,1,0:T(8,128)(2,1)} %get-tuple-element.302), channel_id=1, source_target_pairs={{0,2},{2,0},{4,6},{6,4},{8,10},{10,8},{12,14},{14,12},{16,18},{18,... | collective-permute-start | bytes 7077896 | tf_op jit(solution)/shard_map/ppermute | solution.py:384
  102.8 16.5 %collective-permute-start.7 = (bf16[2,8,192,384]{3,2,1,0:T(8,128)(2,1)}, bf16[2,8,192,384]{3,2,1,0:T(8,128)(2,1)}, u32[]{:S(2)}, u32[]{:S(2)}) collective-permute-start(bf16[2,8,192,384]{3,2,1,0:T(8,128)(2,1)} %get-tuple-element.304), channel_id=1, source_target_pairs={{0,2},{2,0},{4,6},{6,4},{8,10},{10,8},{12,14},{14,12},{16,18},{18,... | collective-permute-start | bytes 7077896 | tf_op jit(solution)/shard_map/ppermute | solution.py:384
  103.4 15.0 %collective-permute-start.8 = (bf16[256,768]{1,0:T(8,128)(2,1)S(1)}, bf16[256,768]{1,0:T(8,128)(2,1)S(1)}, u32[]{:S(2)}, u32[]{:S(2)}) collective-permute-start(bf16[256,768]{1,0:T(8,128)(2,1)S(1)} %get-tuple-element.551), channel_id=1, source_target_pairs={{0,0},{2,1},{1,2},{3,3},{4,4},{6,5},{5,6},{7,7},{8,8},{10,9},{9,10... | collective-permute-start | bytes 1179656 | tf_op jit(solution)/shard_map/ppermute | solution.py:90
  104.1 14.3 %collective-permute-start.9 = (bf16[256,768]{1,0:T(8,128)(2,1)S(1)}, bf16[256,768]{1,0:T(8,128)(2,1)S(1)}, u32[]{:S(2)}, u32[]{:S(2)}) collective-permute-start(bf16[256,768]{1,0:T(8,128)(2,1)S(1)} %get-tuple-element.552), channel_id=1, source_target_pairs={{2,0},{0,1},{3,2},{1,3},{6,4},{4,5},{7,6},{5,7},{10,8},{8,9},{11,1... | collective-permute-start | bytes 1179656 | tf_op jit(solution)/shard_map/ppermute | solution.py:91
  119.3 25.8 %collective-permute-start.13 = (bf16[2,512,384]{2,1,0:T(8,128)(2,1)}, bf16[2,512,384]{2,1,0:T(8,128)(2,1)}, u32[]{:S(2)}, u32[]{:S(2)}) collective-permute-start(bf16[2,512,384]{2,1,0:T(8,128)(2,1)} %get-tuple-element.323), channel_id=1, source_target_pairs={{0,2},{1,3},{2,0},{3,1},{4,6},{5,7},{6,4},{7,5},{8,10},{9,11},{10,... | collective-permute-start | bytes 2359304 | tf_op jit(solution)/shard_map/ppermute | solution.py:105
  119.4 25.8 %copy-start.31 = (bf16[512,768]{1,0:T(8,128)(2,1)S(1)}, bf16[512,768]{1,0:T(8,128)(2,1)}, u32[]{:S(2)}) copy-start(bf16[512,768]{1,0:T(8,128)(2,1)} %copy-done.30) | copy-start | bytes 2359300
  119.4 25.8 %copy-start.34 = (bf16[512,768]{1,0:T(8,128)(2,1)S(1)}, bf16[512,768]{1,0:T(8,128)(2,1)}, u32[]{:S(2)}) copy-start(bf16[512,768]{1,0:T(8,128)(2,1)} %copy-done.33) | copy-start | bytes 2359300
  119.4 25.8 %copy-start.42 = (bf16[512,384]{1,0:T(8,128)(2,1)S(1)}, bf16[512,384]{1,0:T(8,128)(2,1)}, u32[]{:S(2)}) copy-start(bf16[512,384]{1,0:T(8,128)(2,1)} %get-tuple-element.329.refs_1_) | copy-start | bytes 1179652
  129.8 22.3 %collective-permute-start.10 = (bf16[2,2,2,128,384]{4,3,2,1,0:T(8,128)(2,1)}, bf16[2,2,2,128,384]{4,3,2,1,0:T(8,128)(2,1)S(1)}, u32[]{:S(2)}, u32[]{:S(2)}) collective-permute-start(bf16[2,2,2,128,384]{4,3,2,1,0:T(8,128)(2,1)} %bitcast.261), channel_id=1, source_target_pairs={{0,1},{1,0},{2,3},{3,2},{4,5},{5,4},{6,7},{7,6},{8,9},{9,8},{10,11... | collective-permute-start | bytes 2359304 | tf_op jit(solution)/shard_map/ppermute | solution.py:395
  130.1 21.9 %collective-permute-start.11 = (bf16[2,2,2,128,384]{4,3,2,1,0:T(8,128)(2,1)}, bf16[2,2,2,128,384]{4,3,2,1,0:T(8,128)(2,1)S(1)}, u32[]{:S(2)}, u32[]{:S(2)}) collective-permute-start(bf16[2,2,2,128,384]{4,3,2,1,0:T(8,128)(2,1)} %bitcast.260), channel_id=1, source_target_pairs={{0,4},{1,5},{2,6},{3,7},{4,0},{5,1},{6,2},{7,3},{8,12},{9,13},{10,... | collective-permute-start | bytes 2359304 | tf_op jit(solution)/shard_map/ppermute | solution.py:395
  132.7 19.4 %collective-permute-start.12 = (bf16[2,2,2,128,384]{4,3,2,1,0:T(8,128)(2,1)}, bf16[2,2,2,128,384]{4,3,2,1,0:T(8,128)(2,1)S(1)}, u32[]{:S(2)}, u32[]{:S(2)}) collective-permute-start(bf16[2,2,2,128,384]{4,3,2,1,0:T(8,128)(2,1)} %bitcast.259), channel_id=1, source_target_pairs={{0,8},{1,9},{2,10},{3,11},{4,12},{5,13},{6,14},{7,15},{8,0},{9,1},... | collective-permute-start | bytes 2359304 | tf_op jit(solution)/shard_map/ppermute | solution.py:395
  145.1 6.9 %collective-permute-start.14 = (bf16[2,512,384]{2,1,0:T(8,128)(2,1)}, bf16[2,512,384]{2,1,0:T(8,128)(2,1)S(1)}, u32[]{:S(2)}, u32[]{:S(2)}) collective-permute-start(bf16[2,512,384]{2,1,0:T(8,128)(2,1)} %get-tuple-element.328), channel_id=1, source_target_pairs={{0,2},{1,3},{2,0},{3,1},{4,6},{5,7},{6,4},{7,5},{8,10},{9,11},{10,... | collective-permute-start | bytes 2359304 | tf_op jit(solution)/shard_map/ppermute | solution.py:105
  152.1 7.1 %collective-permute-start.17 = (bf16[2,8,144,384]{3,2,1,0:T(8,128)(2,1)S(1)}, bf16[2,8,144,384]{3,2,1,0:T(8,128)(2,1)S(1)}, u32[]{:S(2)}, u32[]{:S(2)}) collective-permute-start(bf16[2,8,144,384]{3,2,1,0:T(8,128)(2,1)S(1)} %get-tuple-element.348), channel_id=1, source_target_pairs={{0,2},{2,0},{4,6},{6,4},{8,10},{10,8},{12,14},{14,12},{16,18},{18,... | collective-permute-start | bytes 5308424 | tf_op jit(solution)/shard_map/ppermute | solution.py:384
  159.2 17.5 %copy-start.28 = (bf16[2,8,96,384]{3,2,1,0:T(8,128)(2,1)}, bf16[2,8,96,384]{3,2,1,0:T(8,128)(2,1)S(1)}, u32[]{:S(2)}) copy-start(bf16[2,8,96,384]{3,2,1,0:T(8,128)(2,1)S(1)} %get-tuple-element.359) | copy-start | bytes 3538948
  159.2 17.5 %copy-start.48 = (bf16[2,8,144,384]{3,2,1,0:T(8,128)(2,1)}, bf16[2,8,144,384]{3,2,1,0:T(8,128)(2,1)S(1)}, u32[]{:S(2)}) copy-start(bf16[2,8,144,384]{3,2,1,0:T(8,128)(2,1)S(1)} %collective-permute-done.17) | copy-start | bytes 5308420
  159.2 21.6 %collective-permute-start.18 = (bf16[2,8,96,384]{3,2,1,0:T(8,128)(2,1)S(1)}, bf16[2,8,96,384]{3,2,1,0:T(8,128)(2,1)S(1)}, u32[]{:S(2)}, u32[]{:S(2)}) collective-permute-start(bf16[2,8,96,384]{3,2,1,0:T(8,128)(2,1)S(1)} %get-tuple-element.360), channel_id=1, source_target_pairs={{0,2},{2,0},{4,6},{6,4},{8,10},{10,8},{12,14},{14,12},{16,18},{18,... | collective-permute-start | bytes 3538952 | tf_op jit(solution)/shard_map/ppermute | solution.py:384
  159.8 16.9 %collective-permute-start.19 = (bf16[256,768]{1,0:T(8,128)(2,1)S(1)}, bf16[256,768]{1,0:T(8,128)(2,1)S(1)}, u32[]{:S(2)}, u32[]{:S(2)}) collective-permute-start(bf16[256,768]{1,0:T(8,128)(2,1)S(1)} %get-tuple-element.549), channel_id=1, source_target_pairs={{0,0},{2,1},{1,2},{3,3},{4,4},{6,5},{5,6},{7,7},{8,8},{10,9},{9,10... | collective-permute-start | bytes 1179656 | tf_op jit(solution)/shard_map/ppermute | solution.py:90
  160.5 16.2 %collective-permute-start.20 = (bf16[256,768]{1,0:T(8,128)(2,1)S(1)}, bf16[256,768]{1,0:T(8,128)(2,1)S(1)}, u32[]{:S(2)}, u32[]{:S(2)}) collective-permute-start(bf16[256,768]{1,0:T(8,128)(2,1)S(1)} %get-tuple-element.550), channel_id=1, source_target_pairs={{2,0},{0,1},{3,2},{1,3},{6,4},{4,5},{7,6},{5,7},{10,8},{8,9},{11,1... | collective-permute-start | bytes 1179656 | tf_op jit(solution)/shard_map/ppermute | solution.py:91
  163.4 14.3 %collective-permute-start.15 = (bf16[2,2,128,384]{3,2,1,0:T(8,128)(2,1)S(1)}, bf16[2,2,128,384]{3,2,1,0:T(8,128)(2,1)S(1)}, u32[]{:S(2)}, u32[]{:S(2)}) collective-permute-start(bf16[2,2,128,384]{3,2,1,0:T(8,128)(2,1)S(1)} %bitcast.223), channel_id=1, source_target_pairs={{0,4},{1,5},{2,6},{3,7},{4,0},{5,1},{6,2},{7,3},{8,12},{9,13},{10,... | collective-permute-start | bytes 1179656 | tf_op jit(solution)/shard_map/ppermute | solution.py:395
  163.6 17.2 %collective-permute-start.16 = (bf16[2,2,128,384]{3,2,1,0:T(8,128)(2,1)S(1)}, bf16[2,2,128,384]{3,2,1,0:T(8,128)(2,1)S(1)}, u32[]{:S(2)}, u32[]{:S(2)}) collective-permute-start(bf16[2,2,128,384]{3,2,1,0:T(8,128)(2,1)S(1)} %bitcast.222), channel_id=1, source_target_pairs={{0,1},{1,0},{2,3},{3,2},{4,5},{5,4},{6,7},{7,6},{8,9},{9,8},{10,11... | collective-permute-start | bytes 1179656 | tf_op jit(solution)/shard_map/ppermute | solution.py:395
  180.8 27.9 %collective-permute-start.24 = (bf16[2,512,384]{2,1,0:T(8,128)(2,1)S(1)}, bf16[2,512,384]{2,1,0:T(8,128)(2,1)S(1)}, u32[]{:S(2)}, u32[]{:S(2)}) collective-permute-start(bf16[2,512,384]{2,1,0:T(8,128)(2,1)S(1)} %copy-done.64), channel_id=1, source_target_pairs={{0,2},{1,3},{2,0},{3,1},{4,6},{5,7},{6,4},{7,5},{8,10},{9,11},{10,... | collective-permute-start | bytes 2359304 | tf_op jit(solution)/shard_map/ppermute | solution.py:105
  188.0 20.6 %collective-permute-start.23 = (bf16[2,2,2,96,384]{4,3,2,1,0:T(8,128)(2,1)}, bf16[2,2,2,96,384]{4,3,2,1,0:T(8,128)(2,1)S(1)}, u32[]{:S(2)}, u32[]{:S(2)}) collective-permute-start(bf16[2,2,2,96,384]{4,3,2,1,0:T(8,128)(2,1)} %bitcast.262), channel_id=1, source_target_pairs={{0,4},{1,5},{2,6},{3,7},{4,0},{5,1},{6,2},{7,3},{8,12},{9,13},{10,... | collective-permute-start | bytes 1769480 | tf_op jit(solution)/shard_map/ppermute | solution.py:395
  188.2 20.5 %collective-permute-start.21 = (bf16[2,256,384]{2,1,0:T(8,128)(2,1)}, bf16[2,256,384]{2,1,0:T(8,128)(2,1)S(1)}, u32[]{:S(2)}, u32[]{:S(2)}) collective-permute-start(bf16[2,256,384]{2,1,0:T(8,128)(2,1)} %bitcast.264), channel_id=1, source_target_pairs={{0,8},{1,9},{2,10},{3,11},{4,12},{5,13},{6,14},{7,15},{8,0},{9,1},... | collective-permute-start | bytes 1179656 | tf_op jit(solution)/shard_map/ppermute | solution.py:395
  189.9 18.8 %collective-permute-start.22 = (bf16[2,2,128,384]{3,2,1,0:T(8,128)(2,1)}, bf16[2,2,128,384]{3,2,1,0:T(8,128)(2,1)S(1)}, u32[]{:S(2)}, u32[]{:S(2)}) collective-permute-start(bf16[2,2,128,384]{3,2,1,0:T(8,128)(2,1)} %bitcast.263), channel_id=1, source_target_pairs={{0,16},{1,17},{2,18},{3,19},{4,20},{5,21},{6,22},{7,23},{8,24},{9,... | collective-permute-start | bytes 1179656 | tf_op jit(solution)/shard_map/ppermute | solution.py:395
  192.5 16.3 %copy-start.21 = (bf16[512,768]{1,0:T(8,128)(2,1)S(1)}, bf16[512,768]{1,0:T(8,128)(2,1)}, u32[]{:S(2)}) copy-start(bf16[512,768]{1,0:T(8,128)(2,1)} %get-tuple-element.398.refs_3_.refs_5_) | copy-start | bytes 2359300
  192.5 16.3 %copy-start.23 = (bf16[512,384]{1,0:T(8,128)(2,1)S(1)}, bf16[512,384]{1,0:T(8,128)(2,1)}, u32[]{:S(2)}) copy-start(bf16[512,384]{1,0:T(8,128)(2,1)} %get-tuple-element.396.refs_1_.refs_0_) | copy-start | bytes 1179652
  192.5 24.5 %collective-permute-start.25 = (bf16[2,2,2,144,384]{4,3,2,1,0:T(8,128)(2,1)}, bf16[2,2,2,144,384]{4,3,2,1,0:T(8,128)(2,1)S(1)}, u32[]{:S(2)}, u32[]{:S(2)}) collective-permute-start(bf16[2,2,2,144,384]{4,3,2,1,0:T(8,128)(2,1)} %bitcast.258), channel_id=1, source_target_pairs={{0,1},{1,0},{2,3},{3,2},{4,5},{5,4},{6,7},{7,6},{8,9},{9,8},{10,11... | collective-permute-start | bytes 2654216 | tf_op jit(solution)/shard_map/ppermute | solution.py:395
  208.6 8.4 %collective-permute-start.27 = (bf16[2,512,384]{2,1,0:T(8,128)(2,1)}, bf16[2,512,384]{2,1,0:T(8,128)(2,1)S(1)}, u32[]{:S(2)}, u32[]{:S(2)}) collective-permute-start(bf16[2,512,384]{2,1,0:T(8,128)(2,1)} %get-tuple-element.401), channel_id=1, source_target_pairs={{0,2},{1,3},{2,0},{3,1},{4,6},{5,7},{6,4},{7,5},{8,10},{9,11},{10,... | collective-permute-start | bytes 2359304 | tf_op jit(solution)/shard_map/ppermute | solution.py:105
  210.7 6.3 %collective-permute-start.26 = (bf16[2,8,48,384]{3,2,1,0:T(8,128)(2,1)S(1)}, bf16[2,8,48,384]{3,2,1,0:T(8,128)(2,1)S(1)}, u32[]{:S(2)}, u32[]{:S(2)}) collective-permute-start(bf16[2,8,48,384]{3,2,1,0:T(8,128)(2,1)S(1)} %get-tuple-element.400), channel_id=1, source_target_pairs={{0,2},{2,0},{4,6},{6,4},{8,10},{10,8},{12,14},{14,12},{16,18},{18,... | collective-permute-start | bytes 1769480 | tf_op jit(solution)/shard_map/ppermute | solution.py:384
  218.4 16.5 %copy-start.14 = (bf16[768,768]{1,0:T(8,128)(2,1)S(1)}, bf16[768,768]{1,0:T(8,128)(2,1)}, u32[]{:S(2)}) copy-start(bf16[768,768]{1,0:T(8,128)(2,1)} %refs_6_.5) | copy-start | bytes 3538948
  220.1 23.2 %collective-permute-start.33 = (bf16[2,8,96,384]{3,2,1,0:T(8,128)(2,1)S(1)}, bf16[2,8,96,384]{3,2,1,0:T(8,128)(2,1)S(1)}, u32[]{:S(2)}, u32[]{:S(2)}) collective-permute-start(bf16[2,8,96,384]{3,2,1,0:T(8,128)(2,1)S(1)} %get-tuple-element.431), channel_id=1, source_target_pairs={{0,2},{2,0},{4,6},{6,4},{8,10},{10,8},{12,14},{14,12},{16,18},{18,... | collective-permute-start | bytes 3538952 | tf_op jit(solution)/shard_map/ppermute | solution.py:384
  220.2 23.1 %collective-permute-start.30 = (bf16[2,2,144,384]{3,2,1,0:T(8,128)(2,1)S(1)}, bf16[2,2,144,384]{3,2,1,0:T(8,128)(2,1)S(1)}, u32[]{:S(2)}, u32[]{:S(2)}) collective-permute-start(bf16[2,2,144,384]{3,2,1,0:T(8,128)(2,1)S(1)} %bitcast.221), channel_id=1, source_target_pairs={{0,4},{1,5},{2,6},{3,7},{4,0},{5,1},{6,2},{7,3},{8,12},{9,13},{10,... | collective-permute-start | bytes 1327112 | tf_op jit(solution)/shard_map/ppermute | solution.py:395
  221.9 12.1 %collective-permute-start.28 = (bf16[256,384]{1,0:T(8,128)(2,1)S(1)}, bf16[256,384]{1,0:T(8,128)(2,1)S(1)}, u32[]{:S(2)}, u32[]{:S(2)}) collective-permute-start(bf16[256,384]{1,0:T(8,128)(2,1)S(1)} %bitcast.231), channel_id=1, source_target_pairs={{0,16},{1,17},{2,18},{3,19},{4,20},{5,21},{6,22},{7,23},{8,24},{9,... | collective-permute-start | bytes 589832 | tf_op jit(solution)/shard_map/ppermute | solution.py:395
  224.0 19.3 %collective-permute-start.31 = (bf16[2,2,96,384]{3,2,1,0:T(8,128)(2,1)S(1)}, bf16[2,2,96,384]{3,2,1,0:T(8,128)(2,1)S(1)}, u32[]{:S(2)}, u32[]{:S(2)}) collective-permute-start(bf16[2,2,96,384]{3,2,1,0:T(8,128)(2,1)S(1)} %bitcast.227), channel_id=1, source_target_pairs={{0,1},{1,0},{2,3},{3,2},{4,5},{5,4},{6,7},{7,6},{8,9},{9,8},{10,11... | collective-permute-start | bytes 884744 | tf_op jit(solution)/shard_map/ppermute | solution.py:395
  224.4 19.0 %collective-permute-start.32 = (bf16[2,2,2,48,384]{4,3,2,1,0:T(8,128)(2,1)S(1)}, bf16[2,2,2,48,384]{4,3,2,1,0:T(8,128)(2,1)S(1)}, u32[]{:S(2)}, u32[]{:S(2)}) collective-permute-start(bf16[2,2,2,48,384]{4,3,2,1,0:T(8,128)(2,1)S(1)} %bitcast.225), channel_id=1, source_target_pairs={{0,1},{1,0},{2,3},{3,2},{4,5},{5,4},{6,7},{7,6},{8,9},{9,8},{10,11... | collective-permute-start | bytes 884744 | tf_op jit(solution)/shard_map/ppermute | solution.py:395
  234.0 9.3 %collective-permute-start.29 = (bf16[2,128,384]{2,1,0:T(8,128)(2,1)S(1)}, bf16[2,128,384]{2,1,0:T(8,128)(2,1)S(1)}, u32[]{:S(2)}, u32[]{:S(2)}) collective-permute-start(bf16[2,128,384]{2,1,0:T(8,128)(2,1)S(1)} %bitcast.230), channel_id=1, source_target_pairs={{0,1},{1,0},{2,3},{3,2},{4,5},{5,4},{6,7},{7,6},{8,9},{9,8},{10,11... | collective-permute-start | bytes 589832 | tf_op jit(solution)/shard_map/ppermute | solution.py:395
  244.5 17.1 %collective-permute-start.39 = (bf16[2,240,384]{2,1,0:T(8,128)(2,1)S(1)}, bf16[2,240,384]{2,1,0:T(8,128)(2,1)S(1)}, u32[]{:S(2)}, u32[]{:S(2)}) collective-permute-start(bf16[2,240,384]{2,1,0:T(8,128)(2,1)S(1)} %bitcast.224), channel_id=1, source_target_pairs={{0,8},{1,9},{2,10},{3,11},{4,12},{5,13},{6,14},{7,15},{8,0},{9,1},... | collective-permute-start | bytes 1105928 | tf_op jit(solution)/shard_map/ppermute | solution.py:395
  247.8 3.2 %collective-permute-start.40 = (f32[16,768]{1,0:T(8,128)S(1)}, f32[16,768]{1,0:T(8,128)S(1)}, u32[]{:S(2)}, u32[]{:S(2)}) collective-permute-start(f32[16,768]{1,0:T(8,128)S(1)} %get-tuple-element.457), channel_id=1, source_target_pairs={{0,2},{1,3},{2,0},{3,1},{4,6},{5,7},{6,4},{7,5},{8,10},{9,11},{10,... | collective-permute-start | bytes 147464 | tf_op jit(solution)/shard_map/ppermute | solution.py:395
  247.8 13.7 %collective-permute-start.36 = (bf16[2,2,2,48,384]{4,3,2,1,0:T(8,128)(2,1)S(1)}, bf16[2,2,2,48,384]{4,3,2,1,0:T(8,128)(2,1)S(1)}, u32[]{:S(2)}, u32[]{:S(2)}) collective-permute-start(bf16[2,2,2,48,384]{4,3,2,1,0:T(8,128)(2,1)S(1)} %bitcast.228), channel_id=1, source_target_pairs={{0,4},{1,5},{2,6},{3,7},{4,0},{5,1},{6,2},{7,3},{8,12},{9,13},{10,... | collective-permute-start | bytes 884744 | tf_op jit(solution)/shard_map/ppermute | solution.py:395
  248.2 13.4 %collective-permute-start.37 = (bf16[2,2,2,48,384]{4,3,2,1,0:T(8,128)(2,1)S(1)}, bf16[2,2,2,48,384]{4,3,2,1,0:T(8,128)(2,1)S(1)}, u32[]{:S(2)}, u32[]{:S(2)}) collective-permute-start(bf16[2,2,2,48,384]{4,3,2,1,0:T(8,128)(2,1)S(1)} %bitcast.226), channel_id=1, source_target_pairs={{0,1},{1,0},{2,3},{3,2},{4,5},{5,4},{6,7},{7,6},{8,9},{9,8},{10,11... | collective-permute-start | bytes 884744 | tf_op jit(solution)/shard_map/ppermute | solution.py:395
  249.4 11.1 %collective-permute-start.38 = (bf16[2,2,48,384]{3,2,1,0:T(8,128)(2,1)S(1)}, bf16[2,2,48,384]{3,2,1,0:T(8,128)(2,1)S(1)}, u32[]{:S(2)}, u32[]{:S(2)}) collective-permute-start(bf16[2,2,48,384]{3,2,1,0:T(8,128)(2,1)S(1)} %bitcast.233), channel_id=1, source_target_pairs={{0,4},{1,5},{2,6},{3,7},{4,0},{5,1},{6,2},{7,3},{8,12},{9,13},{10,... | collective-permute-start | bytes 442376 | tf_op jit(solution)/shard_map/ppermute | solution.py:395
  251.0 5.6 %collective-permute-start.41 = (f32[16,768]{1,0:T(8,128)S(1)}, f32[16,768]{1,0:T(8,128)S(1)}, u32[]{:S(2)}, u32[]{:S(2)}) collective-permute-start(f32[16,768]{1,0:T(8,128)S(1)} %add.79), channel_id=1, source_target_pairs={{0,8},{1,9},{2,10},{3,11},{4,12},{5,13},{6,14},{7,15},{8,0},{9,1},... | collective-permute-start | bytes 147464 | tf_op jit(solution)/shard_map/ppermute | solution.py:395
  256.7 28.3 %collective-permute-start.34 = (bf16[256,768]{1,0:T(8,128)(2,1)S(1)}, bf16[256,768]{1,0:T(8,128)(2,1)S(1)}, u32[]{:S(2)}, u32[]{:S(2)}) collective-permute-start(bf16[256,768]{1,0:T(8,128)(2,1)S(1)} %get-tuple-element.547), channel_id=1, source_target_pairs={{0,0},{2,1},{1,2},{3,3},{4,4},{6,5},{5,6},{7,7},{8,8},{10,9},{9,10... | collective-permute-start | bytes 1179656 | tf_op jit(solution)/shard_map/ppermute | solution.py:90
  260.4 26.2 %collective-permute-start.35 = (bf16[256,768]{1,0:T(8,128)(2,1)S(1)}, bf16[256,768]{1,0:T(8,128)(2,1)S(1)}, u32[]{:S(2)}, u32[]{:S(2)}) collective-permute-start(bf16[256,768]{1,0:T(8,128)(2,1)S(1)} %get-tuple-element.548), channel_id=1, source_target_pairs={{2,0},{0,1},{3,2},{1,3},{6,4},{4,5},{7,6},{5,7},{10,8},{8,9},{11,1... | collective-permute-start | bytes 1179656 | tf_op jit(solution)/shard_map/ppermute | solution.py:91
  262.4 9.4 %collective-permute-start.43 = (bf16[2,2,48,384]{3,2,1,0:T(8,128)(2,1)S(1)}, bf16[2,2,48,384]{3,2,1,0:T(8,128)(2,1)S(1)}, u32[]{:S(2)}, u32[]{:S(2)}) collective-permute-start(bf16[2,2,48,384]{3,2,1,0:T(8,128)(2,1)S(1)} %bitcast.235), channel_id=1, source_target_pairs={{0,1},{1,0},{2,3},{3,2},{4,5},{5,4},{6,7},{7,6},{8,9},{9,8},{10,11... | collective-permute-start | bytes 442376 | tf_op jit(solution)/shard_map/ppermute | solution.py:395
  262.4 9.4 %collective-permute-start.44 = (bf16[2,2,48,384]{3,2,1,0:T(8,128)(2,1)S(1)}, bf16[2,2,48,384]{3,2,1,0:T(8,128)(2,1)S(1)}, u32[]{:S(2)}, u32[]{:S(2)}) collective-permute-start(bf16[2,2,48,384]{3,2,1,0:T(8,128)(2,1)S(1)} %bitcast.234), channel_id=1, source_target_pairs={{0,4},{1,5},{2,6},{3,7},{4,0},{5,1},{6,2},{7,3},{8,12},{9,13},{10,... | collective-permute-start | bytes 442376 | tf_op jit(solution)/shard_map/ppermute | solution.py:395
  262.9 6.4 %collective-permute-start.45 = (f32[16,768]{1,0:T(8,128)S(1)}, f32[16,768]{1,0:T(8,128)S(1)}, u32[]{:S(2)}, u32[]{:S(2)}) collective-permute-start(f32[16,768]{1,0:T(8,128)S(1)} %add.80), channel_id=1, source_target_pairs={{0,4},{1,5},{2,6},{3,7},{4,0},{5,1},{6,2},{7,3},{8,12},{9,13},{10,... | collective-permute-start | bytes 147464 | tf_op jit(solution)/shard_map/ppermute | solution.py:395
  272.6 20.9 %copy-start.47 = (f32[32,512]{1,0:T(8,128)S(1)}, f32[32,512]{1,0:T(8,128)}, u32[]{:S(2)}) copy-start(f32[32,512]{1,0:T(8,128)} %constant.96.clone.refs_9_) | copy-start | bytes 196612
  272.6 10.5 %collective-permute-start.47 = (bf16[2,144,384]{2,1,0:T(8,128)(2,1)S(1)}, bf16[2,144,384]{2,1,0:T(8,128)(2,1)S(1)}, u32[]{:S(2)}, u32[]{:S(2)}) collective-permute-start(bf16[2,144,384]{2,1,0:T(8,128)(2,1)S(1)} %bitcast.229), channel_id=1, source_target_pairs={{0,8},{1,9},{2,10},{3,11},{4,12},{5,13},{6,14},{7,15},{8,0},{9,1},... | collective-permute-start | bytes 663560 | tf_op jit(solution)/shard_map/ppermute | solution.py:395
  274.4 14.7 %collective-permute-start.46 = (bf16[240,384]{1,0:T(8,128)(2,1)S(1)}, bf16[240,384]{1,0:T(8,128)(2,1)S(1)}, u32[]{:S(2)}, u32[]{:S(2)}) collective-permute-start(bf16[240,384]{1,0:T(8,128)(2,1)S(1)} %bitcast.232), channel_id=1, source_target_pairs={{0,16},{1,17},{2,18},{3,19},{4,20},{5,21},{6,22},{7,23},{8,24},{9,... | collective-permute-start | bytes 552968 | tf_op jit(solution)/shard_map/ppermute | solution.py:395
  274.7 4.5 %collective-permute-start.48 = (f32[16,768]{1,0:T(8,128)S(1)}, f32[16,768]{1,0:T(8,128)S(1)}, u32[]{:S(2)}, u32[]{:S(2)}) collective-permute-start(f32[16,768]{1,0:T(8,128)S(1)} %add.81), channel_id=1, source_target_pairs={{0,1},{1,0},{2,3},{3,2},{4,5},{5,4},{6,7},{7,6},{8,9},{9,8},{10,11... | collective-permute-start | bytes 147464 | tf_op jit(solution)/shard_map/ppermute | solution.py:395
  279.3 9.8 %collective-permute-start.42 = (bf16[128,384]{1,0:T(8,128)(2,1)S(1)}, bf16[128,384]{1,0:T(8,128)(2,1)S(1)}, u32[]{:S(2)}, u32[]{:S(2)}) collective-permute-start(bf16[128,384]{1,0:T(8,128)(2,1)S(1)} %bitcast.237), channel_id=1, source_target_pairs={{0,4},{1,5},{2,6},{3,7},{4,0},{5,1},{6,2},{7,3},{8,12},{9,13},{10,... | collective-permute-start | bytes 294920 | tf_op jit(solution)/shard_map/ppermute | solution.py:395
  283.0 6.1 %collective-permute-start.50 = (f32[16,768]{1,0:T(8,128)S(1)}, f32[16,768]{1,0:T(8,128)S(1)}, u32[]{:S(2)}, u32[]{:S(2)}) collective-permute-start(f32[16,768]{1,0:T(8,128)S(1)} %add.82), channel_id=1, source_target_pairs={{0,16},{1,17},{2,18},{3,19},{4,20},{5,21},{6,22},{7,23},{8,24},{9,... | collective-permute-start | bytes 147464 | tf_op jit(solution)/shard_map/ppermute | solution.py:395
  285.0 8.5 %collective-permute-start.49 = (bf16[144,384]{1,0:T(8,128)(2,1)S(1)}, bf16[144,384]{1,0:T(8,128)(2,1)S(1)}, u32[]{:S(2)}, u32[]{:S(2)}) collective-permute-start(bf16[144,384]{1,0:T(8,128)(2,1)S(1)} %bitcast.236), channel_id=1, source_target_pairs={{0,16},{1,17},{2,18},{3,19},{4,20},{5,21},{6,22},{7,23},{8,24},{9,... | collective-permute-start | bytes 331784 | tf_op jit(solution)/shard_map/ppermute | solution.py:395
  (52 other events, 314.4 us)
